TPU v7x, 32 devices: a whole 2x2x4 slice. The times are simulated.
32 devices in a mesh: rows: 8 (over z, core), strata: 4 (over y, x).
Axes of the slice: x: 2, y: 2, z: 4, core: 2. Of those that a mesh axis runs over, the one named last changes fastest.
Arguments:
- user_factors: float32 [4096, 512], P(('rows', 'strata')), may hold values from -1.3 to 1.3
- item_factors: float32 [16384, 512], P(('rows', 'strata')), may hold values from -1.3 to 1.3
- ratings: float32 [2, 32768], P(None, ('rows', 'strata')), may hold values from -6 to 6
- user_offsets: int32 [2, 32768], P(None, ('rows', 'strata')), may hold values from 0 to 511, as said below
- item_offsets: int32 [2, 32768], P(None, ('rows', 'strata')), may hold values from 0 to 511
- counts: int32 [2, 32], P(None, ('rows', 'strata')), may hold values from 128 to 1024, as said below
Outputs:
- new_users: float32 [4096, 512], P(('rows', 'strata'))
- new_items: float32 [16384, 512], P(('rows', 'strata'))
Inputs may be any that keep to these rules, and one draw needn't show every extreme that they name: `counts`: some tile of each sub-epoch has all 1024 slots active. `user_offsets`: splitting a user block into 4 runs of 128 users, each tile's slots (active or not) name exactly 32 distinct users of every run.
All inputs are finite; a program needn't handle non-finite values.
Results may differ from a plain program's by a relative error of at most 0.0003.
Values sent between devices are 32-bit elements; how exact they have to be, the bound alone decides.
No kernel may reach another device: no remote copies, remote signals or barrier semaphores. Data moves between devices by JAX's collectives and lax.ppermute only.
A program may use at most 64 MiB of HBM per device.

v0:
```python
import jax
import jax.numpy as jnp
from jax import lax
from jax.sharding import PartitionSpec as P


def passed_along(value, axis, steps):
    count = lax.axis_size(axis)
    pairs = [(source, (source + steps) % count) for source in range(count)]
    return lax.ppermute(value, axis, pairs)


def tile_grads(block_u, block_v, user_index, item_index, observed, count):
    slots = jnp.arange(observed.shape[0], dtype=jnp.int32)
    active_mask = (slots < count).astype(jnp.float32)
    u_rows = block_u[user_index]
    v_rows = block_v[item_index]
    errors = active_mask * (observed - jnp.sum(u_rows * v_rows, axis=1))
    grad_u = jnp.zeros_like(block_u).at[user_index].add(errors[:, None] * v_rows)
    grad_v = jnp.zeros_like(block_v).at[item_index].add(errors[:, None] * u_rows)
    return (grad_u, grad_v)


def gather_users(owned_rows):
    return lax.all_gather(owned_rows, "strata", axis=0, tiled=True)


def on_device(user_factors, item_factors, ratings, user_offsets, item_offsets, counts):
    owned_rows = user_factors
    block_v = item_factors
    block_u = gather_users(owned_rows)
    sub_epochs = ratings.shape[0]
    for sub_epoch in range(sub_epochs):
        step_size = 0.04 / (1.0 + 0.5 * sub_epoch)
        grad_u, grad_v = tile_grads(
            block_u,
            block_v,
            user_offsets[sub_epoch],
            item_offsets[sub_epoch],
            ratings[sub_epoch],
            counts[sub_epoch, 0],
        )
        owned_share = lax.psum_scatter(grad_u, "strata", scatter_dimension=0, tiled=True)
        owned_rows = owned_rows + step_size * (owned_share - 0.1 * owned_rows)
        if sub_epoch + 1 < sub_epochs:
            block_u = gather_users(owned_rows)
        block_v = block_v + step_size * (grad_v - 0.1 * block_v)
        if sub_epoch + 1 < sub_epochs:
            block_v = passed_along(block_v, "rows", 1)
    block_v = passed_along(block_v, "rows", 1 - sub_epochs)
    return (owned_rows, block_v)


def solution(mesh):
    return jax.shard_map(
        on_device,
        mesh=mesh,
        in_specs=(
            P(("rows", "strata"), None),
            P(("rows", "strata"), None),
            P(None, ("rows", "strata")),
            P(None, ("rows", "strata")),
            P(None, ("rows", "strata")),
            P(None, ("rows", "strata")),
        ),
        out_specs=(P(("rows", "strata"), None), P(("rows", "strata"), None)),
        check_vma=False,
    )
```

profile of v0, /device:TPU:0, one launch (start us, length us, event | category | flops | bytes accessed | tf_op | source)
XLA Modules:
  0.0 168.1 jit_solution(8278995270363552684)
XLA Ops:
  7.2 0.0 all-gather.3.cloned.1.call-start
  7.2 0.7 all-gather.3.cloned.1.call-update
  7.9 0.0 reduce-scatter.3.cloned.1.call-start
  7.9 0.8 compare_select_fusion
  8.8 6.5 %gather_fusion.1 = f32[1024,512]{1,0:T(8,128)} fusion(f32[512,512]{1,0:T(8,128)} %param.7, s32[1024]{0:T(1024)S(1)} %broadcast_clamp_fusion.2), kind=kCustom, calls=%fused_computation.1 | custom fusion | bytes 4198400 | tf_op jit(solution)/shard_map/gather | solution.py:17
  15.3 0.6 fusion.17
  16.0 23.2 %all-gather.3.cloned.1.call-done = f32[512,512]{1,0:T(8,128)} async-done(((f32[128,512]{1,0:T(8,128)}), f32[512,512]{1,0:T(8,128)}) %all-gather.3.cloned.1.call-update) | async-done | bytes 1048592 | tf_op jit(solution)/shard_map/all_gather | solution.py:25
  39.2 5.2 %gather_fusion = f32[1024,512]{1,0:T(8,128)S(1)} fusion(f32[512,512]{1,0:T(8,128)} %all-gather.3.cloned.1.call-done, s32[1024]{0:T(1024)S(1)} %broadcast_clamp_fusion.3), kind=kCustom, calls=%fused_computation | custom fusion | bytes 4198400 | tf_op jit(solution)/shard_map/gather | solution.py:16
  44.5 1.9 %multiply_reduce_fusion.1 = f32[1024]{0:T(1024)S(1)} fusion(f32[1024,512]{1,0:T(8,128)S(1)} %gather_fusion, f32[1024,512]{1,0:T(8,128)} %gather_fusion.1), kind=kLoop, calls=%fused_computation.17 | loop fusion | flops 1047552 | bytes 4198400 | tf_op jit(solution)/shard_map/reduce_sum | solution.py:18
  46.3 0.7 subtract_select_fusion.1
  47.0 8.8 %scatter_custom_fusion = f32[512,512]{1,0:T(8,128)} fusion(s32[1024]{0:T(1024)S(1)} %bitcast.25, f32[1024,512]{1,0:T(8,128)} %gather_fusion.1, f32[1024]{0:T(1024)S(1)} %subtract_select_fusion.1, f32[]{:T(128)} %constant.6.clone.1), kind=kCustom, calls=%fused_computation.15 | custom fusion | flops 1048576 | bytes 3149828 | tf_op jit(solution)/shard_map/scatter-add | solution.py:19
  55.8 0.0 reduce-scatter.3.cloned.1.call-update
  55.8 0.0 all-gather.5.cloned.1.call-start
  55.8 27.8 %reduce-scatter.3.cloned.1.call-done = f32[128,512]{1,0:T(8,128)} async-done(((f32[512,512]{1,0:T(8,128)}), f32[128,512]{1,0:T(8,128)}) %reduce-scatter.3.cloned.1.call-update) | async-done | bytes 262160 | tf_op jit(solution)/shard_map/reduce_scatter | solution.py:43
  83.7 1.7 %multiply_add_fusion.3 = f32[128,512]{1,0:T(8,128)} fusion(f32[128,512]{1,0:T(8,128)S(1)} %copy-done.2, f32[128,512]{1,0:T(8,128)} %reduce-scatter.3.cloned.1.call-done), kind=kLoop, calls=%fused_computation.29 | loop fusion | flops 262144 | bytes 786432 | tf_op jit(solution)/shard_map/add | solution.py:44
  85.4 0.0 reduce-scatter.5.cloned.1.call-start
  85.4 8.1 %scatter_custom_fusion.1 = f32[512,512]{1,0:T(8,128)} fusion(s32[1024]{0:T(1024)S(1)} %bitcast.23, f32[1024,512]{1,0:T(8,128)S(1)} %gather_fusion, f32[1024]{0:T(1024)S(1)} %subtract_select_fusion.1, f32[]{:T(128)} %constant.6.clone.1), kind=kCustom, calls=%fused_computation.13 | custom fusion | flops 1048576 | bytes 3149828 | tf_op jit(solution)/shard_map/scatter-add | solution.py:20
  93.6 1.5 multiply_add_fusion.1
  95.1 0.2 collective-permute-start
  95.4 16.0 %collective-permute-done = f32[512,512]{1,0:T(8,128)S(1)} collective-permute-done((f32[512,512]{1,0:T(8,128)S(1)}, f32[512,512]{1,0:T(8,128)S(1)}, u32[]{:S(2)}, u32[]{:S(2)}) %collective-permute-start) | collective-permute-done | bytes 1048608 | tf_op jit(solution)/shard_map/ppermute | solution.py:10
  111.4 4.9 %gather_fusion.3 = f32[1024,512]{1,0:T(8,128)} fusion(f32[512,512]{1,0:T(8,128)S(1)} %collective-permute-done, s32[1024]{0:T(1024)S(1)} %broadcast_clamp_fusion), kind=kCustom, calls=%fused_computation.3 | custom fusion | bytes 4198400 | tf_op jit(solution)/shard_map/gather | solution.py:17
  116.2 5.2 %gather_fusion.2 = f32[1024,512]{1,0:T(8,128)S(1)} fusion(f32[512,512]{1,0:T(8,128)} %all-gather.5.cloned.1.call-done, s32[1024]{0:T(1024)S(1)} %broadcast_clamp_fusion.1), kind=kCustom, calls=%fused_computation.2 | custom fusion | bytes 4198400 | tf_op jit(solution)/shard_map/gather | solution.py:16
  121.5 1.9 %multiply_reduce_fusion = f32[1024]{0:T(1024)S(1)} fusion(f32[1024,512]{1,0:T(8,128)S(1)} %gather_fusion.2, f32[1024,512]{1,0:T(8,128)} %gather_fusion.3), kind=kLoop, calls=%fused_computation.12 | loop fusion | flops 1047552 | bytes 4198400 | tf_op jit(solution)/shard_map/reduce_sum | solution.py:18
  123.3 0.6 subtract_select_fusion
  124.0 8.8 %scatter_custom_fusion.2 = f32[512,512]{1,0:T(8,128)} fusion(s32[1024]{0:T(1024)S(1)} %bitcast.21, f32[1024,512]{1,0:T(8,128)} %gather_fusion.3, f32[1024]{0:T(1024)S(1)} %subtract_select_fusion, f32[]{:T(128)} %constant.6.clone.1), kind=kCustom, calls=%fused_computation.10 | custom fusion | flops 1048576 | bytes 3149828 | tf_op jit(solution)/shard_map/scatter-add | solution.py:19
  132.8 8.1 %scatter_custom_fusion.3 = f32[512,512]{1,0:T(8,128)} fusion(s32[1024]{0:T(1024)S(1)} %bitcast.19, f32[1024,512]{1,0:T(8,128)S(1)} %gather_fusion.2, f32[1024]{0:T(1024)S(1)} %subtract_select_fusion, f32[]{:T(128)} %constant.6.clone.1), kind=kCustom, calls=%fused_computation.8 | custom fusion | flops 1048576 | bytes 3149828 | tf_op jit(solution)/shard_map/scatter-add | solution.py:20
  140.9 1.6 multiply_add_fusion
  142.5 0.1 collective-permute-start.1
  142.6 12.3 %collective-permute-done.1 = f32[512,512]{1,0:T(8,128)S(1)} collective-permute-done((f32[512,512]{1,0:T(8,128)S(1)}, f32[512,512]{1,0:T(8,128)S(1)}, u32[]{:S(2)}, u32[]{:S(2)}) %collective-permute-start.1) | collective-permute-done | bytes 1048608 | tf_op jit(solution)/shard_map/ppermute | solution.py:10
  154.9 4.0 %reduce-scatter.5.cloned.1.call-done = f32[128,512]{1,0:T(8,128)} async-done(((f32[512,512]{1,0:T(8,128)}), f32[128,512]{1,0:T(8,128)}) %reduce-scatter.5.cloned.1.call-update) | async-done | bytes 262160 | tf_op jit(solution)/shard_map/reduce_scatter | solution.py:43
  158.8 1.7 %multiply_add_fusion.2 = f32[128,512]{1,0:T(8,128)} fusion(f32[128,512]{1,0:T(8,128)S(1)} %copy-done.1, f32[128,512]{1,0:T(8,128)} %reduce-scatter.5.cloned.1.call-done), kind=kLoop, calls=%fused_computation.28 | loop fusion | flops 262144 | bytes 786432 | tf_op jit(solution)/shard_map/add | solution.py:44
  160.6 1.0 copy.9
  (21 shorter events, 0.1 us)
Async XLA Ops:
  7.2 32.0 %all-gather.3.cloned.1.call-start = ((), (), s32[]{:S(2)}) async-start(), calls=%async_computation.2 | async-start | bytes 1310720 | tf_op jit(solution)/shard_map/all_gather | solution.py:25
  7.9 75.8 %reduce-scatter.3.cloned.1.call-start = ((), (), s32[]{:S(2)}) async-start(), calls=%async_computation.3 | async-start | bytes 1310720 | tf_op jit(solution)/shard_map/reduce_scatter | solution.py:43
  8.7 6.6 %copy-start.5 = (s32[2,1]{0,1:T(1,128)S(1)}, s32[2,1]{0,1:T(1,128)}, u32[]{:S(2)}) copy-start(s32[2,1]{0,1:T(1,128)} %param.11) | copy-start | bytes 28
  8.8 7.2 %copy-start.3 = (s32[2,1024]{1,0:T(2,128)S(1)}, s32[2,1024]{1,0:T(2,128)}, u32[]{:S(2)}) copy-start(s32[2,1024]{1,0:T(2,128)} %param.9) | copy-start | bytes 24580
  8.8 7.2 %copy-start.4 = (f32[2,1024]{1,0:T(2,128)S(1)}, f32[2,1024]{1,0:T(2,128)}, u32[]{:S(2)}) copy-start(f32[2,1024]{1,0:T(2,128)} %param.8) | copy-start | bytes 24580
  47.0 36.7 %copy-start.2 = (f32[128,512]{1,0:T(8,128)S(1)}, f32[128,512]{1,0:T(8,128)}, u32[]{:S(2)}) copy-start(f32[128,512]{1,0:T(8,128)} %param.6) | copy-start | bytes 786436
  55.8 37.8 %copy-start = (f32[512,512]{1,0:T(8,128)S(1)}, f32[512,512]{1,0:T(8,128)}, u32[]{:S(2)}) copy-start(f32[512,512]{1,0:T(8,128)} %param.7) | copy-start | bytes 3145732
  55.8 60.5 %all-gather.5.cloned.1.call-start = ((), (), s32[]{:S(2)}) async-start(), calls=%async_computation.4 | async-start | bytes 1310720 | tf_op jit(solution)/shard_map/all_gather | solution.py:25
  85.4 73.5 %reduce-scatter.5.cloned.1.call-start = ((), (), s32[]{:S(2)}) async-start(), calls=%async_computation.5 | async-start | bytes 1310720 | tf_op jit(solution)/shard_map/reduce_scatter | solution.py:43
  95.1 16.3 %collective-permute-start = (f32[512,512]{1,0:T(8,128)S(1)}, f32[512,512]{1,0:T(8,128)S(1)}, u32[]{:S(2)}, u32[]{:S(2)}) collective-permute-start(f32[512,512]{1,0:T(8,128)S(1)} %multiply_add_fusion.1), channel_id=1, source_target_pairs={{0,4},{4,8},{8,12},{12,16},{16,20},{20,24},{24,28},{28,0},{1,5},{5... | collective-permute-start | bytes 3145736 | tf_op jit(solution)/shard_map/ppermute | solution.py:10
  140.9 17.9 %copy-start.1 = (f32[128,512]{1,0:T(8,128)S(1)}, f32[128,512]{1,0:T(8,128)}, u32[]{:S(2)}) copy-start(f32[128,512]{1,0:T(8,128)} %multiply_add_fusion.3) | copy-start | bytes 786436
  142.5 12.4 %collective-permute-start.1 = (f32[512,512]{1,0:T(8,128)S(1)}, f32[512,512]{1,0:T(8,128)S(1)}, u32[]{:S(2)}, u32[]{:S(2)}) collective-permute-start(f32[512,512]{1,0:T(8,128)S(1)} %multiply_add_fusion), channel_id=1, source_target_pairs={{0,28},{4,0},{8,4},{12,8},{16,12},{20,16},{24,20},{28,24},{1,29},{... | collective-permute-start | bytes 3145736 | tf_op jit(solution)/shard_map/ppermute | solution.py:10
Sparse Core Ops, SparseCore 0:
  9.8 29.3 all-gather.2
  55.9 27.7 reduce-scatter.2
  86.2 26.6 all-gather.4
  132.9 25.8 reduce-scatter.4
where the time goes:
time: 169 us; the launch traced here: 168 us
  waiting for transfers between devices  84.1 us (50%)
  other arithmetic  46.1 us (27%)
  local copies, waits for them, and re-layouts  23.5 us (14%)
  between operations  13.9 us (8%)
    reduce_scatter x2, waiting for transfers between devices, on_device(): lax.psum_scatter(grad_u, 'strata', scatter_dimension=0, tiled=True)  31.8 us
    ppermute x2, waiting for transfers between devices, passed_along(): return lax.ppermute(value, axis, pairs)  28.3 us
    all_gather x2, waiting for transfers between devices, gather_users(): return lax.all_gather(owned_rows, 'strata', axis=0, tiled=True)  23.2 us
    scatter-add x2, other arithmetic, tile_grads(): jnp.zeros_like(block_u).at[user_index].add(errors[:, None] * v_rows)  17.6 us
    scatter-add x2, other arithmetic, tile_grads(): jnp.zeros_like(block_v).at[item_index].add(errors[:, None] * u_rows)  16.2 us
    gather x2, local copies, waits for them, and re-layouts, tile_grads(): v_rows = block_v[item_index]  11.4 us
    gather x2, local copies, waits for them, and re-layouts, tile_grads(): u_rows = block_u[user_index]  10.5 us
    reduce_sum x2, other arithmetic, tile_grads(): errors = active_mask * (observed - jnp.sum(u_rows * v_rows, axis=1))  3.7 us
  transfers between devices with their start and end apart: 6, of which 5 were waited for; matrix products, arithmetic and copies ran while one was open for 19% of the time, Pallas kernels for 0%

commit v1 on v0

v1 whole, which is shorter than its diff:
```python
import functools

import jax
import jax.numpy as jnp
from jax import lax
from jax.experimental import pallas as pl
from jax.experimental.pallas import tpu as pltpu
from jax.sharding import PartitionSpec as P

TOUCHED = 32
WHOLE = (0, 1, 2)

F32 = jnp.float32
BF16 = jnp.bfloat16

NN = (((1,), (0,)), ((), ()))
NT = (((1,), (1,)), ((), ()))
TN = (((0,), (0,)), ((), ()))


def dot(a, b, dims):
    return lax.dot_general(a, b, dims, preferred_element_type=F32)


def split2(x):
    hi = x.astype(BF16)
    return hi, (x - hi.astype(F32)).astype(BF16)


def split3(x):
    hi = x.astype(BF16)
    rest = x - hi.astype(F32)
    mid = rest.astype(BF16)
    return hi, mid, (rest - mid.astype(F32)).astype(BF16)


def pick(selector, x, dims):
    hi, mid, lo = split3(x)
    return (dot(selector, hi, dims) + dot(selector, mid, dims)) + dot(selector, lo, dims)


def iota(shape, dim):
    return lax.broadcasted_iota(jnp.int32, shape, dim)


def one_hot(names, rows):
    return (iota((rows, names.shape[1]), 0) == names).astype(F32).astype(BF16)


def run_selector(hot):
    run, entries = hot.shape
    counted = dot(jnp.ones((8, entries), BF16), hot, NT)
    present = (counted > 0).astype(F32)
    before = (iota((run, run), 0) < iota((run, run), 1)).astype(F32).astype(BF16)
    rank = dot(present.astype(BF16), before, NN)
    wanted = iota((TOUCHED, run), 0).astype(F32)
    return ((rank[:1] == wanted).astype(F32) * present[:1]).astype(BF16)


def call(kernel, outs, *args, smem=(), flops=0):
    in_specs = [
        pl.BlockSpec(memory_space=pltpu.SMEM if at in smem else pltpu.VMEM) for at in range(len(args))
    ]
    size = sum(a.size * a.dtype.itemsize for a in args) + sum(o.size * o.dtype.itemsize for o in outs)
    return pl.pallas_call(
        kernel,
        out_shape=list(outs),
        in_specs=in_specs,
        out_specs=[pl.BlockSpec(memory_space=pltpu.VMEM)] * len(outs),
        compiler_params=pltpu.CompilerParams(vmem_limit_bytes=24 * 2**20),
        cost_estimate=pl.CostEstimate(flops=flops, bytes_accessed=size, transcendentals=0),
    )(*args)


def shaped(shape, dtype=F32):
    return jax.ShapeDtypeStruct(shape, dtype)


def pack_kernel(run, at_ref, user_ref, item_ref, rating_ref, count_ref, *out_refs):
    me = at_ref[0, 0]
    for t, out_ref in enumerate(out_refs):
        users = user_ref[t : t + 1, :]
        group = lax.div(users, run)
        users = (group ^ me) * run + (users - group * run)
        active = (iota(users.shape, 1) < count_ref[t, 0]).astype(F32)
        out_ref[0:1, :] = users.astype(F32)
        out_ref[1:2, :] = item_ref[t : t + 1, :].astype(F32)
        out_ref[2:3, :] = rating_ref[t : t + 1, :]
        out_ref[3:4, :] = active


def prep_kernel(run, entry_ref, sel_ref, n_ref, r_ref):
    users = entry_ref[0:1, :].astype(jnp.int32)
    items = entry_ref[1:2, :].astype(jnp.int32)
    active = entry_ref[3:4, :]
    values = split3(entry_ref[2:3, :] * active)
    weights = [active] + [v.astype(F32) for v in values]
    touched = sel_ref.shape[0]
    hots = []
    for k in range(touched // TOUCHED):
        hot = one_hot(users - k * run, run)
        sel = run_selector(hot)
        sel_ref[k * TOUCHED : (k + 1) * TOUCHED, :] = sel
        hots.append(dot(sel, hot, NN))
    hots = jnp.concatenate(hots, axis=0)
    left = jnp.concatenate([(hots * w).astype(BF16) for w in weights], axis=0)
    table = dot(left, one_hot(items, n_ref.shape[1]), NT)
    n_ref[...] = table[:touched]
    r_ref[...] = (table[touched : 2 * touched] + table[2 * touched : 3 * touched]) + table[3 * touched :]


def owner_selector(names, me, run):
    return run_selector(one_hot(names - me * run, run))


def first_rows_kernel(run, at_ref, names_ref, own_ref, out_ref):
    out_ref[...] = pick(owner_selector(names_ref[0:1, :], at_ref[0, 0], run), own_ref[...], NN)


def selectors_kernel(run, n, at_ref, *refs):
    names, outs = refs[:n], refs[n:]
    for t, out_ref in enumerate(outs):
        for k in range(n):
            out_ref[k * TOUCHED : (k + 1) * TOUCHED, :] = owner_selector(names[k][t : t + 1, :], at_ref[0, 0], run)


def tile_kernel(n, whole, *refs):
    rows, refs = refs[:n], refs[n:]
    if whole:
        sel_ref, refs = refs[0], refs[1:]
    n_ref, r_ref, v_ref = refs[:3]
    outs, (uh_ref, ul_ref, wh_ref, wl_ref) = refs[3 : 3 + n], refs[3 + n :]
    for k in range(n):
        part = slice(k * TOUCHED, (k + 1) * TOUCHED)
        hi, lo = split2(rows[k][...])
        if k in whole:
            sel = sel_ref[part, :]
            hi, lo = dot(sel, hi, NN).astype(BF16), dot(sel, lo, NN).astype(BF16)
        uh_ref[part, :] = hi
        ul_ref[part, :] = lo
    uh, ul = uh_ref[...], ul_ref[...]
    vh, vl = split2(v_ref[...])
    products = dot(uh, vh, NT) + (dot(ul, vh, NT) + dot(uh, vl, NT))
    wh, wl = split2(r_ref[...] - n_ref[...] * products)
    wh_ref[...] = wh
    wl_ref[...] = wl
    grads = dot(wh, vh, NN) + (dot(wl, vh, NN) + dot(wh, vl, NN))
    for k in range(n):
        outs[k][...] = grads[k * TOUCHED : (k + 1) * TOUCHED]


def items_kernel(step, uh_ref, ul_ref, wh_ref, wl_ref, v_ref, out_ref):
    uh, ul, wh, wl = uh_ref[...], ul_ref[...], wh_ref[...], wl_ref[...]
    grads = dot(wh, uh, TN) + (dot(wl, uh, TN) + dot(wh, ul, TN))
    v = v_ref[...]
    out_ref[...] = v + step * (grads - 0.1 * v)


def owner_kernel(n, step, *refs):
    parts, (sel_ref, own_ref), refs = refs[:n], refs[n : n + 2], refs[n + 2 :]
    grads = pick(sel_ref[...], jnp.concatenate([part[...] for part in parts], axis=0), TN)
    own = own_ref[...]
    own = own + step * (grads - 0.1 * own)
    if len(refs) == 1:
        refs[0][...] = own
        return
    next_ref, out_ref, outs = refs[0], refs[1], refs[2:]
    out_ref[...] = own
    rows = pick(next_ref[...], own, NN)
    for k in range(n):
        outs[k][...] = rows[k * TOUCHED : (k + 1) * TOUCHED]


def on_device(user_factors, item_factors, ratings, user_offsets, item_offsets, counts):
    n, row_count = lax.axis_size("strata"), lax.axis_size("rows")
    run, rank = user_factors.shape
    items = item_factors.shape[0]
    subs, entries = ratings.shape
    touched = n * TOUCHED
    me = lax.axis_index("strata").astype(jnp.int32).reshape(1, 1)

    def exchange(value, k, shift=0):
        pairs = [
            (r * n + s, ((r + shift) % row_count) * n + (s ^ k)) for r in range(row_count) for s in range(n)
        ]
        if k == 0 and shift == 0:
            return value
        return lax.ppermute(value, ("rows", "strata"), pairs)

    whole = tuple(k for k in WHOLE if k < n)
    names = [None] * n
    names[0] = user_offsets
    for k in range(n):
        if k not in whole:
            names[k] = exchange(user_offsets, k)
    rows = [None] * n
    for k in whole:
        rows[k] = exchange(user_factors, k)
    for k in range(n):
        if k not in whole:
            mine = call(
                functools.partial(first_rows_kernel, run), [shaped((TOUCHED, rank))],
                me, names[k], user_factors, smem=(0,),
            )[0]
            rows[k] = exchange(mine, k)
    for k in whole[1:]:
        names[k] = exchange(user_offsets, k)

    packed = call(
        functools.partial(pack_kernel, run), [shaped((4, entries))] * subs,
        me, user_offsets, item_offsets, ratings, counts, smem=(0, 4),
    )
    selectors = call(
        functools.partial(selectors_kernel, run, n), [shaped((touched, run), BF16)] * subs,
        me, *names, smem=(0,),
    )

    own, block = user_factors, item_factors
    for t in range(subs):
        step = 0.04 / (1.0 + 0.5 * t)
        here = packed[t] if t == 0 else exchange(packed[t], 0, -t)
        sel, n_table, r_table = call(
            functools.partial(prep_kernel, run),
            [shaped((touched, run), BF16), shaped((touched, items)), shaped((touched, items))],
            here, flops=8 * touched * entries * items,
        )
        now_whole = whole if t == 0 else ()
        outs = call(
            functools.partial(tile_kernel, n, now_whole),
            [shaped((TOUCHED, rank))] * n + [shaped((touched, rank), BF16)] * 2 + [shaped((touched, items), BF16)] * 2,
            *rows, *([sel] if now_whole else []), n_table, r_table, block, flops=12 * touched * rank * items,
        )
        grads, saved = outs[:n], outs[n:]
        parts = [exchange(grads[k], k, t) for k in range(n)]
        block = call(
            functools.partial(items_kernel, step), [shaped(block.shape)], *saved, block,
            flops=6 * touched * rank * items,
        )[0]
        if t + 1 < subs:
            own, *mine = call(
                functools.partial(owner_kernel, n, step), [shaped(own.shape)] + [shaped((TOUCHED, rank))] * n,
                *parts, selectors[t], own, selectors[t + 1], flops=12 * touched * rank * run,
            )
            rows = [exchange(mine[k], k, -(t + 1)) for k in range(n)]
        else:
            own = call(
                functools.partial(owner_kernel, n, step), [shaped(own.shape)],
                *parts, selectors[t], own, flops=6 * touched * rank * run,
            )[0]
    return own, block


def solution(mesh):
    return jax.shard_map(
        on_device,
        mesh=mesh,
        in_specs=(
            P(("rows", "strata"), None),
            P(("rows", "strata"), None),
            P(None, ("rows", "strata")),
            P(None, ("rows", "strata")),
            P(None, ("rows", "strata")),
            P(None, ("rows", "strata")),
        ),
        out_specs=(P(("rows", "strata"), None), P(("rows", "strata"), None)),
        check_vma=False,
    )
```

time: 169 us -> 52.2 us (0.31)
  waiting for transfers between devices: 84.1 us -> 15.2 us
  other arithmetic: 46.1 us -> 0 us
  local copies, waits for them, and re-layouts: 23.5 us -> 1.07 us
  starting transfers between devices: 0.45 us -> 21.2 us
  Pallas kernels: 0 us -> 13.9 us
  between operations: 13.9 us -> 0.78 us
    scatter-add x4 -> x0, other arithmetic: 33.8 us -> none  [the longest x2 17.6 us: tile_grads(): jnp.zeros_like(block_u).at[user_index].add(errors[:, None] * v_rows)]
    reduce_scatter x2 -> x0, waiting for transfers between devices: 31.8 us -> none  [on_device(): lax.psum_scatter(grad_u, 'strata', scatter_dimension=0, tiled=True)]
    all_gather x2 -> x0, waiting for transfers between devices: 23.2 us -> none  [gather_users(): return lax.all_gather(owned_rows, 'strata', axis=0, tiled=True)]
    gather x4 -> x0, local copies, waits for them, and re-layouts: 21.9 us -> none  [the longest x2 11.4 us: tile_grads(): v_rows = block_v[item_index]]
    ppermute x2 -> x18, starting transfers between devices: 0.3 us -> 21.2 us  [exchange(): return lax.ppermute(value, ('rows', 'strata'), pairs)]
    pallas_call x0 -> x11, Pallas kernels: none -> 13.9 us  [call(): pl.pallas_call(kernel, out_shape=list(outs), in_specs=in_specs, out_specs...]
    ppermute x2 -> x18, waiting for transfers between devices: 28.3 us -> 15.2 us  [exchange(): return lax.ppermute(value, ('rows', 'strata'), pairs)]
    add x4 -> x0, other arithmetic: 6.53 us -> none  [the longest x2 3.41 us: on_device(): owned_rows = owned_rows + step_size * (owned_share - 0.1 * owned_rows)]
  transfers between devices with their start and end apart: 6 -> 18, of which waited for: 5 -> 8; matrix products, arithmetic and copies ran while one was open for 19% -> 0% of each run, Pallas kernels for 0% -> 21%
where the time goes in v1:
time: 52.2 us; the launch traced here: 52.1 us
  starting transfers between devices  21.2 us (41%)
  waiting for transfers between devices  15.2 us (29%)
  Pallas kernels  13.9 us (27%)
  local copies, waits for them, and re-layouts  1.07 us (2%)
  between operations  0.78 us (1%)
    ppermute x18, starting transfers between devices, exchange(): return lax.ppermute(value, ('rows', 'strata'), pairs)  21.2 us
    ppermute x18, waiting for transfers between devices, exchange(): return lax.ppermute(value, ('rows', 'strata'), pairs)  15.2 us
    pallas_call x11, Pallas kernels, call(): pl.pallas_call(kernel, out_shape=list(outs), in_specs=in_specs, out_specs...  13.9 us
    unnamed x15, local copies, waits for them, and re-layouts  1.07 us
  transfers between devices with their start and end apart: 18, of which 8 were waited for; matrix products, arithmetic and copies ran while one was open for 0% of the time, Pallas kernels for 21%

profile of v1, /device:TPU:0, one launch (start us, length us, event | category | flops | bytes accessed | tf_op | source)
XLA Modules:
  0.0 52.1 jit_solution(14307496531072038133)
XLA Ops:
  0.6 3.0 %collective-permute-start = (f32[128,512]{1,0:T(8,128)}, f32[128,512]{1,0:T(8,128)S(1)}, u32[]{:S(2)}, u32[]{:S(2)}) collective-permute-start(f32[128,512]{1,0:T(8,128)} %refs_5_.1), channel_id=1, source_target_pairs={{0,1},{1,0},{2,3},{3,2},{4,5},{5,4},{6,7},{7,6},{8,9},{9,8},{10,11... | collective-permute-start | bytes 786440 | tf_op jit(solution)/shard_map/ppermute | solution.py:188
  3.6 1.5 %collective-permute-start.1 = (f32[128,512]{1,0:T(8,128)}, f32[128,512]{1,0:T(8,128)S(1)}, u32[]{:S(2)}, u32[]{:S(2)}) collective-permute-start(f32[128,512]{1,0:T(8,128)} %refs_5_.1), channel_id=1, source_target_pairs={{0,2},{1,3},{2,0},{3,1},{4,6},{5,7},{6,4},{7,5},{8,10},{9,11},{10,... | collective-permute-start | bytes 786440 | tf_op jit(solution)/shard_map/ppermute | solution.py:188
  5.2 6.5 %collective-permute-done.2.names_ref.refs_3_ = s32[2,1024]{1,0:T(2,128)S(1)} collective-permute-done((s32[2,1024]{1,0:T(2,128)}, s32[2,1024]{1,0:T(2,128)S(1)}, u32[]{:S(2)}, u32[]{:S(2)}) %collective-permute-start.2) | collective-permute-done | bytes 8224 | tf_op jit(solution)/shard_map/ppermute | solution.py:188
  11.6 0.9 %copy-done.1 = f32[128,512]{1,0:T(8,128)S(1)} copy-done((f32[128,512]{1,0:T(8,128)S(1)}, f32[128,512]{1,0:T(8,128)}, u32[]{:S(2)}) %copy-start.1) | copy-done | bytes 262168
  13.2 1.5 %collective-permute-start.3 = (f32[32,512]{1,0:T(8,128)S(1)}, f32[32,512]{1,0:T(8,128)S(1)}, u32[]{:S(2)}, u32[]{:S(2)}) collective-permute-start(f32[32,512]{1,0:T(8,128)S(1)} %shard_map.77), channel_id=1, source_target_pairs={{0,3},{1,2},{2,1},{3,0},{4,7},{5,6},{6,5},{7,4},{8,11},{9,10},{10,... | collective-permute-start | bytes 196616 | tf_op jit(solution)/shard_map/ppermute | solution.py:188
  14.8 0.6 %shard_map.78 = (f32[4,1024]{1,0:T(4,128)S(1)}, f32[4,1024]{1,0:T(4,128)S(1)}) custom-call(s32[1,1]{1,0:T(1,128)} %bitcast.at_ref, s32[2,1024]{1,0:T(2,128)S(1)} %copy-done.3, s32[2,1024]{1,0:T(2,128)S(1)} %copy-done.4, f32[2,1024]{1,0:T(2,128)S(1)} %copy-done.5, s32[2,1]{1,0:T(2,128)S(1)} %copy.8.count_ref), custom_call_target="tpu_custom_call" | custom-call | bytes 57356 | tf_op jit(solution)/shard_map/pallas_call | solution.py:65
  15.4 2.4 %shard_map.79 = (bf16[128,128]{1,0:T(8,128)(2,1)S(1)}, f32[128,512]{1,0:T(8,128)S(1)}, f32[128,512]{1,0:T(8,128)S(1)}) custom-call(f32[4,1024]{1,0:T(4,128)S(1)} %get-tuple-element.32.entry_ref), custom_call_target="tpu_custom_call" | custom-call | flops 536870912 | bytes 573440 | tf_op jit(solution)/shard_map/pallas_call | solution.py:65
  17.8 0.6 %collective-permute-done.3.refs_3_ = f32[32,512]{1,0:T(8,128)S(1)} collective-permute-done((f32[32,512]{1,0:T(8,128)S(1)}, f32[32,512]{1,0:T(8,128)S(1)}, u32[]{:S(2)}, u32[]{:S(2)}) %collective-permute-start.3) | collective-permute-done | bytes 65568 | tf_op jit(solution)/shard_map/ppermute | solution.py:188
  18.4 1.1 %shard_map.80 = (f32[32,512]{1,0:T(8,128)S(1)}, f32[32,512]{1,0:T(8,128)S(1)}, f32[32,512]{1,0:T(8,128)S(1)}, f32[32,512]{1,0:T(8,128)S(1)}, bf16[128,512]{1,0:T...) custom-call(f32[128,512]{1,0:T(8,128)S(1)} %copy-done.2, ...), custom_call_target="tpu_custom_call" | custom-call | flops 402653184 | bytes 3244032 | tf_op jit(solution)/shard_map/pallas_call | solution.py:65
  19.5 1.5 %collective-permute-start.4 = (f32[32,512]{1,0:T(8,128)S(1)}, f32[32,512]{1,0:T(8,128)S(1)}, u32[]{:S(2)}, u32[]{:S(2)}) collective-permute-start(f32[32,512]{1,0:T(8,128)S(1)} %get-tuple-element.37), channel_id=1, source_target_pairs={{0,1},{1,0},{2,3},{3,2},{4,5},{5,4},{6,7},{7,6},{8,9},{9,8},{10,11... | collective-permute-start | bytes 196616 | tf_op jit(solution)/shard_map/ppermute | solution.py:188
  21.0 0.6 %collective-permute-start.5 = (f32[32,512]{1,0:T(8,128)S(1)}, f32[32,512]{1,0:T(8,128)S(1)}, u32[]{:S(2)}, u32[]{:S(2)}) collective-permute-start(f32[32,512]{1,0:T(8,128)S(1)} %get-tuple-element.38), channel_id=1, source_target_pairs={{0,2},{1,3},{2,0},{3,1},{4,6},{5,7},{6,4},{7,5},{8,10},{9,11},{10,... | collective-permute-start | bytes 196616 | tf_op jit(solution)/shard_map/ppermute | solution.py:188
  21.6 1.5 %collective-permute-start.6 = (f32[32,512]{1,0:T(8,128)S(1)}, f32[32,512]{1,0:T(8,128)S(1)}, u32[]{:S(2)}, u32[]{:S(2)}) collective-permute-start(f32[32,512]{1,0:T(8,128)S(1)} %get-tuple-element.39), channel_id=1, source_target_pairs={{0,3},{1,2},{2,1},{3,0},{4,7},{5,6},{6,5},{7,4},{8,11},{9,10},{10,... | collective-permute-start | bytes 196616 | tf_op jit(solution)/shard_map/ppermute | solution.py:188
  23.1 1.4 %collective-permute-start.7 = (s32[2,1024]{1,0:T(2,128)S(1)}, s32[2,1024]{1,0:T(2,128)S(1)}, u32[]{:S(2)}, u32[]{:S(2)}) collective-permute-start(s32[2,1024]{1,0:T(2,128)S(1)} %copy-done.3), channel_id=1, source_target_pairs={{0,1},{1,0},{2,3},{3,2},{4,5},{5,4},{6,7},{7,6},{8,9},{9,8},{10,11... | collective-permute-start | bytes 24584 | tf_op jit(solution)/shard_map/ppermute | solution.py:188
  24.5 0.6 %collective-permute-start.8 = (s32[2,1024]{1,0:T(2,128)S(1)}, s32[2,1024]{1,0:T(2,128)S(1)}, u32[]{:S(2)}, u32[]{:S(2)}) collective-permute-start(s32[2,1024]{1,0:T(2,128)S(1)} %copy-done.3), channel_id=1, source_target_pairs={{0,2},{1,3},{2,0},{3,1},{4,6},{5,7},{6,4},{7,5},{8,10},{9,11},{10,... | collective-permute-start | bytes 24584 | tf_op jit(solution)/shard_map/ppermute | solution.py:188
  25.1 1.7 %collective-permute-done.7.refs_1_ = s32[2,1024]{1,0:T(2,128)S(1)} collective-permute-done((s32[2,1024]{1,0:T(2,128)S(1)}, s32[2,1024]{1,0:T(2,128)S(1)}, u32[]{:S(2)}, u32[]{:S(2)}) %collective-permute-start.7) | collective-permute-done | bytes 8224 | tf_op jit(solution)/shard_map/ppermute | solution.py:188
  26.8 1.3 %collective-permute-done.8.refs_2_ = s32[2,1024]{1,0:T(2,128)S(1)} collective-permute-done((s32[2,1024]{1,0:T(2,128)S(1)}, s32[2,1024]{1,0:T(2,128)S(1)}, u32[]{:S(2)}, u32[]{:S(2)}) %collective-permute-start.8) | collective-permute-done | bytes 8224 | tf_op jit(solution)/shard_map/ppermute | solution.py:188
  28.1 2.1 %shard_map.81 = (bf16[128,128]{1,0:T(8,128)(2,1)S(1)}, bf16[128,128]{1,0:T(8,128)(2,1)S(1)}) custom-call(s32[1,1]{1,0:T(1,128)} %bitcast.at_ref, s32[2,1024]{1,0:T(2,128)S(1)} %copy-done.3, s32[2,1024]{1,0:T(2,128)S(1)} %collective-permute-done.7.refs_1_, s32[2,1024]{1,0:T(2,128)S(1)} %collective-permute-done.8.refs_2_, ...), custom_call_target="tpu_custom_call" | custom-call | bytes 98308 | tf_op jit(solution)/shard_map/pallas_call | solution.py:65
  30.8 2.4 %collective-permute-start.9 = (f32[32,512]{1,0:T(8,128)S(1)}, f32[32,512]{1,0:T(8,128)S(1)}, u32[]{:S(2)}, u32[]{:S(2)}) collective-permute-start(f32[32,512]{1,0:T(8,128)S(1)} %get-tuple-element.42), channel_id=1, source_target_pairs={{0,28},{1,29},{2,30},{3,31},{4,0},{5,1},{6,2},{7,3},{8,4},{9,5},{1... | collective-permute-start | bytes 196616 | tf_op jit(solution)/shard_map/ppermute | solution.py:188
  33.3 1.4 %collective-permute-start.10 = (f32[32,512]{1,0:T(8,128)S(1)}, f32[32,512]{1,0:T(8,128)S(1)}, u32[]{:S(2)}, u32[]{:S(2)}) collective-permute-start(f32[32,512]{1,0:T(8,128)S(1)} %get-tuple-element.43), channel_id=1, source_target_pairs={{0,29},{1,28},{2,31},{3,30},{4,1},{5,0},{6,3},{7,2},{8,5},{9,4},{1... | collective-permute-start | bytes 196616 | tf_op jit(solution)/shard_map/ppermute | solution.py:188
  35.2 1.9 %collective-permute-start.12 = (f32[32,512]{1,0:T(8,128)S(1)}, f32[32,512]{1,0:T(8,128)S(1)}, u32[]{:S(2)}, u32[]{:S(2)}) collective-permute-start(f32[32,512]{1,0:T(8,128)S(1)} %get-tuple-element.45), channel_id=1, source_target_pairs={{0,31},{1,30},{2,29},{3,28},{4,3},{5,2},{6,1},{7,0},{8,7},{9,6},{1... | collective-permute-start | bytes 196616 | tf_op jit(solution)/shard_map/ppermute | solution.py:188
  37.1 2.4 %shard_map.83 = (bf16[128,128]{1,0:T(8,128)(2,1)}, f32[128,512]{1,0:T(8,128)S(1)}, f32[128,512]{1,0:T(8,128)S(1)}) custom-call(f32[4,1024]{1,0:T(4,128)S(1)} %collective-permute-done.13.entry_ref), custom_call_target="tpu_custom_call" | custom-call | flops 536870912 | bytes 573440 | tf_op jit(solution)/shard_map/pallas_call | solution.py:65
  39.6 0.6 %shard_map.84.refs_6_.v_ref = f32[512,512]{1,0:T(8,128)S(1)} custom-call(bf16[128,512]{1,0:T(8,128)(2,1)S(1)} %get-tuple-element.49.uh_ref, bf16[128,512]{1,0:T(8,128)(2,1)S(1)} %get-tuple-element.50.ul_ref, bf16[128,512]{1,0:T(8,128)(2,1)S(1)} %get-tuple-element.51.wh_ref, bf16[128,512]{1,0:T(8,128)(2,1)S(1)} %get-tuple-element.52.wl_ref, ...), custom_call_target="tpu_custom_call" | custom-call | flops 201326592 | bytes 2621440 | tf_op jit(solution)/shard_map/pallas_call | solution.py:65
  40.2 0.9 %shard_map.85 = (f32[32,512]{1,0:T(8,128)S(1)}, f32[32,512]{1,0:T(8,128)S(1)}, f32[32,512]{1,0:T(8,128)S(1)}, f32[32,512]{1,0:T(8,128)S(1)}, bf16[128,512]{1,0:T...) custom-call(f32[32,512]{1,0:T(8,128)S(1)} %collective-permute-done.9.refs, ...), custom_call_target="tpu_custom_call" | custom-call | flops 402653184 | bytes 2621440 | tf_op jit(solution)/shard_map/pallas_call | solution.py:65
  41.2 1.0 %collective-permute-start.14 = (f32[32,512]{1,0:T(8,128)S(1)}, f32[32,512]{1,0:T(8,128)S(1)}, u32[]{:S(2)}, u32[]{:S(2)}) collective-permute-start(f32[32,512]{1,0:T(8,128)S(1)} %get-tuple-element.53), channel_id=1, source_target_pairs={{0,4},{1,5},{2,6},{3,7},{4,8},{5,9},{6,10},{7,11},{8,12},{9,13},{1... | collective-permute-start | bytes 196616 | tf_op jit(solution)/shard_map/ppermute | solution.py:188
  42.2 1.1 %collective-permute-start.15 = (f32[32,512]{1,0:T(8,128)S(1)}, f32[32,512]{1,0:T(8,128)S(1)}, u32[]{:S(2)}, u32[]{:S(2)}) collective-permute-start(f32[32,512]{1,0:T(8,128)S(1)} %get-tuple-element.54), channel_id=1, source_target_pairs={{0,5},{1,4},{2,7},{3,6},{4,9},{5,8},{6,11},{7,10},{8,13},{9,12},{1... | collective-permute-start | bytes 196616 | tf_op jit(solution)/shard_map/ppermute | solution.py:188
  43.5 1.0 %collective-permute-start.17 = (f32[32,512]{1,0:T(8,128)S(1)}, f32[32,512]{1,0:T(8,128)S(1)}, u32[]{:S(2)}, u32[]{:S(2)}) collective-permute-start(f32[32,512]{1,0:T(8,128)S(1)} %get-tuple-element.56), channel_id=1, source_target_pairs={{0,7},{1,6},{2,5},{3,4},{4,11},{5,10},{6,9},{7,8},{8,15},{9,14},{1... | collective-permute-start | bytes 196616 | tf_op jit(solution)/shard_map/ppermute | solution.py:188
  44.5 1.6 %shard_map.87 = f32[512,512]{1,0:T(8,128)} custom-call(bf16[128,512]{1,0:T(8,128)(2,1)S(1)} %get-tuple-element.58.uh_ref, bf16[128,512]{1,0:T(8,128)(2,1)S(1)} %get-tuple-element.59.ul_ref, bf16[128,512]{1,0:T(8,128)(2,1)S(1)} %get-tuple-element.60.wh_ref, bf16[128,512]{1,0:T(8,128)(2,1)S(1)} %get-tuple-element.61.wl_ref, f32[512,512]{1,0:T(8,128)S(1)} %shard_map.84.refs_6_.v_ref), custom_call_target="tpu_custom_call" | custom-call | flops 201326592 | bytes 2621440 | tf_op jit(solution)/shard_map/pallas_call | solution.py:65
  46.1 0.7 %collective-permute-done.14.refs_0_ = f32[32,512]{1,0:T(8,128)S(1)} collective-permute-done((f32[32,512]{1,0:T(8,128)S(1)}, f32[32,512]{1,0:T(8,128)S(1)}, u32[]{:S(2)}, u32[]{:S(2)}) %collective-permute-start.14) | collective-permute-done | bytes 65568 | tf_op jit(solution)/shard_map/ppermute | solution.py:188
  46.7 1.9 %collective-permute-done.15.refs_1_ = f32[32,512]{1,0:T(8,128)S(1)} collective-permute-done((f32[32,512]{1,0:T(8,128)S(1)}, f32[32,512]{1,0:T(8,128)S(1)}, u32[]{:S(2)}, u32[]{:S(2)}) %collective-permute-start.15) | collective-permute-done | bytes 65568 | tf_op jit(solution)/shard_map/ppermute | solution.py:188
  48.6 1.1 %collective-permute-done.16.refs_2_ = f32[32,512]{1,0:T(8,128)S(1)} collective-permute-done((f32[32,512]{1,0:T(8,128)S(1)}, f32[32,512]{1,0:T(8,128)S(1)}, u32[]{:S(2)}, u32[]{:S(2)}) %collective-permute-start.16) | collective-permute-done | bytes 65568 | tf_op jit(solution)/shard_map/ppermute | solution.py:188
  49.8 1.3 %collective-permute-done.17.refs_3_ = f32[32,512]{1,0:T(8,128)S(1)} collective-permute-done((f32[32,512]{1,0:T(8,128)S(1)}, f32[32,512]{1,0:T(8,128)S(1)}, u32[]{:S(2)}, u32[]{:S(2)}) %collective-permute-start.17) | collective-permute-done | bytes 65568 | tf_op jit(solution)/shard_map/ppermute | solution.py:188
  51.1 1.0 %shard_map.86 = f32[128,512]{1,0:T(8,128)} custom-call(f32[32,512]{1,0:T(8,128)S(1)} %collective-permute-done.14.refs_0_, f32[32,512]{1,0:T(8,128)S(1)} %collective-permute-done.15.refs_1_, f32[32,512]{1,0:T(8,128)S(1)} %collective-permute-done.16.refs_2_, f32[32,512]{1,0:T(8,128)S(1)} %collective-permute-done.17.refs_3_, ...), custom_call_target="tpu_custom_call" | custom-call | flops 50331648 | bytes 819200 | tf_op jit(solution)/shard_map/pallas_call | solution.py:65
  (30 shorter events, 2.1 us)
Async XLA Ops:
  0.6 17.8 %collective-permute-start = (f32[128,512]{1,0:T(8,128)}, f32[128,512]{1,0:T(8,128)S(1)}, u32[]{:S(2)}, u32[]{:S(2)}) collective-permute-start(f32[128,512]{1,0:T(8,128)} %refs_5_.1), channel_id=1, source_target_pairs={{0,1},{1,0},{2,3},{3,2},{4,5},{5,4},{6,7},{7,6},{8,9},{9,8},{10,11... | collective-permute-start | bytes 786440 | tf_op jit(solution)/shard_map/ppermute | solution.py:188
  3.6 14.8 %collective-permute-start.1 = (f32[128,512]{1,0:T(8,128)}, f32[128,512]{1,0:T(8,128)S(1)}, u32[]{:S(2)}, u32[]{:S(2)}) collective-permute-start(f32[128,512]{1,0:T(8,128)} %refs_5_.1), channel_id=1, source_target_pairs={{0,2},{1,3},{2,0},{3,1},{4,6},{5,7},{6,4},{7,5},{8,10},{9,11},{10,... | collective-permute-start | bytes 786440 | tf_op jit(solution)/shard_map/ppermute | solution.py:188
  5.2 6.5 %collective-permute-start.2 = (s32[2,1024]{1,0:T(2,128)}, s32[2,1024]{1,0:T(2,128)S(1)}, u32[]{:S(2)}, u32[]{:S(2)}) collective-permute-start(s32[2,1024]{1,0:T(2,128)} %refs_0_.3), channel_id=1, source_target_pairs={{0,3},{1,2},{2,1},{3,0},{4,7},{5,6},{6,5},{7,4},{8,11},{9,10},{10,... | collective-permute-start | bytes 24584 | tf_op jit(solution)/shard_map/ppermute | solution.py:188
  11.6 1.0 %copy-start.1 = (f32[128,512]{1,0:T(8,128)S(1)}, f32[128,512]{1,0:T(8,128)}, u32[]{:S(2)}) copy-start(f32[128,512]{1,0:T(8,128)} %refs_5_.1) | copy-start | bytes 786436
  12.6 2.1 %copy-start.6 = (s32[2,1]{0,1:T(1,128)S(1)}, s32[2,1]{0,1:T(1,128)}, u32[]{:S(2)}) copy-start(s32[2,1]{0,1:T(1,128)} %param.11) | copy-start | bytes 28
  12.6 2.2 %copy-start.3 = (s32[2,1024]{1,0:T(2,128)S(1)}, s32[2,1024]{1,0:T(2,128)}, u32[]{:S(2)}) copy-start(s32[2,1024]{1,0:T(2,128)} %refs_0_.3) | copy-start | bytes 24580
  12.6 2.2 %copy-start.4 = (s32[2,1024]{1,0:T(2,128)S(1)}, s32[2,1024]{1,0:T(2,128)}, u32[]{:S(2)}) copy-start(s32[2,1024]{1,0:T(2,128)} %item_ref.1) | copy-start | bytes 24580
  12.6 2.2 %copy-start.5 = (f32[2,1024]{1,0:T(2,128)S(1)}, f32[2,1024]{1,0:T(2,128)}, u32[]{:S(2)}) copy-start(f32[2,1024]{1,0:T(2,128)} %rating_ref.1) | copy-start | bytes 24580
  13.2 5.3 %copy-start = (f32[512,512]{1,0:T(8,128)S(1)}, f32[512,512]{1,0:T(8,128)}, u32[]{:S(2)}) copy-start(f32[512,512]{1,0:T(8,128)} %v_ref.1) | copy-start | bytes 3145732
  13.2 5.2 %collective-permute-start.3 = (f32[32,512]{1,0:T(8,128)S(1)}, f32[32,512]{1,0:T(8,128)S(1)}, u32[]{:S(2)}, u32[]{:S(2)}) collective-permute-start(f32[32,512]{1,0:T(8,128)S(1)} %shard_map.77), channel_id=1, source_target_pairs={{0,3},{1,2},{2,1},{3,0},{4,7},{5,6},{6,5},{7,4},{8,11},{9,10},{10,... | collective-permute-start | bytes 196616 | tf_op jit(solution)/shard_map/ppermute | solution.py:188
  15.4 3.1 %copy-start.2 = (f32[128,512]{1,0:T(8,128)S(1)}, f32[128,512]{1,0:T(8,128)}, u32[]{:S(2)}) copy-start(f32[128,512]{1,0:T(8,128)} %refs_5_.1) | copy-start | bytes 786436
  19.5 10.7 %collective-permute-start.4 = (f32[32,512]{1,0:T(8,128)S(1)}, f32[32,512]{1,0:T(8,128)S(1)}, u32[]{:S(2)}, u32[]{:S(2)}) collective-permute-start(f32[32,512]{1,0:T(8,128)S(1)} %get-tuple-element.37), channel_id=1, source_target_pairs={{0,1},{1,0},{2,3},{3,2},{4,5},{5,4},{6,7},{7,6},{8,9},{9,8},{10,11... | collective-permute-start | bytes 196616 | tf_op jit(solution)/shard_map/ppermute | solution.py:188
  21.0 9.3 %collective-permute-start.5 = (f32[32,512]{1,0:T(8,128)S(1)}, f32[32,512]{1,0:T(8,128)S(1)}, u32[]{:S(2)}, u32[]{:S(2)}) collective-permute-start(f32[32,512]{1,0:T(8,128)S(1)} %get-tuple-element.38), channel_id=1, source_target_pairs={{0,2},{1,3},{2,0},{3,1},{4,6},{5,7},{6,4},{7,5},{8,10},{9,11},{10,... | collective-permute-start | bytes 196616 | tf_op jit(solution)/shard_map/ppermute | solution.py:188
  21.6 8.7 %collective-permute-start.6 = (f32[32,512]{1,0:T(8,128)S(1)}, f32[32,512]{1,0:T(8,128)S(1)}, u32[]{:S(2)}, u32[]{:S(2)}) collective-permute-start(f32[32,512]{1,0:T(8,128)S(1)} %get-tuple-element.39), channel_id=1, source_target_pairs={{0,3},{1,2},{2,1},{3,0},{4,7},{5,6},{6,5},{7,4},{8,11},{9,10},{10,... | collective-permute-start | bytes 196616 | tf_op jit(solution)/shard_map/ppermute | solution.py:188
  23.1 3.7 %collective-permute-start.7 = (s32[2,1024]{1,0:T(2,128)S(1)}, s32[2,1024]{1,0:T(2,128)S(1)}, u32[]{:S(2)}, u32[]{:S(2)}) collective-permute-start(s32[2,1024]{1,0:T(2,128)S(1)} %copy-done.3), channel_id=1, source_target_pairs={{0,1},{1,0},{2,3},{3,2},{4,5},{5,4},{6,7},{7,6},{8,9},{9,8},{10,11... | collective-permute-start | bytes 24584 | tf_op jit(solution)/shard_map/ppermute | solution.py:188
  24.5 3.7 %collective-permute-start.8 = (s32[2,1024]{1,0:T(2,128)S(1)}, s32[2,1024]{1,0:T(2,128)S(1)}, u32[]{:S(2)}, u32[]{:S(2)}) collective-permute-start(s32[2,1024]{1,0:T(2,128)S(1)} %copy-done.3), channel_id=1, source_target_pairs={{0,2},{1,3},{2,0},{3,1},{4,6},{5,7},{6,4},{7,5},{8,10},{9,11},{10,... | collective-permute-start | bytes 24584 | tf_op jit(solution)/shard_map/ppermute | solution.py:188
  26.8 10.3 %collective-permute-start.13 = (f32[4,1024]{1,0:T(4,128)S(1)}, f32[4,1024]{1,0:T(4,128)S(1)}, u32[]{:S(2)}, u32[]{:S(2)}) collective-permute-start(f32[4,1024]{1,0:T(4,128)S(1)} %get-tuple-element.46), channel_id=1, source_target_pairs={{0,28},{1,29},{2,30},{3,31},{4,0},{5,1},{6,2},{7,3},{8,4},{9,5},{1... | collective-permute-start | bytes 49160 | tf_op jit(solution)/shard_map/ppermute | solution.py:188
  30.8 9.4 %collective-permute-start.9 = (f32[32,512]{1,0:T(8,128)S(1)}, f32[32,512]{1,0:T(8,128)S(1)}, u32[]{:S(2)}, u32[]{:S(2)}) collective-permute-start(f32[32,512]{1,0:T(8,128)S(1)} %get-tuple-element.42), channel_id=1, source_target_pairs={{0,28},{1,29},{2,30},{3,31},{4,0},{5,1},{6,2},{7,3},{8,4},{9,5},{1... | collective-permute-start | bytes 196616 | tf_op jit(solution)/shard_map/ppermute | solution.py:188
  33.3 6.9 %collective-permute-start.10 = (f32[32,512]{1,0:T(8,128)S(1)}, f32[32,512]{1,0:T(8,128)S(1)}, u32[]{:S(2)}, u32[]{:S(2)}) collective-permute-start(f32[32,512]{1,0:T(8,128)S(1)} %get-tuple-element.43), channel_id=1, source_target_pairs={{0,29},{1,28},{2,31},{3,30},{4,1},{5,0},{6,3},{7,2},{8,5},{9,4},{1... | collective-permute-start | bytes 196616 | tf_op jit(solution)/shard_map/ppermute | solution.py:188
  34.7 5.5 %collective-permute-start.11 = (f32[32,512]{1,0:T(8,128)S(1)}, f32[32,512]{1,0:T(8,128)S(1)}, u32[]{:S(2)}, u32[]{:S(2)}) collective-permute-start(f32[32,512]{1,0:T(8,128)S(1)} %get-tuple-element.44), channel_id=1, source_target_pairs={{0,30},{1,31},{2,28},{3,29},{4,2},{5,3},{6,0},{7,1},{8,6},{9,7},{1... | collective-permute-start | bytes 196616 | tf_op jit(solution)/shard_map/ppermute | solution.py:188
  35.2 5.0 %collective-permute-start.12 = (f32[32,512]{1,0:T(8,128)S(1)}, f32[32,512]{1,0:T(8,128)S(1)}, u32[]{:S(2)}, u32[]{:S(2)}) collective-permute-start(f32[32,512]{1,0:T(8,128)S(1)} %get-tuple-element.45), channel_id=1, source_target_pairs={{0,31},{1,30},{2,29},{3,28},{4,3},{5,2},{6,1},{7,0},{8,7},{9,6},{1... | collective-permute-start | bytes 196616 | tf_op jit(solution)/shard_map/ppermute | solution.py:188
  41.2 5.5 %collective-permute-start.14 = (f32[32,512]{1,0:T(8,128)S(1)}, f32[32,512]{1,0:T(8,128)S(1)}, u32[]{:S(2)}, u32[]{:S(2)}) collective-permute-start(f32[32,512]{1,0:T(8,128)S(1)} %get-tuple-element.53), channel_id=1, source_target_pairs={{0,4},{1,5},{2,6},{3,7},{4,8},{5,9},{6,10},{7,11},{8,12},{9,13},{1... | collective-permute-start | bytes 196616 | tf_op jit(solution)/shard_map/ppermute | solution.py:188
  42.2 6.5 %collective-permute-start.15 = (f32[32,512]{1,0:T(8,128)S(1)}, f32[32,512]{1,0:T(8,128)S(1)}, u32[]{:S(2)}, u32[]{:S(2)}) collective-permute-start(f32[32,512]{1,0:T(8,128)S(1)} %get-tuple-element.54), channel_id=1, source_target_pairs={{0,5},{1,4},{2,7},{3,6},{4,9},{5,8},{6,11},{7,10},{8,13},{9,12},{1... | collective-permute-start | bytes 196616 | tf_op jit(solution)/shard_map/ppermute | solution.py:188
  43.2 6.6 %collective-permute-start.16 = (f32[32,512]{1,0:T(8,128)S(1)}, f32[32,512]{1,0:T(8,128)S(1)}, u32[]{:S(2)}, u32[]{:S(2)}) collective-permute-start(f32[32,512]{1,0:T(8,128)S(1)} %get-tuple-element.55), channel_id=1, source_target_pairs={{0,6},{1,7},{2,4},{3,5},{4,10},{5,11},{6,8},{7,9},{8,14},{9,15},{1... | collective-permute-start | bytes 196616 | tf_op jit(solution)/shard_map/ppermute | solution.py:188
  43.5 7.6 %collective-permute-start.17 = (f32[32,512]{1,0:T(8,128)S(1)}, f32[32,512]{1,0:T(8,128)S(1)}, u32[]{:S(2)}, u32[]{:S(2)}) collective-permute-start(f32[32,512]{1,0:T(8,128)S(1)} %get-tuple-element.56), channel_id=1, source_target_pairs={{0,7},{1,6},{2,5},{3,4},{4,11},{5,10},{6,9},{7,8},{8,15},{9,14},{1... | collective-permute-start | bytes 196616 | tf_op jit(solution)/shard_map/ppermute | solution.py:188

commit v2 on v0

v2 whole, which is shorter than its diff:
```python
import functools

import jax
import jax.numpy as jnp
from jax import lax
from jax.experimental import pallas as pl
from jax.experimental.pallas import tpu as pltpu
from jax.sharding import PartitionSpec as P

TOUCHED = 32
WHOLE = (0, 1, 2)


def first_pieces(n, whole):
    rest = tuple(k for k in range(n) if k not in whole)
    return (whole, rest) if rest else (whole,)


def later_pieces(n):
    order = (0, *range(n - 1, 0, -1))
    return (order[: n // 2], order[n // 2 :])


F32 = jnp.float32
BF16 = jnp.bfloat16
LANES = 128
FIELDS = 3
FIRST_FLOPS = 10**11
SPLIT_FLOPS = 0
PACK_FLOPS = 10**8
PREP_FLOPS = 10**8
TILE_FLOPS = 10**9

NN = (((1,), (0,)), ((), ()))
NT = (((1,), (1,)), ((), ()))
TN = (((0,), (0,)), ((), ()))


def dot(a, b, dims):
    return lax.dot_general(a, b, dims, preferred_element_type=F32)


def split2(x):
    hi = x.astype(BF16)
    return hi, (x - hi.astype(F32)).astype(BF16)


def split3(x):
    hi = x.astype(BF16)
    rest = x - hi.astype(F32)
    mid = rest.astype(BF16)
    return hi, mid, (rest - mid.astype(F32)).astype(BF16)


def pick(selector, x, dims):
    hi, mid, lo = split3(x)
    return (dot(selector, hi, dims) + dot(selector, mid, dims)) + dot(selector, lo, dims)


def iota(shape, dim):
    return lax.broadcasted_iota(jnp.int32, shape, dim)


def one_hot(names, rows):
    return (iota((rows, names.shape[1]), 0) == names).astype(F32).astype(BF16)


def touched_by(names):
    def present(run):
        hot = iota((run, names.shape[1]), 0) == names
        return jnp.max(jnp.where(hot, 1.0, 0.0), axis=1, keepdims=True)

    return present


def ranks(present):
    run = present.shape[0]
    before = (iota((run, run), 0) > iota((run, run), 1)).astype(F32).astype(BF16)
    return jnp.where(present > 0.0, dot(before, present.astype(BF16), NN), -1.0)


def selector(rank):
    return (iota((TOUCHED, rank.shape[1]), 0).astype(F32) == rank).astype(F32).astype(BF16)


def call(kernel, outs, *args, smem=(), hbm=(), scratch=(), flops=0):
    def space(at):
        return pltpu.SMEM if at in smem else pltpu.HBM if at in hbm else pltpu.VMEM

    in_specs = [pl.BlockSpec(memory_space=space(at)) for at in range(len(args))]
    size = sum(a.size * a.dtype.itemsize for a in (*args, *outs)) if flops else 0
    return pl.pallas_call(
        kernel,
        out_shape=list(outs),
        in_specs=[pl.BlockSpec(memory_space=pltpu.VMEM)] * len(args),
        out_specs=[pl.BlockSpec(memory_space=pltpu.VMEM)] * len(outs),
        compiler_params=pltpu.CompilerParams(vmem_limit_bytes=24 * 2**20),
        cost_estimate=pl.CostEstimate(flops=flops, bytes_accessed=size, transcendentals=0),
    )(*args)


def shaped(shape, dtype=F32):
    return jax.ShapeDtypeStruct(shape, dtype)


def split_kernel(own_ref, *out_refs):
    for out_ref, part in zip(out_refs, split3(own_ref[...])):
        out_ref[...] = part


def first_rows_kernel(names_ref, *refs):
    *part_refs, out_ref = refs
    run = part_refs[0].shape[0]
    present = touched_by(names_ref[0:1, :] - lax.axis_index("strata") * run)(run)
    rank = ranks(jnp.broadcast_to(present, (run, LANES)))[:, :TOUCHED]
    sel = (iota(rank.shape, 1).astype(F32) == rank).astype(F32).astype(BF16)
    hi, mid, lo = [dot(sel, ref[...], TN) for ref in part_refs]
    out_ref[...] = (hi + mid) + lo


def run_names(user_ref, t, k, run):
    return user_ref[t : t + 1, :] - (lax.axis_index("strata") ^ k) * run


def pack_entries(n, t, user_ref, item_ref, rating_ref, count_ref, rank, out_ref):
    run = rank.shape[0]
    compact = jnp.zeros((1, user_ref.shape[1]), F32)
    for k in range(n):
        hot = iota((run, user_ref.shape[1]), 0) == run_names(user_ref, t, k, run)
        value = rank[:, t * n + k : t * n + k + 1] + float(k * TOUCHED)
        compact = compact + jnp.sum(jnp.where(hot, value, 0.0), axis=0, keepdims=True)
    active = iota(compact.shape, 1) < count_ref[t : t + 1, 0:1]
    out_ref[0:1, :] = jnp.where(active, compact, -1.0)
    out_ref[1:2, :] = item_ref[t : t + 1, :].astype(F32)
    out_ref[2:3, :] = rating_ref[t : t + 1, :]


def pack_first_kernel(n, user_ref, item_ref, rating_ref, count_ref, rank_ref, codes_ref, out_ref):
    run, width = rank_ref.shape
    lane = iota((run, width), 1)
    present = jnp.zeros((run, width), F32)
    for t in range(user_ref.shape[0]):
        for k in range(n):
            named = touched_by(run_names(user_ref, t, k, run))(run)
            present = jnp.where(lane == t * n + k, named, present)
    rank = ranks(present)
    rank_ref[...] = rank
    codes_ref[...] = rank.T[: codes_ref.shape[0]]
    pack_entries(n, 0, user_ref, item_ref, rating_ref, count_ref, rank, out_ref)


def pack_kernel(n, user_ref, item_ref, rating_ref, count_ref, rank_ref, *out_refs):
    for t, out_ref in enumerate(out_refs, 1):
        pack_entries(n, t, user_ref, item_ref, rating_ref, count_ref, rank_ref[...], out_ref)


def prep_kernel(entry_ref, n_ref, r_ref):
    touched, items = n_ref.shape
    per = max((entry_ref.shape[0] - TOUCHED) // FIELDS, 1)
    lines = [entry_ref[at : at + 1, :] for at in range(entry_ref.shape[0] - FIELDS * per, entry_ref.shape[0])]
    fields = [jnp.concatenate(lines[f * per : (f + 1) * per], axis=1) for f in range(FIELDS)]
    users = fields[0].astype(jnp.int32)
    hot = (iota((touched, users.shape[1]), 0) == users).astype(F32)
    values = split3(fields[2])
    left = [hot.astype(BF16)] + [(hot * v.astype(F32)).astype(BF16) for v in values]
    table = dot(jnp.concatenate(left, axis=0), one_hot(fields[1].astype(jnp.int32), items), NT)
    n_ref[...] = table[:touched]
    r_ref[...] = (table[touched : 2 * touched] + table[2 * touched : 3 * touched]) + table[3 * touched :]


def twice(ah, al, bh, bl, dims):
    both = dot(jnp.concatenate([ah, al], axis=0), bh, dims)
    rows = ah.shape[0]
    return (both[:rows] + both[rows:]) + dot(ah, bl, dims)


def tile_kernel(piece, whole, first, *refs):
    rows, refs = refs[: len(piece)], refs[len(piece) :]
    if first:
        (codes_ref, low_ref), refs = refs[:2], refs[2:]
    parts = 1 if first and 0 in piece else 2
    v_refs, (n_ref, r_ref), refs = refs[:parts], refs[parts : parts + 2], refs[parts + 2 :]
    outs, (uh_ref, ul_ref, wh_ref, wl_ref), v_outs = refs[: len(piece)], refs[len(piece) :][:4], refs[len(piece) + 4 :]
    if v_outs:
        vh, vl = split2(v_refs[0][...])
        v_outs[0][...] = vh
        v_outs[1][...] = vl
    else:
        vh, vl = v_refs[0][...], v_refs[1][...]
    tables = ([], [])
    for at, k in enumerate(piece):
        if first and k == 0:
            hi, lo = rows[at][...], low_ref[...]
        else:
            hi, lo = split2(rows[at][...] if k in whole else rows[at][:TOUCHED, :])
        if k in whole:
            sel = selector(codes_ref[k : k + 1, :])
            hi, lo = dot(sel, hi, NN).astype(BF16), dot(sel, lo, NN).astype(BF16)
        part = slice(at * TOUCHED, (at + 1) * TOUCHED)
        uh_ref[part, :] = hi
        ul_ref[part, :] = lo
        for table, ref in zip(tables, (n_ref, r_ref)):
            table.append(ref[k * TOUCHED : (k + 1) * TOUCHED, :])
    n_table, r_table = [jnp.concatenate(table, axis=0) for table in tables]
    uh, ul = uh_ref[...], ul_ref[...]
    wh, wl = split2(r_table - n_table * twice(uh, ul, vh, vl, NT))
    wh_ref[...] = wh
    wl_ref[...] = wl
    grads = twice(wh, wl, vh, vl, NN)
    for at, k in enumerate(piece):
        outs[at][:TOUCHED, :] = grads[at * TOUCHED : (at + 1) * TOUCHED]
        if first:
            run = codes_ref.shape[1]
            outs[at][TOUCHED:, :] = jnp.zeros((outs[at].shape[0] - TOUCHED, outs[at].shape[1]), F32)
            n = n_ref.shape[0] // TOUCHED
            for t in range(codes_ref.shape[0] // n):
                outs[at][TOUCHED + t : TOUCHED + t + 1, :run] = codes_ref[t * n + k : t * n + k + 1, :]


def items_kernel(step, count, *refs):
    uh, ul, wh, wl = [jnp.concatenate([refs[4 * at + i][...] for at in range(count)], axis=0) for i in range(4)]
    v_ref, out_ref, *part_refs = refs[4 * count :]
    grads = dot(wh, uh, TN) + (dot(wl, uh, TN) + dot(wh, ul, TN))
    v = v_ref[...]
    v = v + step * (grads - 0.1 * v)
    out_ref[...] = v
    if part_refs:
        part_refs[0][...], part_refs[1][...] = split2(v)


def owner_kernel(n, t, step, entry_rows, *refs):
    parts, refs = refs[:n], refs[n:]
    if t == 0:
        ranked = parts
    else:
        ranked, refs = refs[:n], refs[n:]
    if entry_rows:
        entry_ref, refs = refs[0], refs[1:]
    own_ref, out_ref, outs = refs[0], refs[1], refs[2:]
    run = own_ref.shape[0]

    def selectors(sub):
        at = slice(TOUCHED + sub, TOUCHED + sub + 1)
        return jnp.concatenate([selector(ref[at, :run]) for ref in ranked], axis=0)

    grads = pick(selectors(t), jnp.concatenate([part[:TOUCHED, :] for part in parts], axis=0), TN)
    own = own_ref[...]
    own = own + step * (grads - 0.1 * own)
    out_ref[...] = own
    if outs:
        rows = pick(selectors(t + 1), own, NN)
        for k in range(n):
            outs[k][:TOUCHED, :] = rows[k * TOUCHED : (k + 1) * TOUCHED]
        per, width = entry_rows // FIELDS, own_ref.shape[1]
        for f in range(FIELDS):
            for at in range(per):
                low = TOUCHED + f * per + at
                outs[0][low : low + 1, :] = entry_ref[f : f + 1, at * width : (at + 1) * width]


def on_device(user_factors, item_factors, ratings, user_offsets, item_offsets, counts):
    n, row_count = lax.axis_size("strata"), lax.axis_size("rows")
    run, rank = user_factors.shape
    items = item_factors.shape[0]
    subs, entries = ratings.shape
    touched = n * TOUCHED
    entry_rows = FIELDS * (entries // rank)
    ranked_rows = TOUCHED + -(-subs // 8) * 8

    def exchange(value, k, shift=0):
        if k == 0 and shift == 0:
            return value
        pairs = [
            (r * n + s, ((r + shift) % row_count) * n + (s ^ k)) for r in range(row_count) for s in range(n)
        ]
        return lax.ppermute(value, ("rows", "strata"), pairs)

    whole = tuple(k for k in WHOLE if k < n)
    pieces = call(split_kernel, [shaped((run, rank), BF16)] * 3, user_factors, flops=SPLIT_FLOPS)
    rows = [pieces[0]] + [None] * (n - 1)
    for k in range(n):
        if k in whole:
            rows[k] = exchange(user_factors, k)
        elif k:
            mine = call(
                first_rows_kernel, [shaped((TOUCHED, rank))], exchange(user_offsets, k), *pieces,
                flops=FIRST_FLOPS,
            )[0]
            rows[k] = exchange(mine, k)

    listed = (user_offsets, item_offsets, ratings, counts)
    if len(whole) < n:
        listed, mine = lax.optimization_barrier((listed, mine))
    width = -(-subs * n // LANES) * LANES
    ranked, codes, packed = call(
        functools.partial(pack_first_kernel, n),
        [shaped((run, width)), shaped((subs * n, run)), shaped((FIELDS, entries))],
        *listed, flops=PACK_FLOPS,
    )

    own, block = user_factors, item_factors
    block_parts = None
    for t in range(subs):
        step = 0.04 / (1.0 + 0.5 * t)
        first, last = t == 0, t + 1 == subs
        n_table, r_table = call(
            prep_kernel, [shaped((touched, items))] * 2, packed if first else rows[0], flops=PREP_FLOPS,
        )
        height = ranked_rows if first else TOUCHED
        parts, saved = [None] * n, []
        for piece in first_pieces(n, whole) if first else later_pieces(n):
            splits = first and 0 in piece
            size = len(piece) * TOUCHED
            outs = call(
                functools.partial(tile_kernel, piece, whole if first else (), first),
                [shaped((height, rank))] * len(piece) + [shaped((size, rank), BF16)] * 2
                + [shaped((size, items), BF16)] * 2 + [shaped(block.shape, BF16)] * (2 * splits),
                *[rows[k] for k in piece], *([codes, pieces[1]] if first else []),
                *([block] if splits else block_parts), n_table, r_table, flops=TILE_FLOPS,
            )
            for k, grads in zip(piece, outs):
                parts[k] = exchange(grads, k, t)
            saved += outs[len(piece) :][:4]
            if splits:
                block_parts = outs[len(piece) + 4 :]
        block, *block_parts = call(
            functools.partial(items_kernel, step, len(saved) // 4),
            [shaped(block.shape)] + ([] if last else [shaped(block.shape, BF16)] * 2),
            *saved, block, flops=6 * touched * rank * items,
        )
        if not last:
            parts, block, block_parts = lax.optimization_barrier((parts, block, block_parts))
        if first:
            codes_parts = parts
            if not last:
                ranked = lax.optimization_barrier((ranked, saved[0]))[0]
                later = call(
                    functools.partial(pack_kernel, n), [shaped((FIELDS, entries))] * (subs - 1),
                    *listed, ranked, flops=PACK_FLOPS,
                )
        own, *mine = call(
            functools.partial(owner_kernel, n, t, step, 0 if last else entry_rows),
            [shaped(own.shape)] + ([] if last else [shaped((TOUCHED + (k == 0) * entry_rows, rank)) for k in range(n)]),
            *parts, *([] if first else codes_parts), *([] if last else [later[t]]), own, flops=12 * touched * rank * run,
        )
        if not last:
            rows = [None] * n
            for k in (k for piece in later_pieces(n) for k in piece):
                rows[k] = exchange(mine[k], k, -(t + 1))
    return own, block


def solution(mesh):
    return jax.shard_map(
        on_device,
        mesh=mesh,
        in_specs=(
            P(("rows", "strata"), None),
            P(("rows", "strata"), None),
            P(None, ("rows", "strata")),
            P(None, ("rows", "strata")),
            P(None, ("rows", "strata")),
            P(None, ("rows", "strata")),
        ),
        out_specs=(P(("rows", "strata"), None), P(("rows", "strata"), None)),
        check_vma=False,
    )
```

time: 169 us -> 42.8 us (0.25)
  waiting for transfers between devices: 84.1 us -> 8.75 us
  other arithmetic: 46.1 us -> 0 us
  local copies, waits for them, and re-layouts: 23.5 us -> 1.1 us
  starting transfers between devices: 0.45 us -> 21.5 us
  between operations: 13.9 us -> 0.77 us
  Pallas kernels: 0 us -> 10.5 us
    scatter-add x4 -> x0, other arithmetic: 33.8 us -> none  [the longest x2 17.6 us: tile_grads(): jnp.zeros_like(block_u).at[user_index].add(errors[:, None] * v_rows)]
    reduce_scatter x2 -> x0, waiting for transfers between devices: 31.8 us -> none  [on_device(): lax.psum_scatter(grad_u, 'strata', scatter_dimension=0, tiled=True)]
    all_gather x2 -> x0, waiting for transfers between devices: 23.2 us -> none  [gather_users(): return lax.all_gather(owned_rows, 'strata', axis=0, tiled=True)]
    gather x4 -> x0, local copies, waits for them, and re-layouts: 21.9 us -> none  [the longest x2 11.4 us: tile_grads(): v_rows = block_v[item_index]]
    ppermute x2 -> x15, starting transfers between devices: 0.3 us -> 21.5 us  [exchange(): return lax.ppermute(value, ('rows', 'strata'), pairs)]
    ppermute x2 -> x15, waiting for transfers between devices: 28.3 us -> 8.75 us  [exchange(): return lax.ppermute(value, ('rows', 'strata'), pairs)]
    pallas_call x0 -> x14, Pallas kernels: none -> 10.5 us  [call(): pl.pallas_call(kernel, out_shape=list(outs), in_specs=[pl.BlockSpec(memor...]
    add x4 -> x0, other arithmetic: 6.53 us -> none  [the longest x2 3.41 us: on_device(): owned_rows = owned_rows + step_size * (owned_share - 0.1 * owned_rows)]
  transfers between devices with their start and end apart: 6 -> 15, of which waited for: 5 -> 7; matrix products, arithmetic and copies ran while one was open for 19% -> 0% of each run, Pallas kernels for 0% -> 21%
where the time goes in v2:
time: 42.8 us; the launch traced here: 42.6 us
  starting transfers between devices  21.5 us (50%)
  Pallas kernels  10.5 us (25%)
  waiting for transfers between devices  8.75 us (20%)
  local copies, waits for them, and re-layouts  1.1 us (3%)
  between operations  0.77 us (2%)
    ppermute x15, starting transfers between devices, exchange(): return lax.ppermute(value, ('rows', 'strata'), pairs)  21.5 us
    pallas_call x14, Pallas kernels, call(): pl.pallas_call(kernel, out_shape=list(outs), in_specs=[pl.BlockSpec(memor...  10.5 us
    ppermute x15, waiting for transfers between devices, exchange(): return lax.ppermute(value, ('rows', 'strata'), pairs)  8.75 us
    unnamed x14, local copies, waits for them, and re-layouts  1.01 us
  transfers between devices with their start and end apart: 15, of which 7 were waited for; matrix products, arithmetic and copies ran while one was open for 0% of the time, Pallas kernels for 21%

profile of v2, /device:TPU:0, one launch (start us, length us, event | category | flops | bytes accessed | tf_op | source)
XLA Modules:
  0.0 42.6 jit_solution(12406633884964238654)
XLA Ops:
  0.6 4.0 %collective-permute-start.2 = (s32[2,1024]{1,0:T(2,128)}, s32[2,1024]{1,0:T(2,128)S(1)}, u32[]{:S(2)}, u32[]{:S(2)}) collective-permute-start(s32[2,1024]{1,0:T(2,128)} %user_ref.1), channel_id=1, source_target_pairs={{0,3},{1,2},{2,1},{3,0},{4,7},{5,6},{6,5},{7,4},{8,11},{9,10},{10,... | collective-permute-start | bytes 24584 | tf_op jit(solution)/shard_map/ppermute | solution.py:276
  4.6 0.5 %collective-permute-start.1 = (f32[128,512]{1,0:T(8,128)}, f32[128,512]{1,0:T(8,128)S(1)}, u32[]{:S(2)}, u32[]{:S(2)}) collective-permute-start(f32[128,512]{1,0:T(8,128)} %refs_5_.3), channel_id=1, source_target_pairs={{0,2},{1,3},{2,0},{3,1},{4,6},{5,7},{6,4},{7,5},{8,10},{9,11},{10,... | collective-permute-start | bytes 786440 | tf_op jit(solution)/shard_map/ppermute | solution.py:276
  5.2 1.0 %copy-done.1 = f32[128,512]{1,0:T(8,128)S(1)} copy-done((f32[128,512]{1,0:T(8,128)S(1)}, f32[128,512]{1,0:T(8,128)}, u32[]{:S(2)}) %copy-start.1) | copy-done | bytes 262168
  6.5 0.5 %shard_map.78 = f32[32,512]{1,0:T(8,128)S(1)} custom-call(s32[2,1024]{1,0:T(2,128)S(1)} %collective-permute-done.2.names_ref, bf16[128,512]{1,0:T(8,128)(2,1)S(1)} %get-tuple-element.58.refs_0_, bf16[128,512]{1,0:T(8,128)(2,1)S(1)} %get-tuple-element.59.refs_1_.refs_4_.refs_2_, bf16[128,512]{1,0:T(8,128)(2,1)S(1)} %get-tuple-element.60.refs_2_), custom_call_target="tpu_custom_call" | custom-call | flops 99999997952 | bytes 466944 | tf_op jit(solution)/shard_map/pallas_call | solution.py:92
  6.9 3.1 %collective-permute-start.5 = (f32[32,512]{1,0:T(8,128)S(1)}, f32[32,512]{1,0:T(8,128)S(1)}, u32[]{:S(2)}, u32[]{:S(2)}) collective-permute-start(f32[32,512]{1,0:T(8,128)S(1)} %shard_map.78), channel_id=1, source_target_pairs={{0,3},{1,2},{2,1},{3,0},{4,7},{5,6},{6,5},{7,4},{8,11},{9,10},{10,... | collective-permute-start | bytes 196616 | tf_op jit(solution)/shard_map/ppermute | solution.py:276
  10.1 1.2 %shard_map.79 = (f32[128,128]{1,0:T(8,128)S(1)}, f32[8,128]{1,0:T(8,128)S(1)}, f32[3,1024]{1,0:T(4,128)S(1)}) custom-call(s32[2,1024]{1,0:T(2,128)S(1)} %copy-done.3, s32[2,1024]{1,0:T(2,128)S(1)} %copy-done.4, f32[2,1024]{1,0:T(2,128)S(1)} %copy-done.5, s32[2,1]{1,0:T(2,128)S(1)} %copy.8.count_ref), custom_call_target="tpu_custom_call" | custom-call | flops 100000000 | bytes 106504 | tf_op jit(solution)/shard_map/pallas_call | solution.py:92
  11.3 0.7 %shard_map.80 = (f32[128,512]{1,0:T(8,128)S(1)}, f32[128,512]{1,0:T(8,128)S(1)}) custom-call(f32[3,1024]{1,0:T(4,128)S(1)} %get-tuple-element.66.entry_ref), custom_call_target="tpu_custom_call" | custom-call | flops 100000000 | bytes 536576 | tf_op jit(solution)/shard_map/pallas_call | solution.py:92
  12.1 1.0 %collective-permute-done.1.refs_2_ = f32[128,512]{1,0:T(8,128)S(1)} collective-permute-done((f32[128,512]{1,0:T(8,128)}, f32[128,512]{1,0:T(8,128)S(1)}, u32[]{:S(2)}, u32[]{:S(2)}) %collective-permute-start.1) | collective-permute-done | bytes 262176 | tf_op jit(solution)/shard_map/ppermute | solution.py:276
  13.1 0.4 collective-permute-done.refs_1_
  13.5 0.9 %shard_map.81 = (f32[40,512]{1,0:T(8,128)S(1)}, f32[40,512]{1,0:T(8,128)S(1)}, f32[40,512]{1,0:T(8,128)S(1)}, bf16[96,512]{1,0:T(8,128)(2,1)S(1)}, bf16[96,512]{...) custom-call(f32[128,512]{1,0:T(8,128)S(1)} %copy-done.2, ...), custom_call_target="tpu_custom_call" | custom-call | flops 1000000000 | bytes 4182016 | tf_op jit(solution)/shard_map/pallas_call | solution.py:92
  14.4 0.6 %collective-permute-start.3 = (f32[40,512]{1,0:T(8,128)S(1)}, f32[40,512]{1,0:T(8,128)S(1)}, u32[]{:S(2)}, u32[]{:S(2)}) collective-permute-start(f32[40,512]{1,0:T(8,128)S(1)} %get-tuple-element.70), channel_id=1, source_target_pairs={{0,1},{1,0},{2,3},{3,2},{4,5},{5,4},{6,7},{7,6},{8,9},{9,8},{10,11... | collective-permute-start | bytes 245768 | tf_op jit(solution)/shard_map/ppermute | solution.py:276
  15.0 1.6 %collective-permute-start.4 = (f32[40,512]{1,0:T(8,128)S(1)}, f32[40,512]{1,0:T(8,128)S(1)}, u32[]{:S(2)}, u32[]{:S(2)}) collective-permute-start(f32[40,512]{1,0:T(8,128)S(1)} %get-tuple-element.71), channel_id=1, source_target_pairs={{0,2},{1,3},{2,0},{3,1},{4,6},{5,7},{6,4},{7,5},{8,10},{9,11},{10,... | collective-permute-start | bytes 245768 | tf_op jit(solution)/shard_map/ppermute | solution.py:276
  16.6 0.7 %shard_map.82 = (f32[40,512]{1,0:T(8,128)S(1)}, bf16[32,512]{1,0:T(8,128)(2,1)S(1)}, bf16[32,512]{1,0:T(8,128)(2,1)S(1)}, bf16[32,512]{1,0:T(8,128)(2,1)S(1)}, bf16[32,512]{1,0:T(8,128)(2,1)S(1)}) custom-call(f32[32,512]{1,0:T(8,128)S(1)} %collective-permute-done.5.refs_0_, f32[8,128]{1,0:T(8,128)S(1)} %get-tuple-element.65.refs_3_.refs_1_, ...), custom_call_target="tpu_custom_call" | custom-call | flops 1000000000 | bytes 1986560 | tf_op jit(solution)/shard_map/pallas_call | solution.py:92
  17.2 1.4 %collective-permute-start.6 = (f32[40,512]{1,0:T(8,128)S(1)}, f32[40,512]{1,0:T(8,128)S(1)}, u32[]{:S(2)}, u32[]{:S(2)}) collective-permute-start(f32[40,512]{1,0:T(8,128)S(1)} %get-tuple-element.74), channel_id=1, source_target_pairs={{0,3},{1,2},{2,1},{3,0},{4,7},{5,6},{6,5},{7,4},{8,11},{9,10},{10,... | collective-permute-start | bytes 245768 | tf_op jit(solution)/shard_map/ppermute | solution.py:276
  18.7 0.4 shard_map.84.refs_4_
  19.1 0.7 %shard_map.83 = (f32[512,512]{1,0:T(8,128)S(1)}, bf16[512,512]{1,0:T(8,128)(2,1)S(1)}, bf16[512,512]{1,0:T(8,128)(2,1)S(1)}) custom-call(bf16[96,512]{1,0:T(8,128)(2,1)S(1)} %get-tuple-element.75.refs_0_, bf16[96,512]{1,0:T(8,128)(2,1)S(1)} %get-tuple-element.76.refs_1_, bf16[96,512]{1,0:T(8,128)(2,1)S(1)} %get-tuple-element.77.refs_2_, ...), custom_call_target="tpu_custom_call" | custom-call | flops 201326592 | bytes 3670016 | tf_op jit(solution)/shard_map/pallas_call | solution.py:92
  19.9 2.7 %collective-permute-done.6.refs_3_.refs_7_ = f32[40,512]{1,0:T(8,128)S(1)} collective-permute-done((f32[40,512]{1,0:T(8,128)S(1)}, f32[40,512]{1,0:T(8,128)S(1)}, u32[]{:S(2)}, u32[]{:S(2)}) %collective-permute-start.6) | collective-permute-done | bytes 81952 | tf_op jit(solution)/shard_map/ppermute | solution.py:276
  22.6 0.6 %shard_map.85 = (f32[128,512]{1,0:T(8,128)S(1)}, f32[38,512]{1,0:T(8,128)S(1)}, f32[32,512]{1,0:T(8,128)S(1)}, f32[32,512]{1,0:T(8,128)S(1)}, f32[32,512]{1,0:T(8,128)S(1)}) custom-call(f32[40,512]{1,0:T(8,128)S(1)} %get-tuple-element.86.refs_0_.refs_4_, f32[40,512]{1,0:T(8,128)S(1)} %collective-permute-done.3.refs_1_.refs_5_, ...), custom_call_target="tpu_custom_call" | custom-call | flops 100663296 | bytes 1138688 | tf_op jit(solution)/shard_map/pallas_call | solution.py:92
  23.2 4.6 %collective-permute-start.8 = (f32[32,512]{1,0:T(8,128)S(1)}, f32[32,512]{1,0:T(8,128)S(1)}, u32[]{:S(2)}, u32[]{:S(2)}) collective-permute-start(f32[32,512]{1,0:T(8,128)S(1)} %get-tuple-element.93), channel_id=1, source_target_pairs={{0,31},{1,30},{2,29},{3,28},{4,3},{5,2},{6,1},{7,0},{8,7},{9,6},{1... | collective-permute-start | bytes 196616 | tf_op jit(solution)/shard_map/ppermute | solution.py:276
  27.8 1.2 %collective-permute-start.10 = (f32[32,512]{1,0:T(8,128)S(1)}, f32[32,512]{1,0:T(8,128)S(1)}, u32[]{:S(2)}, u32[]{:S(2)}) collective-permute-start(f32[32,512]{1,0:T(8,128)S(1)} %get-tuple-element.99), channel_id=1, source_target_pairs={{0,30},{1,31},{2,28},{3,29},{4,2},{5,3},{6,0},{7,1},{8,6},{9,7},{1... | collective-permute-start | bytes 196616 | tf_op jit(solution)/shard_map/ppermute | solution.py:276
  29.0 0.5 %collective-permute-start.11 = (f32[32,512]{1,0:T(8,128)S(1)}, f32[32,512]{1,0:T(8,128)S(1)}, u32[]{:S(2)}, u32[]{:S(2)}) collective-permute-start(f32[32,512]{1,0:T(8,128)S(1)} %get-tuple-element.100), channel_id=1, source_target_pairs={{0,29},{1,28},{2,31},{3,30},{4,1},{5,0},{6,3},{7,2},{8,5},{9,4},{1... | collective-permute-start | bytes 196616 | tf_op jit(solution)/shard_map/ppermute | solution.py:276
  29.5 0.7 %shard_map.86 = (f32[128,512]{1,0:T(8,128)S(1)}, f32[128,512]{1,0:T(8,128)S(1)}) custom-call(f32[38,512]{1,0:T(8,128)S(1)} %collective-permute-done.7.entry_ref.refs_0_), custom_call_target="tpu_custom_call" | custom-call | flops 100000000 | bytes 602112 | tf_op jit(solution)/shard_map/pallas_call | solution.py:92
  30.2 0.7 %shard_map.87 = (f32[32,512]{1,0:T(8,128)S(1)}, f32[32,512]{1,0:T(8,128)S(1)}, bf16[64,512]{1,0:T(8,128)(2,1)S(1)}, bf16[64,512]{1,0:T(8,128)(2,1)S(1)}, bf16[64...) custom-call(f32[38,512]{1,0:T(8,128)S(1)} %collective-permute-done.7.entry_ref.refs_0_, ...), custom_call_target="tpu_custom_call" | custom-call | flops 1000000000 | bytes 2109440 | tf_op jit(solution)/shard_map/pallas_call | solution.py:92
  31.2 2.5 %collective-permute-start.14 = (f32[32,512]{1,0:T(8,128)S(1)}, f32[32,512]{1,0:T(8,128)S(1)}, u32[]{:S(2)}, u32[]{:S(2)}) collective-permute-start(f32[32,512]{1,0:T(8,128)S(1)} %get-tuple-element.103), channel_id=1, source_target_pairs={{0,7},{1,6},{2,5},{3,4},{4,11},{5,10},{6,9},{7,8},{8,15},{9,14},{1... | collective-permute-start | bytes 196616 | tf_op jit(solution)/shard_map/ppermute | solution.py:276
  33.7 0.7 %shard_map.88 = (f32[32,512]{1,0:T(8,128)S(1)}, f32[32,512]{1,0:T(8,128)S(1)}, bf16[64,512]{1,0:T(8,128)(2,1)S(1)}, bf16[64,512]{1,0:T(8,128)(2,1)S(1)}, bf16[64...) custom-call(f32[32,512]{1,0:T(8,128)S(1)} %collective-permute-done.10.refs_0_, ...), custom_call_target="tpu_custom_call" | custom-call | flops 1000000000 | bytes 2097152 | tf_op jit(solution)/shard_map/pallas_call | solution.py:92
  34.4 0.5 %collective-permute-start.12 = (f32[32,512]{1,0:T(8,128)S(1)}, f32[32,512]{1,0:T(8,128)S(1)}, u32[]{:S(2)}, u32[]{:S(2)}) collective-permute-start(f32[32,512]{1,0:T(8,128)S(1)} %get-tuple-element.101), channel_id=1, source_target_pairs={{0,5},{1,4},{2,7},{3,6},{4,9},{5,8},{6,11},{7,10},{8,13},{9,12},{1... | collective-permute-start | bytes 196616 | tf_op jit(solution)/shard_map/ppermute | solution.py:276
  34.9 0.6 %collective-permute-start.13 = (f32[32,512]{1,0:T(8,128)S(1)}, f32[32,512]{1,0:T(8,128)S(1)}, u32[]{:S(2)}, u32[]{:S(2)}) collective-permute-start(f32[32,512]{1,0:T(8,128)S(1)} %get-tuple-element.102), channel_id=1, source_target_pairs={{0,6},{1,7},{2,4},{3,5},{4,10},{5,11},{6,8},{7,9},{8,14},{9,15},{1... | collective-permute-start | bytes 196616 | tf_op jit(solution)/shard_map/ppermute | solution.py:276
  35.6 1.6 %shard_map.90 = f32[512,512]{1,0:T(8,128)} custom-call(bf16[64,512]{1,0:T(8,128)(2,1)S(1)} %get-tuple-element.105.refs_0_, bf16[64,512]{1,0:T(8,128)(2,1)S(1)} %get-tuple-element.106.refs_1_, bf16[64,512]{1,0:T(8,128)(2,1)S(1)} %get-tuple-element.107.refs_2_, bf16[64,512]{1,0:T(8,128)(2,1)S(1)} %get-tuple-element.108.refs_3_, ...), custom_call_target="tpu_custom_call" | custom-call | flops 201326592 | bytes 2621440 | tf_op jit(solution)/shard_map/pallas_call | solution.py:92
  37.2 1.9 %collective-permute-done.14.refs_3_ = f32[32,512]{1,0:T(8,128)S(1)} collective-permute-done((f32[32,512]{1,0:T(8,128)S(1)}, f32[32,512]{1,0:T(8,128)S(1)}, u32[]{:S(2)}, u32[]{:S(2)}) %collective-permute-start.14) | collective-permute-done | bytes 65568 | tf_op jit(solution)/shard_map/ppermute | solution.py:276
  39.0 1.8 %collective-permute-done.12.refs_1_ = f32[32,512]{1,0:T(8,128)S(1)} collective-permute-done((f32[32,512]{1,0:T(8,128)S(1)}, f32[32,512]{1,0:T(8,128)S(1)}, u32[]{:S(2)}, u32[]{:S(2)}) %collective-permute-start.12) | collective-permute-done | bytes 65568 | tf_op jit(solution)/shard_map/ppermute | solution.py:276
  40.9 0.7 %collective-permute-done.13.refs_2_ = f32[32,512]{1,0:T(8,128)S(1)} collective-permute-done((f32[32,512]{1,0:T(8,128)S(1)}, f32[32,512]{1,0:T(8,128)S(1)}, u32[]{:S(2)}, u32[]{:S(2)}) %collective-permute-start.13) | collective-permute-done | bytes 65568 | tf_op jit(solution)/shard_map/ppermute | solution.py:276
  41.6 1.0 %shard_map.89 = f32[128,512]{1,0:T(8,128)} custom-call(f32[32,512]{1,0:T(8,128)S(1)} %collective-permute-done.9.refs_0_, f32[32,512]{1,0:T(8,128)S(1)} %collective-permute-done.12.refs_1_, f32[32,512]{1,0:T(8,128)S(1)} %collective-permute-done.13.refs_2_, f32[32,512]{1,0:T(8,128)S(1)} %collective-permute-done.14.refs_3_, ...), custom_call_target="tpu_custom_call" | custom-call | flops 100663296 | bytes 1114112 | tf_op jit(solution)/shard_map/pallas_call | solution.py:92
  (27 shorter events, 0.8 us)
Async XLA Ops:
  0.6 5.8 %collective-permute-start.2 = (s32[2,1024]{1,0:T(2,128)}, s32[2,1024]{1,0:T(2,128)S(1)}, u32[]{:S(2)}, u32[]{:S(2)}) collective-permute-start(s32[2,1024]{1,0:T(2,128)} %user_ref.1), channel_id=1, source_target_pairs={{0,3},{1,2},{2,1},{3,0},{4,7},{5,6},{6,5},{7,4},{8,11},{9,10},{10,... | collective-permute-start | bytes 24584 | tf_op jit(solution)/shard_map/ppermute | solution.py:276
  4.6 8.6 %collective-permute-start.1 = (f32[128,512]{1,0:T(8,128)}, f32[128,512]{1,0:T(8,128)S(1)}, u32[]{:S(2)}, u32[]{:S(2)}) collective-permute-start(f32[128,512]{1,0:T(8,128)} %refs_5_.3), channel_id=1, source_target_pairs={{0,2},{1,3},{2,0},{3,1},{4,6},{5,7},{6,4},{7,5},{8,10},{9,11},{10,... | collective-permute-start | bytes 786440 | tf_op jit(solution)/shard_map/ppermute | solution.py:276
  5.1 8.4 %collective-permute-start = (f32[128,512]{1,0:T(8,128)}, f32[128,512]{1,0:T(8,128)S(1)}, u32[]{:S(2)}, u32[]{:S(2)}) collective-permute-start(f32[128,512]{1,0:T(8,128)} %refs_5_.3), channel_id=1, source_target_pairs={{0,1},{1,0},{2,3},{3,2},{4,5},{5,4},{6,7},{7,6},{8,9},{9,8},{10,11... | collective-permute-start | bytes 786440 | tf_op jit(solution)/shard_map/ppermute | solution.py:276
  5.2 1.0 %copy-start.1 = (f32[128,512]{1,0:T(8,128)S(1)}, f32[128,512]{1,0:T(8,128)}, u32[]{:S(2)}) copy-start(f32[128,512]{1,0:T(8,128)} %refs_5_.3) | copy-start | bytes 786436
  6.4 3.6 %copy-start.6 = (s32[2,1]{0,1:T(1,128)S(1)}, s32[2,1]{0,1:T(1,128)}, u32[]{:S(2)}) copy-start(s32[2,1]{0,1:T(1,128)} %param.11) | copy-start | bytes 28
  6.4 3.7 %copy-start.3 = (s32[2,1024]{1,0:T(2,128)S(1)}, s32[2,1024]{1,0:T(2,128)}, u32[]{:S(2)}) copy-start(s32[2,1024]{1,0:T(2,128)} %user_ref.1) | copy-start | bytes 24580
  6.4 3.7 %copy-start.4 = (s32[2,1024]{1,0:T(2,128)S(1)}, s32[2,1024]{1,0:T(2,128)}, u32[]{:S(2)}) copy-start(s32[2,1024]{1,0:T(2,128)} %item_ref.1) | copy-start | bytes 24580
  6.4 3.7 %copy-start.5 = (f32[2,1024]{1,0:T(2,128)S(1)}, f32[2,1024]{1,0:T(2,128)}, u32[]{:S(2)}) copy-start(f32[2,1024]{1,0:T(2,128)} %rating_ref.1) | copy-start | bytes 24580
  6.4 7.1 %copy-start = (f32[512,512]{1,0:T(8,128)S(1)}, f32[512,512]{1,0:T(8,128)}, u32[]{:S(2)}) copy-start(f32[512,512]{1,0:T(8,128)} %refs_8_.1) | copy-start | bytes 3145732
  6.9 9.6 %collective-permute-start.5 = (f32[32,512]{1,0:T(8,128)S(1)}, f32[32,512]{1,0:T(8,128)S(1)}, u32[]{:S(2)}, u32[]{:S(2)}) collective-permute-start(f32[32,512]{1,0:T(8,128)S(1)} %shard_map.78), channel_id=1, source_target_pairs={{0,3},{1,2},{2,1},{3,0},{4,7},{5,6},{6,5},{7,4},{8,11},{9,10},{10,... | collective-permute-start | bytes 196616 | tf_op jit(solution)/shard_map/ppermute | solution.py:276
  11.3 2.2 %copy-start.2 = (f32[128,512]{1,0:T(8,128)S(1)}, f32[128,512]{1,0:T(8,128)}, u32[]{:S(2)}) copy-start(f32[128,512]{1,0:T(8,128)} %refs_5_.3) | copy-start | bytes 786436
  14.4 5.4 %collective-permute-start.3 = (f32[40,512]{1,0:T(8,128)S(1)}, f32[40,512]{1,0:T(8,128)S(1)}, u32[]{:S(2)}, u32[]{:S(2)}) collective-permute-start(f32[40,512]{1,0:T(8,128)S(1)} %get-tuple-element.70), channel_id=1, source_target_pairs={{0,1},{1,0},{2,3},{3,2},{4,5},{5,4},{6,7},{7,6},{8,9},{9,8},{10,11... | collective-permute-start | bytes 245768 | tf_op jit(solution)/shard_map/ppermute | solution.py:276
  15.0 4.8 %collective-permute-start.4 = (f32[40,512]{1,0:T(8,128)S(1)}, f32[40,512]{1,0:T(8,128)S(1)}, u32[]{:S(2)}, u32[]{:S(2)}) collective-permute-start(f32[40,512]{1,0:T(8,128)S(1)} %get-tuple-element.71), channel_id=1, source_target_pairs={{0,2},{1,3},{2,0},{3,1},{4,6},{5,7},{6,4},{7,5},{8,10},{9,11},{10,... | collective-permute-start | bytes 245768 | tf_op jit(solution)/shard_map/ppermute | solution.py:276
  17.2 5.3 %collective-permute-start.6 = (f32[40,512]{1,0:T(8,128)S(1)}, f32[40,512]{1,0:T(8,128)S(1)}, u32[]{:S(2)}, u32[]{:S(2)}) collective-permute-start(f32[40,512]{1,0:T(8,128)S(1)} %get-tuple-element.74), channel_id=1, source_target_pairs={{0,3},{1,2},{2,1},{3,0},{4,7},{5,6},{6,5},{7,4},{8,11},{9,10},{10,... | collective-permute-start | bytes 245768 | tf_op jit(solution)/shard_map/ppermute | solution.py:276
  23.2 6.3 %collective-permute-start.7 = (f32[38,512]{1,0:T(8,128)S(1)}, f32[38,512]{1,0:T(8,128)S(1)}, u32[]{:S(2)}, u32[]{:S(2)}) collective-permute-start(f32[38,512]{1,0:T(8,128)S(1)} %get-tuple-element.92), channel_id=1, source_target_pairs={{0,28},{1,29},{2,30},{3,31},{4,0},{5,1},{6,2},{7,3},{8,4},{9,5},{1... | collective-permute-start | bytes 233480 | tf_op jit(solution)/shard_map/ppermute | solution.py:276
  23.2 7.0 %collective-permute-start.8 = (f32[32,512]{1,0:T(8,128)S(1)}, f32[32,512]{1,0:T(8,128)S(1)}, u32[]{:S(2)}, u32[]{:S(2)}) collective-permute-start(f32[32,512]{1,0:T(8,128)S(1)} %get-tuple-element.93), channel_id=1, source_target_pairs={{0,31},{1,30},{2,29},{3,28},{4,3},{5,2},{6,1},{7,0},{8,7},{9,6},{1... | collective-permute-start | bytes 196616 | tf_op jit(solution)/shard_map/ppermute | solution.py:276
  27.8 5.9 %collective-permute-start.10 = (f32[32,512]{1,0:T(8,128)S(1)}, f32[32,512]{1,0:T(8,128)S(1)}, u32[]{:S(2)}, u32[]{:S(2)}) collective-permute-start(f32[32,512]{1,0:T(8,128)S(1)} %get-tuple-element.99), channel_id=1, source_target_pairs={{0,30},{1,31},{2,28},{3,29},{4,2},{5,3},{6,0},{7,1},{8,6},{9,7},{1... | collective-permute-start | bytes 196616 | tf_op jit(solution)/shard_map/ppermute | solution.py:276
  29.0 4.7 %collective-permute-start.11 = (f32[32,512]{1,0:T(8,128)S(1)}, f32[32,512]{1,0:T(8,128)S(1)}, u32[]{:S(2)}, u32[]{:S(2)}) collective-permute-start(f32[32,512]{1,0:T(8,128)S(1)} %get-tuple-element.100), channel_id=1, source_target_pairs={{0,29},{1,28},{2,31},{3,30},{4,1},{5,0},{6,3},{7,2},{8,5},{9,4},{1... | collective-permute-start | bytes 196616 | tf_op jit(solution)/shard_map/ppermute | solution.py:276
  30.9 6.2 %collective-permute-start.9 = (f32[32,512]{1,0:T(8,128)S(1)}, f32[32,512]{1,0:T(8,128)S(1)}, u32[]{:S(2)}, u32[]{:S(2)}) collective-permute-start(f32[32,512]{1,0:T(8,128)S(1)} %get-tuple-element.98), channel_id=1, source_target_pairs={{0,4},{1,5},{2,6},{3,7},{4,8},{5,9},{6,10},{7,11},{8,12},{9,13},{1... | collective-permute-start | bytes 196616 | tf_op jit(solution)/shard_map/ppermute | solution.py:276
  31.2 7.9 %collective-permute-start.14 = (f32[32,512]{1,0:T(8,128)S(1)}, f32[32,512]{1,0:T(8,128)S(1)}, u32[]{:S(2)}, u32[]{:S(2)}) collective-permute-start(f32[32,512]{1,0:T(8,128)S(1)} %get-tuple-element.103), channel_id=1, source_target_pairs={{0,7},{1,6},{2,5},{3,4},{4,11},{5,10},{6,9},{7,8},{8,15},{9,14},{1... | collective-permute-start | bytes 196616 | tf_op jit(solution)/shard_map/ppermute | solution.py:276
  34.4 6.4 %collective-permute-start.12 = (f32[32,512]{1,0:T(8,128)S(1)}, f32[32,512]{1,0:T(8,128)S(1)}, u32[]{:S(2)}, u32[]{:S(2)}) collective-permute-start(f32[32,512]{1,0:T(8,128)S(1)} %get-tuple-element.101), channel_id=1, source_target_pairs={{0,5},{1,4},{2,7},{3,6},{4,9},{5,8},{6,11},{7,10},{8,13},{9,12},{1... | collective-permute-start | bytes 196616 | tf_op jit(solution)/shard_map/ppermute | solution.py:276
  34.9 6.7 %collective-permute-start.13 = (f32[32,512]{1,0:T(8,128)S(1)}, f32[32,512]{1,0:T(8,128)S(1)}, u32[]{:S(2)}, u32[]{:S(2)}) collective-permute-start(f32[32,512]{1,0:T(8,128)S(1)} %get-tuple-element.102), channel_id=1, source_target_pairs={{0,6},{1,7},{2,4},{3,5},{4,10},{5,11},{6,8},{7,9},{8,14},{9,15},{1... | collective-permute-start | bytes 196616 | tf_op jit(solution)/shard_map/ppermute | solution.py:276

commit v3 on v2

v3 whole, which is shorter than its diff:
```python
import functools

import jax
import jax.numpy as jnp
from jax import lax
from jax.experimental import pallas as pl
from jax.experimental.pallas import tpu as pltpu
from jax.sharding import PartitionSpec as P

TOUCHED = 32
WHOLE = (0, 1, 2)


BLOCK_LATE = 0
STACK_LATE = False
VMEM = 24
PACK_LATE = True
HOME_CHUNKS = 4
FIN_LATE = True
FLOPS = dict(
    split=80000000, first=100000000000, pack=1400000000, prep0=900000000, block=200000000, tile0=1000000000, tile1=800000000, items=900000000, pack1=500000000,
    prep1=900000000, stack=0, next=900000000, owner=6000000000, join=0, preph=900000000, home=2000000000, fin=1200000000,
)

F32 = jnp.float32
BF16 = jnp.bfloat16
LANES = 128
FIELDS = 3

NN = (((1,), (0,)), ((), ()))
NT = (((1,), (1,)), ((), ()))
TN = (((0,), (0,)), ((), ()))


def dot(a, b, dims):
    return lax.dot_general(a, b, dims, preferred_element_type=F32)


def split2(x):
    hi = x.astype(BF16)
    return hi, (x - hi.astype(F32)).astype(BF16)


def split3(x):
    hi = x.astype(BF16)
    rest = x - hi.astype(F32)
    mid = rest.astype(BF16)
    return hi, mid, (rest - mid.astype(F32)).astype(BF16)


def pick(selector, x, dims):
    hi, mid, lo = split3(x)
    return (dot(selector, hi, dims) + dot(selector, mid, dims)) + dot(selector, lo, dims)


def iota(shape, dim):
    return lax.broadcasted_iota(jnp.int32, shape, dim)


def one_hot(names, rows):
    return (iota((rows, names.shape[1]), 0) == names).astype(F32).astype(BF16)


def touched_by(names):
    def present(run):
        hot = iota((run, names.shape[1]), 0) == names
        return jnp.max(jnp.where(hot, 1.0, 0.0), axis=1, keepdims=True)

    return present


def ranks(present):
    run = present.shape[0]
    before = (iota((run, run), 0) > iota((run, run), 1)).astype(F32).astype(BF16)
    return jnp.where(present > 0.0, dot(before, present.astype(BF16), NN), -1.0)


def selector(rank):
    return (iota((TOUCHED, rank.shape[1]), 0).astype(F32) == rank).astype(F32).astype(BF16)


def call(kernel, outs, *args, flops=0, after=(), hbm_out=False, scratch=()):
    size = sum(a.size * a.dtype.itemsize for a in (*args, *outs)) if flops else 0

    def body(*refs):
        kernel(*refs[: len(args)], *refs[len(args) + len(after) :])

    return pl.pallas_call(
        body,
        out_shape=list(outs),
        in_specs=[pl.BlockSpec(memory_space=pltpu.VMEM)] * len(args) + [pl.BlockSpec(memory_space=pl.ANY)] * len(after),
        out_specs=[pl.BlockSpec(memory_space=pl.ANY if hbm_out and at == 0 else pltpu.VMEM) for at in range(len(outs))],
        scratch_shapes=list(scratch),
        compiler_params=pltpu.CompilerParams(vmem_limit_bytes=VMEM * 2**20),
        cost_estimate=pl.CostEstimate(flops=flops, bytes_accessed=size, transcendentals=0),
    )(*args, *after)


def shaped(shape, dtype=F32):
    return jax.ShapeDtypeStruct(shape, dtype)


def split_kernel(own_ref, *out_refs):
    for out_ref, part in zip(out_refs, split3(own_ref[...])):
        out_ref[...] = part


def first_rows_kernel(names_ref, *refs):
    *part_refs, out_ref = refs
    run = part_refs[0].shape[0]
    present = touched_by(names_ref[0:1, :] - lax.axis_index("strata") * run)(run)
    rank = ranks(jnp.broadcast_to(present, (run, LANES)))[:, :TOUCHED]
    sel = (iota(rank.shape, 1).astype(F32) == rank).astype(F32).astype(BF16)
    hi, mid, lo = [dot(sel, ref[...], TN) for ref in part_refs]
    out_ref[...] = (hi + mid) + lo


def run_names(user_ref, t, k, run):
    return user_ref[t : t + 1, :] - (lax.axis_index("strata") ^ k) * run


def pack_entries(n, t, user_ref, item_ref, rating_ref, count_ref, rank, out_ref):
    run = rank.shape[0]
    compact = jnp.zeros((1, user_ref.shape[1]), F32)
    for k in range(n):
        hot = iota((run, user_ref.shape[1]), 0) == run_names(user_ref, t, k, run)
        value = rank[:, t * n + k : t * n + k + 1] + float(k * TOUCHED)
        compact = compact + jnp.sum(jnp.where(hot, value, 0.0), axis=0, keepdims=True)
    active = iota(compact.shape, 1) < count_ref[0:1, t : t + 1]
    out_ref[0:1, :] = jnp.where(active, compact, -1.0)
    out_ref[1:2, :] = item_ref[t : t + 1, :].astype(F32)
    out_ref[2:3, :] = rating_ref[t : t + 1, :]


def pack_first_kernel(n, user_ref, item_ref, rating_ref, count_ref, rank_ref, codes_ref, out_ref):
    run, width = rank_ref.shape
    lane = iota((run, width), 1)
    present = jnp.zeros((run, width), F32)
    for t in range(user_ref.shape[0]):
        for k in range(n):
            named = touched_by(run_names(user_ref, t, k, run))(run)
            present = jnp.where(lane == t * n + k, named, present)
    rank = ranks(present)
    rank_ref[...] = rank
    codes_ref[...] = rank.T[: codes_ref.shape[0]]
    pack_entries(n, 0, user_ref, item_ref, rating_ref, count_ref, rank, out_ref)


def pack_kernel(n, t, user_ref, item_ref, rating_ref, count_ref, rank_ref, out_ref):
    pack_entries(n, t, user_ref, item_ref, rating_ref, count_ref, rank_ref[...], out_ref)


def block_kernel(v_ref, vh_ref, vl_ref):
    vh_ref[...], vl_ref[...] = split2(v_ref[...])


def prep_kernel(entry_ref, n_ref, r_ref):
    touched, items = n_ref.shape
    low = touched if entry_ref.shape[0] > touched else 0
    per = (entry_ref.shape[0] - low) // FIELDS
    fields = [
        jnp.concatenate([entry_ref[at : at + 1, :] for at in range(low + f * per, low + (f + 1) * per)], axis=1)
        for f in range(FIELDS)
    ]
    users = fields[0].astype(jnp.int32)
    hot = (iota((touched, users.shape[1]), 0) == users).astype(F32)
    values = split3(fields[2])
    left = [hot.astype(BF16)] + [(hot * v.astype(F32)).astype(BF16) for v in values]
    table = dot(jnp.concatenate(left, axis=0), one_hot(fields[1].astype(jnp.int32), items), NT)
    n_ref[...] = table[:touched]
    r_ref[...] = (table[touched : 2 * touched] + table[2 * touched : 3 * touched]) + table[3 * touched :]


def twice(ah, al, bh, bl, dims):
    both = dot(jnp.concatenate([ah, al], axis=0), bh, dims)
    rows = ah.shape[0]
    return (both[:rows] + both[rows:]) + dot(ah, bl, dims)


def tile_kernel(piece, whole, first, *refs):
    rows, refs = refs[: len(piece)], refs[len(piece) :]
    if first:
        (codes_ref, low_ref), refs = refs[:2], refs[2:]
    (vh_ref, vl_ref, n_ref, r_ref), refs = refs[:4], refs[4:]
    outs, factors_ref = refs[: len(piece)], refs[len(piece)]
    vh, vl = vh_ref[...], vl_ref[...]
    parts = []
    for at, k in enumerate(piece):
        if first and k == 0:
            hi, lo = rows[at][...], low_ref[...]
        else:
            hi, lo = split2(rows[at][...])
        if k in whole:
            sel = selector(codes_ref[k : k + 1, :])
            hi, lo = dot(sel, hi, NN).astype(BF16), dot(sel, lo, NN).astype(BF16)
        parts.append((hi, lo))
    uh, ul = [jnp.concatenate(x, axis=0) for x in zip(*parts)]
    n_table, r_table = [
        jnp.concatenate([ref[k * TOUCHED : (k + 1) * TOUCHED, :] for k in piece], axis=0) for ref in (n_ref, r_ref)
    ]
    weights = r_table - n_table * twice(uh, ul, vh, vl, NT)
    wh, wl = split2(weights)
    grads = twice(wh, wl, vh, vl, NN)
    for at, k in enumerate(piece):
        outs[at][:TOUCHED, :] = grads[at * TOUCHED : (at + 1) * TOUCHED]
        if first:
            run = codes_ref.shape[1]
            outs[at][TOUCHED:, :] = jnp.zeros((outs[at].shape[0] - TOUCHED, outs[at].shape[1]), F32)
            n = n_ref.shape[0] // TOUCHED
            for t in range(codes_ref.shape[0] // n):
                outs[at][TOUCHED + t : TOUCHED + t + 1, :run] = codes_ref[t * n + k : t * n + k + 1, :]
    if first:
        items = weights.shape[1]
        factors_ref[:, :items] = weights
        factors_ref[:, items:] = uh.astype(F32) + ul.astype(F32)


def item_update(step, weights, rows, v):
    (wh, wl), (uh, ul) = split2(weights), split2(rows)
    grads = dot(wh, uh, TN) + (dot(wl, uh, TN) + dot(wh, ul, TN))
    return v + step * (grads - 0.1 * v)


def items_kernel(step, count, *refs):
    factors = jnp.concatenate([ref[...] for ref in refs[:count]], axis=0)
    v_ref, *out_refs = refs[count:]
    v = v_ref[...]
    items = v.shape[0]
    v = item_update(step, factors[:, :items], factors[:, items:], v)
    if len(out_refs) == 3:
        out_refs[0][...] = v
    out_refs[-2][...], out_refs[-1][...] = split2(v)


def home_kernel(step, rows_ref, n_ref, r_ref, v_ref, vh_ref, vl_ref, out_ref, done_ref, held_ref, sems):
    rows = rows_ref[: n_ref.shape[0], :]
    done_ref[...] = jnp.zeros_like(done_ref)
    uh, ul = split2(rows)
    weights = r_ref[...] - n_ref[...] * twice(uh, ul, vh_ref[...], vl_ref[...], NT)
    chunk = held_ref.shape[0] // HOME_CHUNKS
    copies = []
    for at in range(HOME_CHUNKS):
        part = slice(at * chunk, (at + 1) * chunk)
        held_ref[part, :] = item_update(step, weights[:, part], rows, v_ref[part, :])
        copies.append(pltpu.make_async_copy(held_ref.at[part], out_ref.at[part], sems.at[at]))
        copies[-1].start()
    for copy in copies:
        copy.wait()


def join_kernel(*refs):
    *row_refs, entry_ref, out_ref = refs
    at = 0
    for ref in row_refs:
        out_ref[at : at + TOUCHED, :] = ref[...]
        at += TOUCHED
    width = out_ref.shape[1]
    for f in range(entry_ref.shape[0]):
        for low in range(0, entry_ref.shape[1], width):
            out_ref[at : at + 1, :] = entry_ref[f : f + 1, low : low + width]
            at += 1


def stack_kernel(*refs):
    *in_refs, out_ref = refs
    at = 0
    for ref in in_refs:
        out_ref[at : at + ref.shape[0], :] = ref[...]
        at += ref.shape[0]


def owner_kernel(order, t, step, *refs):
    n = len(order)
    parts, refs = refs[:n], refs[n:]
    if t == 0:
        ranked = parts
    else:
        ranked, refs = refs[:n], refs[n:]
    own_ref, out_ref, outs = refs[0], refs[1], refs[2:]
    run = own_ref.shape[0]

    def selectors(sub):
        at = slice(TOUCHED + sub, TOUCHED + sub + 1)
        return jnp.concatenate([selector(ref[at, :run]) for ref in ranked], axis=0)

    grads = pick(selectors(t), jnp.concatenate([part[:TOUCHED, :] for part in parts], axis=0), TN)
    own = own_ref[...]
    own = own + step * (grads - 0.1 * own)
    out_ref[...] = own
    if outs:
        rows = pick(selectors(t + 1), own, NN)
        for at in range(n):
            outs[at][...] = rows[at * TOUCHED : (at + 1) * TOUCHED]


def on_device(user_factors, item_factors, ratings, user_offsets, item_offsets, counts):
    n, row_count = lax.axis_size("strata"), lax.axis_size("rows")
    run, rank = user_factors.shape
    items = item_factors.shape[0]
    subs, entries = ratings.shape
    touched = n * TOUCHED
    ranked_rows = TOUCHED + -(-subs // 8) * 8
    steps = [0.04 / (1.0 + 0.5 * t) for t in range(subs)]
    if subs != 2:
        raise ValueError("two sub-epochs")
    sent = (0, *range(n - 1, 0, -1))
    later_pieces = (sent[: n - n // 4], sent[n - n // 4 :])

    def exchange(value, k, shift=0):
        if k == 0 and shift == 0:
            return value
        pairs = [
            (r * n + s, ((r + shift) % row_count) * n + (s ^ k)) for r in range(row_count) for s in range(n)
        ]
        return lax.ppermute(value, ("rows", "strata"), pairs)

    def prepare(values, flops, after=()):
        return call(prep_kernel, [shaped((touched, items))] * 2, values, flops=flops, after=after)

    def tile(piece, first, *args, after=()):
        *out, factors = call(
            functools.partial(tile_kernel, piece, whole if first else (), first),
            [shaped((ranked_rows if first else TOUCHED, rank))] * len(piece)
            + [shaped((len(piece) * TOUCHED, items + rank) if first else (8, LANES))],
            *[rows[k] for k in piece], *args, flops=FLOPS["tile%d" % (not first)], after=after,
        )
        grads.update(zip(piece, out))
        return factors

    whole = tuple(k for k in WHOLE if k < n)
    pieces = call(split_kernel, [shaped((run, rank), BF16)] * 3, user_factors, flops=FLOPS["split"])
    rows = [pieces[0]] + [None] * (n - 1)
    picked = []
    for k in range(1, n):
        if k in whole:
            rows[k] = exchange(user_factors, k)
        else:
            picked += call(
                first_rows_kernel, [shaped((TOUCHED, rank))], exchange(user_offsets, k), *pieces,
                flops=FLOPS["first"],
            )
            rows[k] = exchange(picked[-1], k)
    listed = (user_offsets, item_offsets, ratings, counts.reshape(1, subs))
    width = -(-subs * n // LANES) * LANES
    ranked, codes, packed = call(
        functools.partial(pack_first_kernel, n),
        [shaped((run, width)), shaped((subs * n, run)), shaped((FIELDS, entries))],
        *listed, flops=FLOPS["pack"], after=picked,
    )
    tables = prepare(packed, FLOPS["prep0"])
    block_parts = call(
        block_kernel, [shaped(item_factors.shape, BF16)] * 2,
        item_factors, flops=FLOPS["block"], after=[*(picked if BLOCK_LATE != 2 else [rows[1]]), *(tables if BLOCK_LATE == 1 else [])],
    )
    next_block = exchange(item_factors, 0, 1)

    grads, factors = {}, []
    rest = tuple(k for k in range(n) if k not in whole)
    for piece in (whole, rest) if rest else (whole,):
        factors.append(tile(piece, True, codes, pieces[1], *block_parts, *tables, after=factors[-1:]))
    parts = [exchange(grads[k], k) for k in range(n)]
    block, *block_parts = call(
        functools.partial(items_kernel, steps[0], len(factors)),
        [shaped(item_factors.shape)] + [shaped(item_factors.shape, BF16)] * 2,
        *factors, item_factors, flops=FLOPS["items"],
    )
    packed = call(
        functools.partial(pack_kernel, n, 1), [shaped((FIELDS, entries))],
        *listed, ranked, flops=FLOPS["pack1"], after=[block] if PACK_LATE else factors[-1:],
    )[0]
    tables = prepare(packed, FLOPS["prep1"])
    factors = call(
        stack_kernel, [shaped((touched, items + rank))], *factors, flops=FLOPS["stack"],
        after=[block] if STACK_LATE else [],
    )[0]
    next_parts = call(
        functools.partial(items_kernel, steps[0], 1), [shaped(item_factors.shape, BF16)] * 2,
        exchange(factors, 0, 1), next_block, flops=FLOPS["next"],
    )
    ranked = [parts[k] for k in sent]
    own, *mine = call(
        functools.partial(owner_kernel, sent, 0, steps[0]),
        [shaped(user_factors.shape)] + [shaped((TOUCHED, rank))] * n,
        *ranked, user_factors, flops=FLOPS["owner"], after=[block, *tables],
    )

    for k, value in zip(sent, mine):
        rows[k] = exchange(value, k)
    grads = {}
    done = []
    for piece in later_pieces:
        done.append(tile(piece, False, *next_parts, *tables, after=done[-1:]))
    parts = [exchange(grads[k], k) for k in range(n)]
    joined = call(
        join_kernel, [shaped((touched + FIELDS * entries // rank, rank))], *rows, packed, flops=FLOPS["join"],
        after=[grads[later_pieces[0][0]]],
    )[0]
    joined = exchange(joined, 0, -1)
    tables_home = prepare(joined, FLOPS["preph"], [grads[later_pieces[-1][0]]])
    block, after_block = call(
        functools.partial(home_kernel, steps[1]), [shaped(block.shape), shaped((8, LANES))],
        joined, *tables_home, block, *block_parts,
        flops=FLOPS["home"], after=[grads[later_pieces[-1][0]]], hbm_out=True,
        scratch=[pltpu.VMEM(block.shape, F32), pltpu.SemaphoreType.DMA((HOME_CHUNKS,))],
    )
    own = call(
        functools.partial(owner_kernel, sent, 1, steps[1]), [shaped(own.shape)],
        *[parts[k] for k in sent], *[dict(zip(sent, ranked))[k] for k in sent], own, flops=FLOPS["fin"],
        after=[after_block] if FIN_LATE else [],
    )[0]
    return own, block


def solution(mesh):
    return jax.shard_map(
        on_device,
        mesh=mesh,
        in_specs=(
            P(("rows", "strata"), None),
            P(("rows", "strata"), None),
            P(None, ("rows", "strata")),
            P(None, ("rows", "strata")),
            P(None, ("rows", "strata")),
            P(None, ("rows", "strata")),
        ),
        out_specs=(P(("rows", "strata"), None), P(("rows", "strata"), None)),
        check_vma=False,
    )
```

time: 42.8 us -> 40.6 us (0.949)
  starting transfers between devices: 21.5 us -> 18.6 us
  Pallas kernels: 10.5 us -> 12.4 us
  waiting for transfers between devices: 8.75 us -> 6.98 us
  local copies, waits for them, and re-layouts: 1.1 us -> 1.63 us
    ppermute x15 -> x16, starting transfers between devices: 21.5 us -> 18.6 us  [exchange(): return lax.ppermute(value, ('rows', 'strata'), pairs)]
    pallas_call x14 -> x19, Pallas kernels: 10.5 us -> 12.4 us  [call(): pl.pallas_call(body, out_shape=list(outs), in_specs=[pl.BlockSpec(memory_...]
    ppermute x15 -> x16, waiting for transfers between devices: 8.75 us -> 6.98 us  [exchange(): return lax.ppermute(value, ('rows', 'strata'), pairs)]
    unnamed x14, local copies, waits for them, and re-layouts: 1.01 us -> 1.63 us
  transfers between devices with their start and end apart: 15 -> 16, of which waited for: 7 -> 5; matrix products, arithmetic and copies ran while one was open for 0% -> 0% of each run, Pallas kernels for 21% -> 28%
where the time goes in v3:
time: 40.6 us; the launch traced here: 40.5 us
  starting transfers between devices  18.6 us (46%)
  Pallas kernels  12.4 us (31%)
  waiting for transfers between devices  6.98 us (17%)
  local copies, waits for them, and re-layouts  1.63 us (4%)
  between operations  0.88 us (2%)
    ppermute x16, starting transfers between devices, exchange(): return lax.ppermute(value, ('rows', 'strata'), pairs)  18.6 us
    pallas_call x19, Pallas kernels, call(): pl.pallas_call(body, out_shape=list(outs), in_specs=[pl.BlockSpec(memory_...  12.4 us
    ppermute x16, waiting for transfers between devices, exchange(): return lax.ppermute(value, ('rows', 'strata'), pairs)  6.98 us
    unnamed x14, local copies, waits for them, and re-layouts  1.63 us
  transfers between devices with their start and end apart: 16, of which 5 were waited for; matrix products, arithmetic and copies ran while one was open for 0% of the time, Pallas kernels for 28%

profile of v3, /device:TPU:0, one launch (start us, length us, event | category | flops | bytes accessed | tf_op | source)
XLA Modules:
  0.0 40.5 jit_solution(858888559597650925)
XLA Ops:
  0.6 4.0 %collective-permute-start.2 = (s32[2,1024]{1,0:T(2,128)}, s32[2,1024]{1,0:T(2,128)S(1)}, u32[]{:S(2)}, u32[]{:S(2)}) collective-permute-start(s32[2,1024]{1,0:T(2,128)} %refs_0_.7), channel_id=1, source_target_pairs={{0,3},{1,2},{2,1},{3,0},{4,7},{5,6},{6,5},{7,4},{8,11},{9,10},{10,... | collective-permute-start | bytes 24584 | tf_op jit(solution)/shard_map/ppermute | solution.py:315
  4.6 0.5 %collective-permute-start = (f32[128,512]{1,0:T(8,128)}, f32[128,512]{1,0:T(8,128)S(1)}, u32[]{:S(2)}, u32[]{:S(2)}) collective-permute-start(f32[128,512]{1,0:T(8,128)} %refs_4_.1), channel_id=1, source_target_pairs={{0,1},{1,0},{2,3},{3,2},{4,5},{5,4},{6,7},{7,6},{8,9},{9,8},{10,11... | collective-permute-start | bytes 786440 | tf_op jit(solution)/shard_map/ppermute | solution.py:315
  5.2 1.0 %copy-done.1 = f32[128,512]{1,0:T(8,128)S(1)} copy-done((f32[128,512]{1,0:T(8,128)S(1)}, f32[128,512]{1,0:T(8,128)}, u32[]{:S(2)}) %copy-start.1) | copy-done | bytes 262168
  6.4 0.5 %shard_map.78.refs_4_.refs_1_ = f32[32,512]{1,0:T(8,128)S(1)} custom-call(s32[2,1024]{1,0:T(2,128)S(1)} %collective-permute-done.2.refs_0_, bf16[128,512]{1,0:T(8,128)(2,1)S(1)} %get-tuple-element.39.refs_1_.refs_0_, bf16[128,512]{1,0:T(8,128)(2,1)S(1)} %get-tuple-element.40.refs_2_.refs_4_, bf16[128,512]{1,0:T(8,128)(2,1)S(1)} %get-tuple-element.41.refs_3_), custom_call_target="tpu_custom_call" | custom-call | flops 99999997952 | bytes 466944 | tf_op jit(solution)/shard_map/pallas_call | solution.py:88
  6.9 3.1 %collective-permute-start.3 = (f32[32,512]{1,0:T(8,128)S(1)}, f32[32,512]{1,0:T(8,128)S(1)}, u32[]{:S(2)}, u32[]{:S(2)}) collective-permute-start(f32[32,512]{1,0:T(8,128)S(1)} %shard_map.78.refs_4_.refs_1_), channel_id=1, source_target_pairs={{0,3},{1,2},{2,1},{3,0},{4,7},{5,6},{6,5},{7,4},{8,11},{9,10},{10,... | collective-permute-start | bytes 196616 | tf_op jit(solution)/shard_map/ppermute | solution.py:315
  10.2 0.6 %copy-done.6 = s32[2,1]{0,1:T(1,128)S(1)} copy-done((s32[2,1]{0,1:T(1,128)S(1)}, s32[2,1]{0,1:T(1,128)}, u32[]{:S(2)}) %copy-start.6) | copy-done | bytes 32
  10.8 1.2 %shard_map.79 = (f32[128,128]{1,0:T(8,128)S(1)}, f32[8,128]{1,0:T(8,128)S(1)}, f32[3,1024]{1,0:T(4,128)S(1)}) custom-call(s32[2,1024]{1,0:T(2,128)S(1)} %copy-done.3, s32[2,1024]{1,0:T(2,128)S(1)} %copy-done.4, f32[2,1024]{1,0:T(2,128)S(1)} %copy-done.5, s32[1,2]{1,0:T(1,128)S(1)} %bitcast.1, f32[32,512]{1,0:T(8,128)S(1)} %shard_map.78.refs_4_.refs_1_), custom_call_target="tpu_custom_call" | custom-call | flops 1400000000 | bytes 106504 | tf_op jit(solution)/shard_map/pallas_call | solution.py:88
  12.0 0.8 %shard_map.81 = (f32[128,512]{1,0:T(8,128)S(1)}, f32[128,512]{1,0:T(8,128)S(1)}) custom-call(f32[3,1024]{1,0:T(4,128)S(1)} %get-tuple-element.45.refs_0_), custom_call_target="tpu_custom_call" | custom-call | flops 900000000 | bytes 536576 | tf_op jit(solution)/shard_map/pallas_call | solution.py:88
  12.8 1.4 %collective-permute-done.1.refs_2_ = f32[128,512]{1,0:T(8,128)S(1)} collective-permute-done((f32[128,512]{1,0:T(8,128)}, f32[128,512]{1,0:T(8,128)S(1)}, u32[]{:S(2)}, u32[]{:S(2)}) %collective-permute-start.1) | collective-permute-done | bytes 262176 | tf_op jit(solution)/shard_map/ppermute | solution.py:315
  14.2 0.9 %shard_map.82 = (f32[40,512]{1,0:T(8,128)S(1)}, f32[40,512]{1,0:T(8,128)S(1)}, f32[40,512]{1,0:T(8,128)S(1)}, f32[96,1024]{1,0:T(8,128)S(1)}) custom-call(bf16[128,512]{1,0:T(8,128)(2,1)S(1)} %get-tuple-element.39.refs_1_.refs_0_, f32[128,512]{1,0:T(8,128)S(1)} %collective-permute-done.refs_1_, f32[128,512]{1,0:T(8,128)S(1)} %collective-permute-done.1.refs_2_, ...), custom_call_target="tpu_custom_call" | custom-call | flops 1000000000 | bytes 3002368 | tf_op jit(solution)/shard_map/pallas_call | solution.py:88
  15.2 1.6 %collective-permute-start.6 = (f32[40,512]{1,0:T(8,128)S(1)}, f32[40,512]{1,0:T(8,128)S(1)}, u32[]{:S(2)}, u32[]{:S(2)}) collective-permute-start(f32[40,512]{1,0:T(8,128)S(1)} %get-tuple-element.52), channel_id=1, source_target_pairs={{0,1},{1,0},{2,3},{3,2},{4,5},{5,4},{6,7},{7,6},{8,9},{9,8},{10,11... | collective-permute-start | bytes 245768 | tf_op jit(solution)/shard_map/ppermute | solution.py:315
  16.7 0.7 %shard_map.83 = (f32[40,512]{1,0:T(8,128)S(1)}, f32[32,1024]{1,0:T(8,128)S(1)}) custom-call(f32[32,512]{1,0:T(8,128)S(1)} %collective-permute-done.3.refs_0_, f32[8,128]{1,0:T(8,128)S(1)} %get-tuple-element.42.refs_3_.refs_1_, bf16[128,512]{1,0:T(8,128)(2,1)S(1)} %get-tuple-element.40.refs_2_.refs_4_, ...), custom_call_target="tpu_custom_call" | custom-call | flops 1000000000 | bytes 1986560 | tf_op jit(solution)/shard_map/pallas_call | solution.py:88
  17.4 1.9 %collective-permute-start.4 = (f32[40,512]{1,0:T(8,128)S(1)}, f32[40,512]{1,0:T(8,128)S(1)}, u32[]{:S(2)}, u32[]{:S(2)}) collective-permute-start(f32[40,512]{1,0:T(8,128)S(1)} %get-tuple-element.50), channel_id=1, source_target_pairs={{0,3},{1,2},{2,1},{3,0},{4,7},{5,6},{6,5},{7,4},{8,11},{9,10},{10,... | collective-permute-start | bytes 245768 | tf_op jit(solution)/shard_map/ppermute | solution.py:315
  19.4 0.7 %shard_map.84 = (f32[512,512]{1,0:T(8,128)S(1)}, bf16[512,512]{1,0:T(8,128)(2,1)S(1)}, bf16[512,512]{1,0:T(8,128)(2,1)S(1)}) custom-call(f32[96,1024]{1,0:T(8,128)S(1)} %get-tuple-element.49.refs_7_.refs_0_, f32[32,1024]{1,0:T(8,128)S(1)} %get-tuple-element.53.refs_1_, f32[512,512]{1,0:T(8,128)S(1)} %copy-done), custom_call_target="tpu_custom_call" | custom-call | flops 900000000 | bytes 3670016 | tf_op jit(solution)/shard_map/pallas_call | solution.py:88
  20.2 0.4 %shard_map.85.refs_0_.refs_4_ = f32[3,1024]{1,0:T(4,128)S(1)} custom-call(s32[2,1024]{1,0:T(2,128)S(1)} %copy-done.3, s32[2,1024]{1,0:T(2,128)S(1)} %copy-done.4, f32[2,1024]{1,0:T(2,128)S(1)} %copy-done.5, s32[1,2]{1,0:T(1,128)S(1)} %bitcast.2, f32[128,128]{1,0:T(8,128)S(1)} %get-tuple-element.55.refs_4_, f32[512,512]{1,0:T(8,128)S(1)} %get-tuple-element.54.refs_5_.refs_3_), custom_call_target="tpu_custom_call" | custom-call | flops 500000000 | bytes 102408 | tf_op jit(solution)/shard_map/pallas_call | solution.py:88
  20.6 0.8 %shard_map.86 = (f32[128,512]{1,0:T(8,128)S(1)}, f32[128,512]{1,0:T(8,128)S(1)}) custom-call(f32[3,1024]{1,0:T(4,128)S(1)} %shard_map.85.refs_0_.refs_4_), custom_call_target="tpu_custom_call" | custom-call | flops 900000000 | bytes 536576 | tf_op jit(solution)/shard_map/pallas_call | solution.py:88
  21.4 1.4 %collective-permute-done.4.refs_1_.refs_5_ = f32[40,512]{1,0:T(8,128)S(1)} collective-permute-done((f32[40,512]{1,0:T(8,128)S(1)}, f32[40,512]{1,0:T(8,128)S(1)}, u32[]{:S(2)}, u32[]{:S(2)}) %collective-permute-start.4) | collective-permute-done | bytes 81952 | tf_op jit(solution)/shard_map/ppermute | solution.py:315
  22.8 0.6 %shard_map.87 = (f32[128,512]{1,0:T(8,128)S(1)}, f32[32,512]{1,0:T(8,128)S(1)}, f32[32,512]{1,0:T(8,128)S(1)}, f32[32,512]{1,0:T(8,128)S(1)}, f32[32,512]{1,0:T(8,128)S(1)}) custom-call(f32[40,512]{1,0:T(8,128)S(1)} %get-tuple-element.48.refs_0_.refs_4_, f32[40,512]{1,0:T(8,128)S(1)} %collective-permute-done.4.refs_1_.refs_5_, ...), custom_call_target="tpu_custom_call" | custom-call | flops 6000000000 | bytes 1114112 | tf_op jit(solution)/shard_map/pallas_call | solution.py:88
  23.3 2.0 %collective-permute-start.7 = (f32[32,512]{1,0:T(8,128)S(1)}, f32[32,512]{1,0:T(8,128)S(1)}, u32[]{:S(2)}, u32[]{:S(2)}) collective-permute-start(f32[32,512]{1,0:T(8,128)S(1)} %get-tuple-element.59), channel_id=1, source_target_pairs={{0,3},{1,2},{2,1},{3,0},{4,7},{5,6},{6,5},{7,4},{8,11},{9,10},{10,... | collective-permute-start | bytes 196616 | tf_op jit(solution)/shard_map/ppermute | solution.py:315
  25.3 0.4 %collective-permute-start.8 = (f32[32,512]{1,0:T(8,128)S(1)}, f32[32,512]{1,0:T(8,128)S(1)}, u32[]{:S(2)}, u32[]{:S(2)}) collective-permute-start(f32[32,512]{1,0:T(8,128)S(1)} %get-tuple-element.60), channel_id=1, source_target_pairs={{0,2},{1,3},{2,0},{3,1},{4,6},{5,7},{6,4},{7,5},{8,10},{9,11},{10,... | collective-permute-start | bytes 196616 | tf_op jit(solution)/shard_map/ppermute | solution.py:315
  25.7 1.2 %collective-permute-start.13 = (f32[32,512]{1,0:T(8,128)S(1)}, f32[32,512]{1,0:T(8,128)S(1)}, u32[]{:S(2)}, u32[]{:S(2)}) collective-permute-start(f32[32,512]{1,0:T(8,128)S(1)} %get-tuple-element.66), channel_id=1, source_target_pairs={{0,1},{1,0},{2,3},{3,2},{4,5},{5,4},{6,7},{7,6},{8,9},{9,8},{10,11... | collective-permute-start | bytes 196616 | tf_op jit(solution)/shard_map/ppermute | solution.py:315
  26.9 2.9 %collective-permute-done.9.refs_0_ = f32[128,1024]{1,0:T(8,128)S(1)} collective-permute-done((f32[128,1024]{1,0:T(8,128)S(1)}, f32[128,1024]{1,0:T(8,128)S(1)}, u32[]{:S(2)}, u32[]{:S(2)}) %collective-permute-start.9) | collective-permute-done | bytes 524320 | tf_op jit(solution)/shard_map/ppermute | solution.py:315
  29.8 0.7 %shard_map.89 = (bf16[512,512]{1,0:T(8,128)(2,1)S(1)}, bf16[512,512]{1,0:T(8,128)(2,1)S(1)}) custom-call(f32[128,1024]{1,0:T(8,128)S(1)} %collective-permute-done.9.refs_0_, f32[512,512]{1,0:T(8,128)S(1)} %collective-permute-done.10.refs_1_), custom_call_target="tpu_custom_call" | custom-call | flops 900000000 | bytes 2621440 | tf_op jit(solution)/shard_map/pallas_call | solution.py:88
  30.6 0.8 %shard_map.90 = (f32[32,512]{1,0:T(8,128)S(1)}, f32[32,512]{1,0:T(8,128)S(1)}, f32[32,512]{1,0:T(8,128)S(1)}, f32[8,128]{1,0:T(8,128)S(1)}) custom-call(f32[32,512]{1,0:T(8,128)S(1)} %get-tuple-element.58.refs_0_, f32[32,512]{1,0:T(8,128)S(1)} %collective-permute-done.7.refs_1_.refs_3_, f32[32,512]{1,0:T(8,128)S(1)} %collective-permute-done.8.refs_2_, ...), custom_call_target="tpu_custom_call" | custom-call | flops 800000000 | bytes 1970176 | tf_op jit(solution)/shard_map/pallas_call | solution.py:88
  31.6 1.1 %collective-permute-start.11 = (f32[32,512]{1,0:T(8,128)S(1)}, f32[32,512]{1,0:T(8,128)S(1)}, u32[]{:S(2)}, u32[]{:S(2)}) collective-permute-start(f32[32,512]{1,0:T(8,128)S(1)} %get-tuple-element.64), channel_id=1, source_target_pairs={{0,3},{1,2},{2,1},{3,0},{4,7},{5,6},{6,5},{7,4},{8,11},{9,10},{10,... | collective-permute-start | bytes 196616 | tf_op jit(solution)/shard_map/ppermute | solution.py:315
  32.7 1.8 %collective-permute-start.12 = (f32[32,512]{1,0:T(8,128)S(1)}, f32[32,512]{1,0:T(8,128)S(1)}, u32[]{:S(2)}, u32[]{:S(2)}) collective-permute-start(f32[32,512]{1,0:T(8,128)S(1)} %get-tuple-element.65), channel_id=1, source_target_pairs={{0,2},{1,3},{2,0},{3,1},{4,6},{5,7},{6,4},{7,5},{8,10},{9,11},{10,... | collective-permute-start | bytes 196616 | tf_op jit(solution)/shard_map/ppermute | solution.py:315
  34.5 0.7 %shard_map.91 = (f32[32,512]{1,0:T(8,128)S(1)}, f32[8,128]{1,0:T(8,128)}) custom-call(f32[32,512]{1,0:T(8,128)S(1)} %collective-permute-done.13.refs_0_.refs_1_, bf16[512,512]{1,0:T(8,128)(2,1)S(1)} %get-tuple-element.61.refs_3_.refs_1_, bf16[512,512]{1,0:T(8,128)(2,1)S(1)} %get-tuple-element.62.refs_4_.refs_2_, ...), custom_call_target="tpu_custom_call" | custom-call | flops 800000000 | bytes 1708032 | tf_op jit(solution)/shard_map/pallas_call | solution.py:88
  35.2 0.7 %collective-permute-start.14 = (f32[32,512]{1,0:T(8,128)S(1)}, f32[32,512]{1,0:T(8,128)S(1)}, u32[]{:S(2)}, u32[]{:S(2)}) collective-permute-start(f32[32,512]{1,0:T(8,128)S(1)} %get-tuple-element.68.refs_1_.refs_6_), channel_id=1, source_target_pairs={{0,1},{1,0},{2,3},{3,2},{4,5},{5,4},{6,7},{7,6},{8,9},{9,8},{10,11... | collective-permute-start | bytes 196616 | tf_op jit(solution)/shard_map/ppermute | solution.py:315
  35.8 0.7 %shard_map.93 = (f32[128,512]{1,0:T(8,128)S(1)}, f32[128,512]{1,0:T(8,128)S(1)}) custom-call(f32[134,512]{1,0:T(8,128)S(1)} %collective-permute-done.15.refs_0_, f32[32,512]{1,0:T(8,128)S(1)} %get-tuple-element.68.refs_1_.refs_6_), custom_call_target="tpu_custom_call" | custom-call | flops 900000000 | bytes 798720 | tf_op jit(solution)/shard_map/pallas_call | solution.py:88
  36.6 1.8 %shard_map.94 = (f32[512,512]{1,0:T(8,128)}, f32[8,128]{1,0:T(8,128)S(1)}) custom-call(f32[134,512]{1,0:T(8,128)S(1)} %collective-permute-done.15.refs_0_, f32[128,512]{1,0:T(8,128)S(1)} %get-tuple-element.70.refs_1_, f32[128,512]{1,0:T(8,128)S(1)} %get-tuple-element.71.refs_2_, f32[512,512]{1,0:T(8,128)S(1)} %get-tuple-element.54.refs_5_.refs_3_, ...), custom_call_target="tpu_custom_call" | custom-call | flops 2000000000 | bytes 3948544 | tf_op jit(solution)/shard_map/pallas_call | solution.py:88
  38.4 1.1 %collective-permute-done.14.refs_3_ = f32[32,512]{1,0:T(8,128)S(1)} collective-permute-done((f32[32,512]{1,0:T(8,128)S(1)}, f32[32,512]{1,0:T(8,128)S(1)}, u32[]{:S(2)}, u32[]{:S(2)}) %collective-permute-start.14) | collective-permute-done | bytes 65568 | tf_op jit(solution)/shard_map/ppermute | solution.py:315
  39.5 1.0 %shard_map.95 = f32[128,512]{1,0:T(8,128)} custom-call(f32[32,512]{1,0:T(8,128)S(1)} %get-tuple-element.63.refs_5_.refs_0_, f32[32,512]{1,0:T(8,128)S(1)} %collective-permute-done.11.refs_1_, f32[32,512]{1,0:T(8,128)S(1)} %collective-permute-done.12.refs_2_, f32[32,512]{1,0:T(8,128)S(1)} %collective-permute-done.14.refs_3_, ...), custom_call_target="tpu_custom_call" | custom-call | flops 1200000000 | bytes 1114112 | tf_op jit(solution)/shard_map/pallas_call | solution.py:88
  (33 shorter events, 0.9 us)
Async XLA Ops:
  0.6 5.8 %collective-permute-start.2 = (s32[2,1024]{1,0:T(2,128)}, s32[2,1024]{1,0:T(2,128)S(1)}, u32[]{:S(2)}, u32[]{:S(2)}) collective-permute-start(s32[2,1024]{1,0:T(2,128)} %refs_0_.7), channel_id=1, source_target_pairs={{0,3},{1,2},{2,1},{3,0},{4,7},{5,6},{6,5},{7,4},{8,11},{9,10},{10,... | collective-permute-start | bytes 24584 | tf_op jit(solution)/shard_map/ppermute | solution.py:315
  4.6 8.2 %collective-permute-start = (f32[128,512]{1,0:T(8,128)}, f32[128,512]{1,0:T(8,128)S(1)}, u32[]{:S(2)}, u32[]{:S(2)}) collective-permute-start(f32[128,512]{1,0:T(8,128)} %refs_4_.1), channel_id=1, source_target_pairs={{0,1},{1,0},{2,3},{3,2},{4,5},{5,4},{6,7},{7,6},{8,9},{9,8},{10,11... | collective-permute-start | bytes 786440 | tf_op jit(solution)/shard_map/ppermute | solution.py:315
  5.1 9.1 %collective-permute-start.1 = (f32[128,512]{1,0:T(8,128)}, f32[128,512]{1,0:T(8,128)S(1)}, u32[]{:S(2)}, u32[]{:S(2)}) collective-permute-start(f32[128,512]{1,0:T(8,128)} %refs_4_.1), channel_id=1, source_target_pairs={{0,2},{1,3},{2,0},{3,1},{4,6},{5,7},{6,4},{7,5},{8,10},{9,11},{10,... | collective-permute-start | bytes 786440 | tf_op jit(solution)/shard_map/ppermute | solution.py:315
  5.2 24.6 %collective-permute-start.10 = (f32[512,512]{1,0:T(8,128)}, f32[512,512]{1,0:T(8,128)S(1)}, u32[]{:S(2)}, u32[]{:S(2)}) collective-permute-start(f32[512,512]{1,0:T(8,128)} %refs_2_.4), channel_id=1, source_target_pairs={{0,4},{1,5},{2,6},{3,7},{4,8},{5,9},{6,10},{7,11},{8,12},{9,13},{1... | collective-permute-start | bytes 3145736 | tf_op jit(solution)/shard_map/ppermute | solution.py:315
  5.2 1.0 %copy-start.1 = (f32[128,512]{1,0:T(8,128)S(1)}, f32[128,512]{1,0:T(8,128)}, u32[]{:S(2)}) copy-start(f32[128,512]{1,0:T(8,128)} %refs_4_.1) | copy-start | bytes 786436
  6.4 3.6 %copy-start = (f32[512,512]{1,0:T(8,128)S(1)}, f32[512,512]{1,0:T(8,128)}, u32[]{:S(2)}) copy-start(f32[512,512]{1,0:T(8,128)} %refs_2_.4) | copy-start | bytes 3145732
  6.9 3.3 %copy-start.3 = (s32[2,1024]{1,0:T(2,128)S(1)}, s32[2,1024]{1,0:T(2,128)}, u32[]{:S(2)}) copy-start(s32[2,1024]{1,0:T(2,128)} %refs_0_.7) | copy-start | bytes 24580
  6.9 3.3 %copy-start.4 = (s32[2,1024]{1,0:T(2,128)S(1)}, s32[2,1024]{1,0:T(2,128)}, u32[]{:S(2)}) copy-start(s32[2,1024]{1,0:T(2,128)} %refs_1_.3) | copy-start | bytes 24580
  6.9 3.3 %copy-start.5 = (f32[2,1024]{1,0:T(2,128)S(1)}, f32[2,1024]{1,0:T(2,128)}, u32[]{:S(2)}) copy-start(f32[2,1024]{1,0:T(2,128)} %refs_2_.5) | copy-start | bytes 24580
  6.9 9.8 %collective-permute-start.3 = (f32[32,512]{1,0:T(8,128)S(1)}, f32[32,512]{1,0:T(8,128)S(1)}, u32[]{:S(2)}, u32[]{:S(2)}) collective-permute-start(f32[32,512]{1,0:T(8,128)S(1)} %shard_map.78.refs_4_.refs_1_), channel_id=1, source_target_pairs={{0,3},{1,2},{2,1},{3,0},{4,7},{5,6},{6,5},{7,4},{8,11},{9,10},{10,... | collective-permute-start | bytes 196616 | tf_op jit(solution)/shard_map/ppermute | solution.py:315
  10.2 0.7 %copy-start.6 = (s32[2,1]{0,1:T(1,128)S(1)}, s32[2,1]{0,1:T(1,128)}, u32[]{:S(2)}) copy-start(s32[2,1]{0,1:T(1,128)} %param.11) | copy-start | bytes 28
  15.1 6.3 %collective-permute-start.5 = (f32[40,512]{1,0:T(8,128)S(1)}, f32[40,512]{1,0:T(8,128)S(1)}, u32[]{:S(2)}, u32[]{:S(2)}) collective-permute-start(f32[40,512]{1,0:T(8,128)S(1)} %get-tuple-element.51), channel_id=1, source_target_pairs={{0,2},{1,3},{2,0},{3,1},{4,6},{5,7},{6,4},{7,5},{8,10},{9,11},{10,... | collective-permute-start | bytes 245768 | tf_op jit(solution)/shard_map/ppermute | solution.py:315
  15.2 6.2 %collective-permute-start.6 = (f32[40,512]{1,0:T(8,128)S(1)}, f32[40,512]{1,0:T(8,128)S(1)}, u32[]{:S(2)}, u32[]{:S(2)}) collective-permute-start(f32[40,512]{1,0:T(8,128)S(1)} %get-tuple-element.52), channel_id=1, source_target_pairs={{0,1},{1,0},{2,3},{3,2},{4,5},{5,4},{6,7},{7,6},{8,9},{9,8},{10,11... | collective-permute-start | bytes 245768 | tf_op jit(solution)/shard_map/ppermute | solution.py:315
  17.4 5.3 %collective-permute-start.4 = (f32[40,512]{1,0:T(8,128)S(1)}, f32[40,512]{1,0:T(8,128)S(1)}, u32[]{:S(2)}, u32[]{:S(2)}) collective-permute-start(f32[40,512]{1,0:T(8,128)S(1)} %get-tuple-element.50), channel_id=1, source_target_pairs={{0,3},{1,2},{2,1},{3,0},{4,7},{5,6},{6,5},{7,4},{8,11},{9,10},{10,... | collective-permute-start | bytes 245768 | tf_op jit(solution)/shard_map/ppermute | solution.py:315
  19.4 10.5 %collective-permute-start.9 = (f32[128,1024]{1,0:T(8,128)S(1)}, f32[128,1024]{1,0:T(8,128)S(1)}, u32[]{:S(2)}, u32[]{:S(2)}) collective-permute-start(f32[128,1024]{1,0:T(8,128)S(1)} %shard_map.88), channel_id=1, source_target_pairs={{0,4},{1,5},{2,6},{3,7},{4,8},{5,9},{6,10},{7,11},{8,12},{9,13},{1... | collective-permute-start | bytes 1572872 | tf_op jit(solution)/shard_map/ppermute | solution.py:315
  20.6 2.1 %copy-start.2 = (f32[128,512]{1,0:T(8,128)S(1)}, f32[128,512]{1,0:T(8,128)}, u32[]{:S(2)}) copy-start(f32[128,512]{1,0:T(8,128)} %refs_4_.1) | copy-start | bytes 786436
  23.3 7.3 %collective-permute-start.7 = (f32[32,512]{1,0:T(8,128)S(1)}, f32[32,512]{1,0:T(8,128)S(1)}, u32[]{:S(2)}, u32[]{:S(2)}) collective-permute-start(f32[32,512]{1,0:T(8,128)S(1)} %get-tuple-element.59), channel_id=1, source_target_pairs={{0,3},{1,2},{2,1},{3,0},{4,7},{5,6},{6,5},{7,4},{8,11},{9,10},{10,... | collective-permute-start | bytes 196616 | tf_op jit(solution)/shard_map/ppermute | solution.py:315
  25.3 5.3 %collective-permute-start.8 = (f32[32,512]{1,0:T(8,128)S(1)}, f32[32,512]{1,0:T(8,128)S(1)}, u32[]{:S(2)}, u32[]{:S(2)}) collective-permute-start(f32[32,512]{1,0:T(8,128)S(1)} %get-tuple-element.60), channel_id=1, source_target_pairs={{0,2},{1,3},{2,0},{3,1},{4,6},{5,7},{6,4},{7,5},{8,10},{9,11},{10,... | collective-permute-start | bytes 196616 | tf_op jit(solution)/shard_map/ppermute | solution.py:315
  25.7 5.6 %collective-permute-start.13 = (f32[32,512]{1,0:T(8,128)S(1)}, f32[32,512]{1,0:T(8,128)S(1)}, u32[]{:S(2)}, u32[]{:S(2)}) collective-permute-start(f32[32,512]{1,0:T(8,128)S(1)} %get-tuple-element.66), channel_id=1, source_target_pairs={{0,1},{1,0},{2,3},{3,2},{4,5},{5,4},{6,7},{7,6},{8,9},{9,8},{10,11... | collective-permute-start | bytes 196616 | tf_op jit(solution)/shard_map/ppermute | solution.py:315
  31.4 4.4 %collective-permute-start.15 = (f32[134,512]{1,0:T(8,128)S(1)}, f32[134,512]{1,0:T(8,128)S(1)}, u32[]{:S(2)}, u32[]{:S(2)}) collective-permute-start(f32[134,512]{1,0:T(8,128)S(1)} %shard_map.92), channel_id=1, source_target_pairs={{0,28},{1,29},{2,30},{3,31},{4,0},{5,1},{6,2},{7,3},{8,4},{9,5},{1... | collective-permute-start | bytes 823304 | tf_op jit(solution)/shard_map/ppermute | solution.py:315
  31.6 6.8 %collective-permute-start.11 = (f32[32,512]{1,0:T(8,128)S(1)}, f32[32,512]{1,0:T(8,128)S(1)}, u32[]{:S(2)}, u32[]{:S(2)}) collective-permute-start(f32[32,512]{1,0:T(8,128)S(1)} %get-tuple-element.64), channel_id=1, source_target_pairs={{0,3},{1,2},{2,1},{3,0},{4,7},{5,6},{6,5},{7,4},{8,11},{9,10},{10,... | collective-permute-start | bytes 196616 | tf_op jit(solution)/shard_map/ppermute | solution.py:315
  32.7 5.7 %collective-permute-start.12 = (f32[32,512]{1,0:T(8,128)S(1)}, f32[32,512]{1,0:T(8,128)S(1)}, u32[]{:S(2)}, u32[]{:S(2)}) collective-permute-start(f32[32,512]{1,0:T(8,128)S(1)} %get-tuple-element.65), channel_id=1, source_target_pairs={{0,2},{1,3},{2,0},{3,1},{4,6},{5,7},{6,4},{7,5},{8,10},{9,11},{10,... | collective-permute-start | bytes 196616 | tf_op jit(solution)/shard_map/ppermute | solution.py:315
  35.2 4.3 %collective-permute-start.14 = (f32[32,512]{1,0:T(8,128)S(1)}, f32[32,512]{1,0:T(8,128)S(1)}, u32[]{:S(2)}, u32[]{:S(2)}) collective-permute-start(f32[32,512]{1,0:T(8,128)S(1)} %get-tuple-element.68.refs_1_.refs_6_), channel_id=1, source_target_pairs={{0,1},{1,0},{2,3},{3,2},{4,5},{5,4},{6,7},{7,6},{8,9},{9,8},{10,11... | collective-permute-start | bytes 196616 | tf_op jit(solution)/shard_map/ppermute | solution.py:315

commit v4 on v3

--- a/solution.py
+++ b/solution.py
@@ -10,16 +10,11 @@
 TOUCHED = 32
 WHOLE = (0, 1, 2)
 
-
-BLOCK_LATE = 0
-STACK_LATE = False
-VMEM = 24
-PACK_LATE = True
 HOME_CHUNKS = 4
-FIN_LATE = True
 FLOPS = dict(
-    split=80000000, first=100000000000, pack=1400000000, prep0=900000000, block=200000000, tile0=1000000000, tile1=800000000, items=900000000, pack1=500000000,
-    prep1=900000000, stack=0, next=900000000, owner=6000000000, join=0, preph=900000000, home=2000000000, fin=1200000000,
+    split=8 * 10**7, first=10**11, pack=14 * 10**8, prep0=9 * 10**8, block=2 * 10**8, tile0=10**9, tile1=8 * 10**8,
+    items=9 * 10**8, pack1=5 * 10**8, prep1=9 * 10**8, stack=0, next=2 * 10**9, owner=6 * 10**9, join=0,
+    home=25 * 10**8, fin=12 * 10**8,
 )
 
 F32 = jnp.float32
@@ -91,7 +86,7 @@
         in_specs=[pl.BlockSpec(memory_space=pltpu.VMEM)] * len(args) + [pl.BlockSpec(memory_space=pl.ANY)] * len(after),
         out_specs=[pl.BlockSpec(memory_space=pl.ANY if hbm_out and at == 0 else pltpu.VMEM) for at in range(len(outs))],
         scratch_shapes=list(scratch),
-        compiler_params=pltpu.CompilerParams(vmem_limit_bytes=VMEM * 2**20),
+        compiler_params=pltpu.CompilerParams(vmem_limit_bytes=24 * 2**20),
         cost_estimate=pl.CostEstimate(flops=flops, bytes_accessed=size, transcendentals=0),
     )(*args, *after)
 
@@ -154,8 +149,7 @@
     vh_ref[...], vl_ref[...] = split2(v_ref[...])
 
 
-def prep_kernel(entry_ref, n_ref, r_ref):
-    touched, items = n_ref.shape
+def entry_tables(entry_ref, touched, items):
     low = touched if entry_ref.shape[0] > touched else 0
     per = (entry_ref.shape[0] - low) // FIELDS
     fields = [
@@ -167,8 +161,12 @@
     values = split3(fields[2])
     left = [hot.astype(BF16)] + [(hot * v.astype(F32)).astype(BF16) for v in values]
     table = dot(jnp.concatenate(left, axis=0), one_hot(fields[1].astype(jnp.int32), items), NT)
-    n_ref[...] = table[:touched]
-    r_ref[...] = (table[touched : 2 * touched] + table[2 * touched : 3 * touched]) + table[3 * touched :]
+    sums = (table[touched : 2 * touched] + table[2 * touched : 3 * touched]) + table[3 * touched :]
+    return table[:touched], sums
+
+
+def prep_kernel(entry_ref, n_ref, r_ref):
+    n_ref[...], r_ref[...] = entry_tables(entry_ref, *n_ref.shape)
 
 
 def twice(ah, al, bh, bl, dims):
@@ -232,11 +230,22 @@
     out_refs[-2][...], out_refs[-1][...] = split2(v)
 
 
-def home_kernel(step, rows_ref, n_ref, r_ref, v_ref, vh_ref, vl_ref, out_ref, done_ref, held_ref, sems):
-    rows = rows_ref[: n_ref.shape[0], :]
+def message_weights(touched, message_ref, vh, vl):
+    rows = message_ref[:touched, :]
+    uh, ul = split2(rows)
+    counted, sums = entry_tables(message_ref, touched, vh.shape[0])
+    return rows, sums - counted * twice(uh, ul, vh, vl, NT)
+
+
+def next_kernel(step, touched, message_ref, v_ref, vh_ref, vl_ref):
+    v = v_ref[...]
+    rows, weights = message_weights(touched, message_ref, *split2(v))
+    vh_ref[...], vl_ref[...] = split2(item_update(step, weights, rows, v))
+
+
+def home_kernel(step, touched, message_ref, v_ref, vh_ref, vl_ref, out_ref, done_ref, held_ref, sems):
     done_ref[...] = jnp.zeros_like(done_ref)
-    uh, ul = split2(rows)
-    weights = r_ref[...] - n_ref[...] * twice(uh, ul, vh_ref[...], vl_ref[...], NT)
+    rows, weights = message_weights(touched, message_ref, vh_ref[...], vl_ref[...])
     chunk = held_ref.shape[0] // HOME_CHUNKS
     copies = []
     for at in range(HOME_CHUNKS):
@@ -248,25 +257,17 @@
         copy.wait()
 
 
-def join_kernel(*refs):
+def join_kernel(places, *refs):
     *row_refs, entry_ref, out_ref = refs
-    at = 0
-    for ref in row_refs:
-        out_ref[at : at + TOUCHED, :] = ref[...]
-        at += TOUCHED
     width = out_ref.shape[1]
+    at = TOUCHED * sum(len(ks) for ks in places)
+    for ks, ref in zip(places, row_refs):
+        for i, k in enumerate(ks):
+            out_ref[k * TOUCHED : (k + 1) * TOUCHED, :] = ref[i * TOUCHED : (i + 1) * TOUCHED, ref.shape[1] - width :]
     for f in range(entry_ref.shape[0]):
         for low in range(0, entry_ref.shape[1], width):
             out_ref[at : at + 1, :] = entry_ref[f : f + 1, low : low + width]
             at += 1
-
-
-def stack_kernel(*refs):
-    *in_refs, out_ref = refs
-    at = 0
-    for ref in in_refs:
-        out_ref[at : at + ref.shape[0], :] = ref[...]
-        at += ref.shape[0]
 
 
 def owner_kernel(order, t, step, *refs):
@@ -316,6 +317,10 @@
 
     def prepare(values, flops, after=()):
         return call(prep_kernel, [shaped((touched, items))] * 2, values, flops=flops, after=after)
+
+    def join(places, blocks, entry_rows, flops, after):
+        out = shaped((touched + FIELDS * entries // rank, rank))
+        return call(functools.partial(join_kernel, places), [out], *blocks, entry_rows, flops=flops, after=after)[0]
 
     def tile(piece, first, *args, after=()):
         *out, factors = call(
@@ -347,16 +352,17 @@
         [shaped((run, width)), shaped((subs * n, run)), shaped((FIELDS, entries))],
         *listed, flops=FLOPS["pack"], after=picked,
     )
+    entries_first = packed
     tables = prepare(packed, FLOPS["prep0"])
     block_parts = call(
         block_kernel, [shaped(item_factors.shape, BF16)] * 2,
-        item_factors, flops=FLOPS["block"], after=[*(picked if BLOCK_LATE != 2 else [rows[1]]), *(tables if BLOCK_LATE == 1 else [])],
+        item_factors, flops=FLOPS["block"], after=picked,
     )
     next_block = exchange(item_factors, 0, 1)
 
     grads, factors = {}, []
-    rest = tuple(k for k in range(n) if k not in whole)
-    for piece in (whole, rest) if rest else (whole,):
+    first_pieces = ((0, 1), tuple(range(n - 1, 1, -1)))
+    for piece in first_pieces:
         factors.append(tile(piece, True, codes, pieces[1], *block_parts, *tables, after=factors[-1:]))
     parts = [exchange(grads[k], k) for k in range(n)]
     block, *block_parts = call(
@@ -366,16 +372,13 @@
     )
     packed = call(
         functools.partial(pack_kernel, n, 1), [shaped((FIELDS, entries))],
-        *listed, ranked, flops=FLOPS["pack1"], after=[block] if PACK_LATE else factors[-1:],
+        *listed, ranked, flops=FLOPS["pack1"], after=[block],
     )[0]
     tables = prepare(packed, FLOPS["prep1"])
-    factors = call(
-        stack_kernel, [shaped((touched, items + rank))], *factors, flops=FLOPS["stack"],
-        after=[block] if STACK_LATE else [],
-    )[0]
+    joined = join(first_pieces, factors, entries_first, FLOPS["stack"], [])
     next_parts = call(
-        functools.partial(items_kernel, steps[0], 1), [shaped(item_factors.shape, BF16)] * 2,
-        exchange(factors, 0, 1), next_block, flops=FLOPS["next"],
+        functools.partial(next_kernel, steps[0], touched), [shaped(item_factors.shape, BF16)] * 2,
+        exchange(joined, 0, 1), next_block, flops=FLOPS["next"],
     )
     ranked = [parts[k] for k in sent]
     own, *mine = call(
@@ -391,22 +394,17 @@
     for piece in later_pieces:
         done.append(tile(piece, False, *next_parts, *tables, after=done[-1:]))
     parts = [exchange(grads[k], k) for k in range(n)]
-    joined = call(
-        join_kernel, [shaped((touched + FIELDS * entries // rank, rank))], *rows, packed, flops=FLOPS["join"],
-        after=[grads[later_pieces[0][0]]],
-    )[0]
-    joined = exchange(joined, 0, -1)
-    tables_home = prepare(joined, FLOPS["preph"], [grads[later_pieces[-1][0]]])
+    joined = join([(k,) for k in range(n)], rows, packed, FLOPS["join"], [grads[later_pieces[0][0]]])
     block, after_block = call(
-        functools.partial(home_kernel, steps[1]), [shaped(block.shape), shaped((8, LANES))],
-        joined, *tables_home, block, *block_parts,
+        functools.partial(home_kernel, steps[1], touched), [shaped(block.shape), shaped((8, LANES))],
+        exchange(joined, 0, -1), block, *block_parts,
         flops=FLOPS["home"], after=[grads[later_pieces[-1][0]]], hbm_out=True,
         scratch=[pltpu.VMEM(block.shape, F32), pltpu.SemaphoreType.DMA((HOME_CHUNKS,))],
     )
     own = call(
         functools.partial(owner_kernel, sent, 1, steps[1]), [shaped(own.shape)],
         *[parts[k] for k in sent], *[dict(zip(sent, ranked))[k] for k in sent], own, flops=FLOPS["fin"],
-        after=[after_block] if FIN_LATE else [],
+        after=[after_block],
     )[0]
     return own, block
 

time: 40.6 us -> 39.9 us (0.983)
  waiting for transfers between devices: 6.98 us -> 4.55 us
  starting transfers between devices: 18.6 us -> 19.5 us
  Pallas kernels: 12.4 us -> 13.2 us
    ppermute x16, waiting for transfers between devices: 6.98 us -> 4.55 us  [exchange(): return lax.ppermute(value, ('rows', 'strata'), pairs)]
    ppermute x16, starting transfers between devices: 18.6 us -> 19.5 us  [exchange(): return lax.ppermute(value, ('rows', 'strata'), pairs)]
    pallas_call x19 -> x18, Pallas kernels: 12.4 us -> 13.2 us  [call(): pl.pallas_call(body, out_shape=list(outs), in_specs=[pl.BlockSpec(memory_...]
  transfers between devices with their start and end apart: 16 -> 16, of which waited for: 5 -> 8; matrix products, arithmetic and copies ran while one was open for 0% -> 0% of each run, Pallas kernels for 28% -> 31%
where the time goes in v4:
time: 39.9 us; the launch traced here: 39.7 us
  starting transfers between devices  19.5 us (49%)
  Pallas kernels  13.2 us (33%)
  waiting for transfers between devices  4.55 us (11%)
  local copies, waits for them, and re-layouts  1.63 us (4%)
  between operations  0.84 us (2%)
    ppermute x16, starting transfers between devices, exchange(): return lax.ppermute(value, ('rows', 'strata'), pairs)  19.5 us
    pallas_call x18, Pallas kernels, call(): pl.pallas_call(body, out_shape=list(outs), in_specs=[pl.BlockSpec(memory_...  13.2 us
    ppermute x16, waiting for transfers between devices, exchange(): return lax.ppermute(value, ('rows', 'strata'), pairs)  4.55 us
    unnamed x14, local copies, waits for them, and re-layouts  1.63 us
  transfers between devices with their start and end apart: 16, of which 8 were waited for; matrix products, arithmetic and copies ran while one was open for 0% of the time, Pallas kernels for 31%

profile of v4, /device:TPU:0, one launch (start us, length us, event | category | flops | bytes accessed | tf_op | source)
XLA Modules:
  0.0 39.7 jit_solution(1124615590020429694)
XLA Ops:
  0.6 4.0 %collective-permute-start.1 = (s32[2,1024]{1,0:T(2,128)}, s32[2,1024]{1,0:T(2,128)S(1)}, u32[]{:S(2)}, u32[]{:S(2)}) collective-permute-start(s32[2,1024]{1,0:T(2,128)} %refs_0_.7), channel_id=1, source_target_pairs={{0,3},{1,2},{2,1},{3,0},{4,7},{5,6},{6,5},{7,4},{8,11},{9,10},{10,... | collective-permute-start | bytes 24584 | tf_op jit(solution)/shard_map/ppermute | solution.py:316
  4.6 0.5 %collective-permute-start = (f32[128,512]{1,0:T(8,128)}, f32[128,512]{1,0:T(8,128)S(1)}, u32[]{:S(2)}, u32[]{:S(2)}) collective-permute-start(f32[128,512]{1,0:T(8,128)} %refs_4_.1), channel_id=1, source_target_pairs={{0,1},{1,0},{2,3},{3,2},{4,5},{5,4},{6,7},{7,6},{8,9},{9,8},{10,11... | collective-permute-start | bytes 786440 | tf_op jit(solution)/shard_map/ppermute | solution.py:316
  5.2 1.0 %copy-done.1 = f32[128,512]{1,0:T(8,128)S(1)} copy-done((f32[128,512]{1,0:T(8,128)S(1)}, f32[128,512]{1,0:T(8,128)}, u32[]{:S(2)}) %copy-start.1) | copy-done | bytes 262168
  6.4 0.5 %shard_map.78.refs_4_.refs_1_ = f32[32,512]{1,0:T(8,128)S(1)} custom-call(s32[2,1024]{1,0:T(2,128)S(1)} %collective-permute-done.1.refs_0_, bf16[128,512]{1,0:T(8,128)(2,1)S(1)} %get-tuple-element.37.refs_1_.refs_0_, bf16[128,512]{1,0:T(8,128)(2,1)S(1)} %get-tuple-element.38.refs_2_.refs_3_, bf16[128,512]{1,0:T(8,128)(2,1)S(1)} %get-tuple-element.39.refs_3_), custom_call_target="tpu_custom_call" | custom-call | flops 99999997952 | bytes 466944 | tf_op jit(solution)/shard_map/pallas_call | solution.py:83
  6.9 3.1 %collective-permute-start.2 = (f32[32,512]{1,0:T(8,128)S(1)}, f32[32,512]{1,0:T(8,128)S(1)}, u32[]{:S(2)}, u32[]{:S(2)}) collective-permute-start(f32[32,512]{1,0:T(8,128)S(1)} %shard_map.78.refs_4_.refs_1_), channel_id=1, source_target_pairs={{0,3},{1,2},{2,1},{3,0},{4,7},{5,6},{6,5},{7,4},{8,11},{9,10},{10,... | collective-permute-start | bytes 196616 | tf_op jit(solution)/shard_map/ppermute | solution.py:316
  10.2 0.6 %copy-done.6 = s32[2,1]{0,1:T(1,128)S(1)} copy-done((s32[2,1]{0,1:T(1,128)S(1)}, s32[2,1]{0,1:T(1,128)}, u32[]{:S(2)}) %copy-start.6) | copy-done | bytes 32
  10.8 1.2 %shard_map.79 = (f32[128,128]{1,0:T(8,128)S(1)}, f32[8,128]{1,0:T(8,128)S(1)}, f32[3,1024]{1,0:T(4,128)S(1)}) custom-call(s32[2,1024]{1,0:T(2,128)S(1)} %copy-done.3, s32[2,1024]{1,0:T(2,128)S(1)} %copy-done.4, f32[2,1024]{1,0:T(2,128)S(1)} %copy-done.5, s32[1,2]{1,0:T(1,128)S(1)} %bitcast.1, f32[32,512]{1,0:T(8,128)S(1)} %shard_map.78.refs_4_.refs_1_), custom_call_target="tpu_custom_call" | custom-call | flops 1400000000 | bytes 106504 | tf_op jit(solution)/shard_map/pallas_call | solution.py:83
  12.0 0.8 %shard_map.81 = (f32[128,512]{1,0:T(8,128)S(1)}, f32[128,512]{1,0:T(8,128)S(1)}) custom-call(f32[3,1024]{1,0:T(4,128)S(1)} %get-tuple-element.43.refs_0_.refs_2_), custom_call_target="tpu_custom_call" | custom-call | flops 900000000 | bytes 536576 | tf_op jit(solution)/shard_map/pallas_call | solution.py:83
  12.8 0.8 %shard_map.82 = (f32[40,512]{1,0:T(8,128)S(1)}, f32[40,512]{1,0:T(8,128)S(1)}, f32[64,1024]{1,0:T(8,128)S(1)}) custom-call(bf16[128,512]{1,0:T(8,128)(2,1)S(1)} %get-tuple-element.37.refs_1_.refs_0_, f32[128,512]{1,0:T(8,128)S(1)} %collective-permute-done.refs_1_, f32[8,128]{1,0:T(8,128)S(1)} %get-tuple-element.40.refs_2_, ...), custom_call_target="tpu_custom_call" | custom-call | flops 1000000000 | bytes 2527232 | tf_op jit(solution)/shard_map/pallas_call | solution.py:83
  14.2 0.8 %shard_map.83 = (f32[40,512]{1,0:T(8,128)S(1)}, f32[40,512]{1,0:T(8,128)S(1)}, f32[64,1024]{1,0:T(8,128)S(1)}) custom-call(f32[32,512]{1,0:T(8,128)S(1)} %collective-permute-done.2.refs_0_, f32[128,512]{1,0:T(8,128)S(1)} %collective-permute-done.3.refs_1_, f32[8,128]{1,0:T(8,128)S(1)} %get-tuple-element.40.refs_2_, ...), custom_call_target="tpu_custom_call" | custom-call | flops 1000000000 | bytes 2461696 | tf_op jit(solution)/shard_map/pallas_call | solution.py:83
  15.0 1.4 %collective-permute-start.4 = (f32[40,512]{1,0:T(8,128)S(1)}, f32[40,512]{1,0:T(8,128)S(1)}, u32[]{:S(2)}, u32[]{:S(2)}) collective-permute-start(f32[40,512]{1,0:T(8,128)S(1)} %get-tuple-element.48), channel_id=1, source_target_pairs={{0,3},{1,2},{2,1},{3,0},{4,7},{5,6},{6,5},{7,4},{8,11},{9,10},{10,... | collective-permute-start | bytes 245768 | tf_op jit(solution)/shard_map/ppermute | solution.py:316
  16.4 1.6 %collective-permute-start.5 = (f32[40,512]{1,0:T(8,128)S(1)}, f32[40,512]{1,0:T(8,128)S(1)}, u32[]{:S(2)}, u32[]{:S(2)}) collective-permute-start(f32[40,512]{1,0:T(8,128)S(1)} %get-tuple-element.49), channel_id=1, source_target_pairs={{0,2},{1,3},{2,0},{3,1},{4,6},{5,7},{6,4},{7,5},{8,10},{9,11},{10,... | collective-permute-start | bytes 245768 | tf_op jit(solution)/shard_map/ppermute | solution.py:316
  18.0 0.5 %collective-permute-start.6 = (f32[40,512]{1,0:T(8,128)S(1)}, f32[40,512]{1,0:T(8,128)S(1)}, u32[]{:S(2)}, u32[]{:S(2)}) collective-permute-start(f32[40,512]{1,0:T(8,128)S(1)} %get-tuple-element.50), channel_id=1, source_target_pairs={{0,1},{1,0},{2,3},{3,2},{4,5},{5,4},{6,7},{7,6},{8,9},{9,8},{10,11... | collective-permute-start | bytes 245768 | tf_op jit(solution)/shard_map/ppermute | solution.py:316
  18.6 0.7 %shard_map.84 = (f32[512,512]{1,0:T(8,128)S(1)}, bf16[512,512]{1,0:T(8,128)(2,1)S(1)}, bf16[512,512]{1,0:T(8,128)(2,1)S(1)}) custom-call(f32[64,1024]{1,0:T(8,128)S(1)} %get-tuple-element.47.refs_8_.refs_0_, f32[64,1024]{1,0:T(8,128)S(1)} %get-tuple-element.51.refs_1_, f32[512,512]{1,0:T(8,128)S(1)} %copy-done), custom_call_target="tpu_custom_call" | custom-call | flops 900000000 | bytes 3670016 | tf_op jit(solution)/shard_map/pallas_call | solution.py:83
  19.8 0.8 %shard_map.86 = (f32[128,512]{1,0:T(8,128)S(1)}, f32[128,512]{1,0:T(8,128)S(1)}) custom-call(f32[3,1024]{1,0:T(4,128)S(1)} %shard_map.85.refs_0_.refs_4_), custom_call_target="tpu_custom_call" | custom-call | flops 900000000 | bytes 536576 | tf_op jit(solution)/shard_map/pallas_call | solution.py:83
  20.6 0.6 %collective-permute-done.4.refs_1_.refs_5_ = f32[40,512]{1,0:T(8,128)S(1)} collective-permute-done((f32[40,512]{1,0:T(8,128)S(1)}, f32[40,512]{1,0:T(8,128)S(1)}, u32[]{:S(2)}, u32[]{:S(2)}) %collective-permute-start.4) | collective-permute-done | bytes 81952 | tf_op jit(solution)/shard_map/ppermute | solution.py:316
  21.2 1.4 %collective-permute-done.5.refs_2_.refs_6_ = f32[40,512]{1,0:T(8,128)S(1)} collective-permute-done((f32[40,512]{1,0:T(8,128)S(1)}, f32[40,512]{1,0:T(8,128)S(1)}, u32[]{:S(2)}, u32[]{:S(2)}) %collective-permute-start.5) | collective-permute-done | bytes 81952 | tf_op jit(solution)/shard_map/ppermute | solution.py:316
  22.6 0.6 %shard_map.87 = (f32[128,512]{1,0:T(8,128)S(1)}, f32[32,512]{1,0:T(8,128)S(1)}, f32[32,512]{1,0:T(8,128)S(1)}, f32[32,512]{1,0:T(8,128)S(1)}, f32[32,512]{1,0:T(8,128)S(1)}) custom-call(f32[40,512]{1,0:T(8,128)S(1)} %get-tuple-element.46.refs_0_.refs_4_, f32[40,512]{1,0:T(8,128)S(1)} %collective-permute-done.4.refs_1_.refs_5_, ...), custom_call_target="tpu_custom_call" | custom-call | flops 6000000000 | bytes 1114112 | tf_op jit(solution)/shard_map/pallas_call | solution.py:83
  23.1 1.4 %collective-permute-start.7 = (f32[32,512]{1,0:T(8,128)S(1)}, f32[32,512]{1,0:T(8,128)S(1)}, u32[]{:S(2)}, u32[]{:S(2)}) collective-permute-start(f32[32,512]{1,0:T(8,128)S(1)} %get-tuple-element.57), channel_id=1, source_target_pairs={{0,3},{1,2},{2,1},{3,0},{4,7},{5,6},{6,5},{7,4},{8,11},{9,10},{10,... | collective-permute-start | bytes 196616 | tf_op jit(solution)/shard_map/ppermute | solution.py:316
  24.5 0.7 %collective-permute-start.8 = (f32[32,512]{1,0:T(8,128)S(1)}, f32[32,512]{1,0:T(8,128)S(1)}, u32[]{:S(2)}, u32[]{:S(2)}) collective-permute-start(f32[32,512]{1,0:T(8,128)S(1)} %get-tuple-element.58), channel_id=1, source_target_pairs={{0,2},{1,3},{2,0},{3,1},{4,6},{5,7},{6,4},{7,5},{8,10},{9,11},{10,... | collective-permute-start | bytes 196616 | tf_op jit(solution)/shard_map/ppermute | solution.py:316
  25.2 1.5 %collective-permute-start.13 = (f32[32,512]{1,0:T(8,128)S(1)}, f32[32,512]{1,0:T(8,128)S(1)}, u32[]{:S(2)}, u32[]{:S(2)}) collective-permute-start(f32[32,512]{1,0:T(8,128)S(1)} %get-tuple-element.64), channel_id=1, source_target_pairs={{0,1},{1,0},{2,3},{3,2},{4,5},{5,4},{6,7},{7,6},{8,9},{9,8},{10,11... | collective-permute-start | bytes 196616 | tf_op jit(solution)/shard_map/ppermute | solution.py:316
  26.7 1.7 %shard_map.89 = (bf16[512,512]{1,0:T(8,128)(2,1)S(1)}, bf16[512,512]{1,0:T(8,128)(2,1)S(1)}) custom-call(f32[134,512]{1,0:T(8,128)S(1)} %collective-permute-done.9.refs_0_, f32[512,512]{1,0:T(8,128)S(1)} %collective-permute-done.10.refs_1_), custom_call_target="tpu_custom_call" | custom-call | flops 2000000000 | bytes 2371584 | tf_op jit(solution)/shard_map/pallas_call | solution.py:83
  28.8 0.8 %collective-permute-done.8.refs_2_ = f32[32,512]{1,0:T(8,128)S(1)} collective-permute-done((f32[32,512]{1,0:T(8,128)S(1)}, f32[32,512]{1,0:T(8,128)S(1)}, u32[]{:S(2)}, u32[]{:S(2)}) %collective-permute-start.8) | collective-permute-done | bytes 65568 | tf_op jit(solution)/shard_map/ppermute | solution.py:316
  29.5 0.8 %shard_map.90 = (f32[32,512]{1,0:T(8,128)S(1)}, f32[32,512]{1,0:T(8,128)S(1)}, f32[32,512]{1,0:T(8,128)S(1)}, f32[8,128]{1,0:T(8,128)S(1)}) custom-call(f32[32,512]{1,0:T(8,128)S(1)} %get-tuple-element.56.refs_0_, f32[32,512]{1,0:T(8,128)S(1)} %collective-permute-done.7.refs_1_.refs_3_, f32[32,512]{1,0:T(8,128)S(1)} %collective-permute-done.8.refs_2_, ...), custom_call_target="tpu_custom_call" | custom-call | flops 800000000 | bytes 1970176 | tf_op jit(solution)/shard_map/pallas_call | solution.py:83
  30.3 1.2 %collective-permute-start.15 = (f32[134,512]{1,0:T(8,128)S(1)}, f32[134,512]{1,0:T(8,128)S(1)}, u32[]{:S(2)}, u32[]{:S(2)}) collective-permute-start(f32[134,512]{1,0:T(8,128)S(1)} %shard_map.92), channel_id=1, source_target_pairs={{0,28},{1,29},{2,30},{3,31},{4,0},{5,1},{6,2},{7,3},{8,4},{9,5},{1... | collective-permute-start | bytes 823304 | tf_op jit(solution)/shard_map/ppermute | solution.py:316
  31.5 1.0 %collective-permute-start.11 = (f32[32,512]{1,0:T(8,128)S(1)}, f32[32,512]{1,0:T(8,128)S(1)}, u32[]{:S(2)}, u32[]{:S(2)}) collective-permute-start(f32[32,512]{1,0:T(8,128)S(1)} %get-tuple-element.62), channel_id=1, source_target_pairs={{0,3},{1,2},{2,1},{3,0},{4,7},{5,6},{6,5},{7,4},{8,11},{9,10},{10,... | collective-permute-start | bytes 196616 | tf_op jit(solution)/shard_map/ppermute | solution.py:316
  32.5 1.2 %collective-permute-start.12 = (f32[32,512]{1,0:T(8,128)S(1)}, f32[32,512]{1,0:T(8,128)S(1)}, u32[]{:S(2)}, u32[]{:S(2)}) collective-permute-start(f32[32,512]{1,0:T(8,128)S(1)} %get-tuple-element.63), channel_id=1, source_target_pairs={{0,2},{1,3},{2,0},{3,1},{4,6},{5,7},{6,4},{7,5},{8,10},{9,11},{10,... | collective-permute-start | bytes 196616 | tf_op jit(solution)/shard_map/ppermute | solution.py:316
  33.8 0.7 %shard_map.91 = (f32[32,512]{1,0:T(8,128)S(1)}, f32[8,128]{1,0:T(8,128)}) custom-call(f32[32,512]{1,0:T(8,128)S(1)} %collective-permute-done.13.refs_0_.refs_1_, bf16[512,512]{1,0:T(8,128)(2,1)S(1)} %get-tuple-element.59.refs_3_.refs_1_, bf16[512,512]{1,0:T(8,128)(2,1)S(1)} %get-tuple-element.60.refs_4_.refs_2_, ...), custom_call_target="tpu_custom_call" | custom-call | flops 800000000 | bytes 1708032 | tf_op jit(solution)/shard_map/pallas_call | solution.py:83
  34.4 1.3 %collective-permute-start.14 = (f32[32,512]{1,0:T(8,128)S(1)}, f32[32,512]{1,0:T(8,128)S(1)}, u32[]{:S(2)}, u32[]{:S(2)}) collective-permute-start(f32[32,512]{1,0:T(8,128)S(1)} %get-tuple-element.66.refs_4_), channel_id=1, source_target_pairs={{0,1},{1,0},{2,3},{3,2},{4,5},{5,4},{6,7},{7,6},{8,9},{9,8},{10,11... | collective-permute-start | bytes 196616 | tf_op jit(solution)/shard_map/ppermute | solution.py:316
  35.7 2.3 %shard_map.93 = (f32[512,512]{1,0:T(8,128)}, f32[8,128]{1,0:T(8,128)S(1)}) custom-call(f32[134,512]{1,0:T(8,128)S(1)} %collective-permute-done.15.refs_0_, f32[512,512]{1,0:T(8,128)S(1)} %get-tuple-element.52.refs_5_.refs_1_, bf16[512,512]{1,0:T(8,128)(2,1)S(1)} %get-tuple-element.68.refs_2_, bf16[512,512]{1,0:T(8,128)(2,1)S(1)} %get-tuple-element.69.refs_3_, ...), custom_call_target="tpu_custom_call" | custom-call | flops 2500000000 | bytes 3424256 | tf_op jit(solution)/shard_map/pallas_call | solution.py:83
  38.1 0.7 %collective-permute-done.14.refs_3_ = f32[32,512]{1,0:T(8,128)S(1)} collective-permute-done((f32[32,512]{1,0:T(8,128)S(1)}, f32[32,512]{1,0:T(8,128)S(1)}, u32[]{:S(2)}, u32[]{:S(2)}) %collective-permute-start.14) | collective-permute-done | bytes 65568 | tf_op jit(solution)/shard_map/ppermute | solution.py:316
  38.7 1.0 %shard_map.94 = f32[128,512]{1,0:T(8,128)} custom-call(f32[32,512]{1,0:T(8,128)S(1)} %get-tuple-element.61.refs_5_.refs_0_, f32[32,512]{1,0:T(8,128)S(1)} %collective-permute-done.11.refs_1_, f32[32,512]{1,0:T(8,128)S(1)} %collective-permute-done.12.refs_2_, f32[32,512]{1,0:T(8,128)S(1)} %collective-permute-done.14.refs_3_, ...), custom_call_target="tpu_custom_call" | custom-call | flops 1200000000 | bytes 1114112 | tf_op jit(solution)/shard_map/pallas_call | solution.py:83
  (32 shorter events, 2.0 us)
Async XLA Ops:
  0.6 5.8 %collective-permute-start.1 = (s32[2,1024]{1,0:T(2,128)}, s32[2,1024]{1,0:T(2,128)S(1)}, u32[]{:S(2)}, u32[]{:S(2)}) collective-permute-start(s32[2,1024]{1,0:T(2,128)} %refs_0_.7), channel_id=1, source_target_pairs={{0,3},{1,2},{2,1},{3,0},{4,7},{5,6},{6,5},{7,4},{8,11},{9,10},{10,... | collective-permute-start | bytes 24584 | tf_op jit(solution)/shard_map/ppermute | solution.py:316
  4.6 8.2 %collective-permute-start = (f32[128,512]{1,0:T(8,128)}, f32[128,512]{1,0:T(8,128)S(1)}, u32[]{:S(2)}, u32[]{:S(2)}) collective-permute-start(f32[128,512]{1,0:T(8,128)} %refs_4_.1), channel_id=1, source_target_pairs={{0,1},{1,0},{2,3},{3,2},{4,5},{5,4},{6,7},{7,6},{8,9},{9,8},{10,11... | collective-permute-start | bytes 786440 | tf_op jit(solution)/shard_map/ppermute | solution.py:316
  5.1 9.1 %collective-permute-start.3 = (f32[128,512]{1,0:T(8,128)}, f32[128,512]{1,0:T(8,128)S(1)}, u32[]{:S(2)}, u32[]{:S(2)}) collective-permute-start(f32[128,512]{1,0:T(8,128)} %refs_4_.1), channel_id=1, source_target_pairs={{0,2},{1,3},{2,0},{3,1},{4,6},{5,7},{6,4},{7,5},{8,10},{9,11},{10,... | collective-permute-start | bytes 786440 | tf_op jit(solution)/shard_map/ppermute | solution.py:316
  5.2 21.5 %collective-permute-start.10 = (f32[512,512]{1,0:T(8,128)}, f32[512,512]{1,0:T(8,128)S(1)}, u32[]{:S(2)}, u32[]{:S(2)}) collective-permute-start(f32[512,512]{1,0:T(8,128)} %refs_2_.4), channel_id=1, source_target_pairs={{0,4},{1,5},{2,6},{3,7},{4,8},{5,9},{6,10},{7,11},{8,12},{9,13},{1... | collective-permute-start | bytes 3145736 | tf_op jit(solution)/shard_map/ppermute | solution.py:316
  5.2 1.0 %copy-start.1 = (f32[128,512]{1,0:T(8,128)S(1)}, f32[128,512]{1,0:T(8,128)}, u32[]{:S(2)}) copy-start(f32[128,512]{1,0:T(8,128)} %refs_4_.1) | copy-start | bytes 786436
  6.4 3.6 %copy-start = (f32[512,512]{1,0:T(8,128)S(1)}, f32[512,512]{1,0:T(8,128)}, u32[]{:S(2)}) copy-start(f32[512,512]{1,0:T(8,128)} %refs_2_.4) | copy-start | bytes 3145732
  6.9 3.3 %copy-start.3 = (s32[2,1024]{1,0:T(2,128)S(1)}, s32[2,1024]{1,0:T(2,128)}, u32[]{:S(2)}) copy-start(s32[2,1024]{1,0:T(2,128)} %refs_0_.7) | copy-start | bytes 24580
  6.9 3.3 %copy-start.4 = (s32[2,1024]{1,0:T(2,128)S(1)}, s32[2,1024]{1,0:T(2,128)}, u32[]{:S(2)}) copy-start(s32[2,1024]{1,0:T(2,128)} %refs_1_.3) | copy-start | bytes 24580
  6.9 3.3 %copy-start.5 = (f32[2,1024]{1,0:T(2,128)S(1)}, f32[2,1024]{1,0:T(2,128)}, u32[]{:S(2)}) copy-start(f32[2,1024]{1,0:T(2,128)} %refs_2_.5) | copy-start | bytes 24580
  6.9 7.1 %collective-permute-start.2 = (f32[32,512]{1,0:T(8,128)S(1)}, f32[32,512]{1,0:T(8,128)S(1)}, u32[]{:S(2)}, u32[]{:S(2)}) collective-permute-start(f32[32,512]{1,0:T(8,128)S(1)} %shard_map.78.refs_4_.refs_1_), channel_id=1, source_target_pairs={{0,3},{1,2},{2,1},{3,0},{4,7},{5,6},{6,5},{7,4},{8,11},{9,10},{10,... | collective-permute-start | bytes 196616 | tf_op jit(solution)/shard_map/ppermute | solution.py:316
  10.2 0.7 %copy-start.6 = (s32[2,1]{0,1:T(1,128)S(1)}, s32[2,1]{0,1:T(1,128)}, u32[]{:S(2)}) copy-start(s32[2,1]{0,1:T(1,128)} %param.11) | copy-start | bytes 28
  15.0 6.2 %collective-permute-start.4 = (f32[40,512]{1,0:T(8,128)S(1)}, f32[40,512]{1,0:T(8,128)S(1)}, u32[]{:S(2)}, u32[]{:S(2)}) collective-permute-start(f32[40,512]{1,0:T(8,128)S(1)} %get-tuple-element.48), channel_id=1, source_target_pairs={{0,3},{1,2},{2,1},{3,0},{4,7},{5,6},{6,5},{7,4},{8,11},{9,10},{10,... | collective-permute-start | bytes 245768 | tf_op jit(solution)/shard_map/ppermute | solution.py:316
  16.4 6.1 %collective-permute-start.5 = (f32[40,512]{1,0:T(8,128)S(1)}, f32[40,512]{1,0:T(8,128)S(1)}, u32[]{:S(2)}, u32[]{:S(2)}) collective-permute-start(f32[40,512]{1,0:T(8,128)S(1)} %get-tuple-element.49), channel_id=1, source_target_pairs={{0,2},{1,3},{2,0},{3,1},{4,6},{5,7},{6,4},{7,5},{8,10},{9,11},{10,... | collective-permute-start | bytes 245768 | tf_op jit(solution)/shard_map/ppermute | solution.py:316
  18.0 4.5 %collective-permute-start.6 = (f32[40,512]{1,0:T(8,128)S(1)}, f32[40,512]{1,0:T(8,128)S(1)}, u32[]{:S(2)}, u32[]{:S(2)}) collective-permute-start(f32[40,512]{1,0:T(8,128)S(1)} %get-tuple-element.50), channel_id=1, source_target_pairs={{0,1},{1,0},{2,3},{3,2},{4,5},{5,4},{6,7},{7,6},{8,9},{9,8},{10,11... | collective-permute-start | bytes 245768 | tf_op jit(solution)/shard_map/ppermute | solution.py:316
  18.6 8.1 %collective-permute-start.9 = (f32[134,512]{1,0:T(8,128)S(1)}, f32[134,512]{1,0:T(8,128)S(1)}, u32[]{:S(2)}, u32[]{:S(2)}) collective-permute-start(f32[134,512]{1,0:T(8,128)S(1)} %shard_map.88), channel_id=1, source_target_pairs={{0,4},{1,5},{2,6},{3,7},{4,8},{5,9},{6,10},{7,11},{8,12},{9,13},{1... | collective-permute-start | bytes 823304 | tf_op jit(solution)/shard_map/ppermute | solution.py:316
  19.8 2.8 %copy-start.2 = (f32[128,512]{1,0:T(8,128)S(1)}, f32[128,512]{1,0:T(8,128)}, u32[]{:S(2)}) copy-start(f32[128,512]{1,0:T(8,128)} %refs_4_.1) | copy-start | bytes 786436
  23.1 5.6 %collective-permute-start.7 = (f32[32,512]{1,0:T(8,128)S(1)}, f32[32,512]{1,0:T(8,128)S(1)}, u32[]{:S(2)}, u32[]{:S(2)}) collective-permute-start(f32[32,512]{1,0:T(8,128)S(1)} %get-tuple-element.57), channel_id=1, source_target_pairs={{0,3},{1,2},{2,1},{3,0},{4,7},{5,6},{6,5},{7,4},{8,11},{9,10},{10,... | collective-permute-start | bytes 196616 | tf_op jit(solution)/shard_map/ppermute | solution.py:316
  24.5 5.0 %collective-permute-start.8 = (f32[32,512]{1,0:T(8,128)S(1)}, f32[32,512]{1,0:T(8,128)S(1)}, u32[]{:S(2)}, u32[]{:S(2)}) collective-permute-start(f32[32,512]{1,0:T(8,128)S(1)} %get-tuple-element.58), channel_id=1, source_target_pairs={{0,2},{1,3},{2,0},{3,1},{4,6},{5,7},{6,4},{7,5},{8,10},{9,11},{10,... | collective-permute-start | bytes 196616 | tf_op jit(solution)/shard_map/ppermute | solution.py:316
  25.2 5.1 %collective-permute-start.13 = (f32[32,512]{1,0:T(8,128)S(1)}, f32[32,512]{1,0:T(8,128)S(1)}, u32[]{:S(2)}, u32[]{:S(2)}) collective-permute-start(f32[32,512]{1,0:T(8,128)S(1)} %get-tuple-element.64), channel_id=1, source_target_pairs={{0,1},{1,0},{2,3},{3,2},{4,5},{5,4},{6,7},{7,6},{8,9},{9,8},{10,11... | collective-permute-start | bytes 196616 | tf_op jit(solution)/shard_map/ppermute | solution.py:316
  30.3 5.4 %collective-permute-start.15 = (f32[134,512]{1,0:T(8,128)S(1)}, f32[134,512]{1,0:T(8,128)S(1)}, u32[]{:S(2)}, u32[]{:S(2)}) collective-permute-start(f32[134,512]{1,0:T(8,128)S(1)} %shard_map.92), channel_id=1, source_target_pairs={{0,28},{1,29},{2,30},{3,31},{4,0},{5,1},{6,2},{7,3},{8,4},{9,5},{1... | collective-permute-start | bytes 823304 | tf_op jit(solution)/shard_map/ppermute | solution.py:316
  31.5 6.6 %collective-permute-start.11 = (f32[32,512]{1,0:T(8,128)S(1)}, f32[32,512]{1,0:T(8,128)S(1)}, u32[]{:S(2)}, u32[]{:S(2)}) collective-permute-start(f32[32,512]{1,0:T(8,128)S(1)} %get-tuple-element.62), channel_id=1, source_target_pairs={{0,3},{1,2},{2,1},{3,0},{4,7},{5,6},{6,5},{7,4},{8,11},{9,10},{10,... | collective-permute-start | bytes 196616 | tf_op jit(solution)/shard_map/ppermute | solution.py:316
  32.5 5.5 %collective-permute-start.12 = (f32[32,512]{1,0:T(8,128)S(1)}, f32[32,512]{1,0:T(8,128)S(1)}, u32[]{:S(2)}, u32[]{:S(2)}) collective-permute-start(f32[32,512]{1,0:T(8,128)S(1)} %get-tuple-element.63), channel_id=1, source_target_pairs={{0,2},{1,3},{2,0},{3,1},{4,6},{5,7},{6,4},{7,5},{8,10},{9,11},{10,... | collective-permute-start | bytes 196616 | tf_op jit(solution)/shard_map/ppermute | solution.py:316
  34.4 4.3 %collective-permute-start.14 = (f32[32,512]{1,0:T(8,128)S(1)}, f32[32,512]{1,0:T(8,128)S(1)}, u32[]{:S(2)}, u32[]{:S(2)}) collective-permute-start(f32[32,512]{1,0:T(8,128)S(1)} %get-tuple-element.66.refs_4_), channel_id=1, source_target_pairs={{0,1},{1,0},{2,3},{3,2},{4,5},{5,4},{6,7},{7,6},{8,9},{9,8},{10,11... | collective-permute-start | bytes 196616 | tf_op jit(solution)/shard_map/ppermute | solution.py:316

commit v5 on v4

--- a/solution.py
+++ b/solution.py
@@ -44,8 +44,8 @@
 
 
 def pick(selector, x, dims):
-    hi, mid, lo = split3(x)
-    return (dot(selector, hi, dims) + dot(selector, mid, dims)) + dot(selector, lo, dims)
+    over = dims[0][0][0]
+    return dot(jnp.concatenate([selector, selector], axis=over), jnp.concatenate(split2(x), axis=0), dims)
 
 
 def iota(shape, dim):
@@ -53,7 +53,17 @@
 
 
 def one_hot(names, rows):
-    return (iota((rows, names.shape[1]), 0) == names).astype(F32).astype(BF16)
+    blocks = []
+    for low in range(0, rows, 256):
+        size = min(256, rows - low)
+        local = jnp.clip(names - low, -1, 256).astype(F32).astype(BF16)
+        row = iota((size, LANES), 0).astype(F32).astype(BF16)
+        one, zero = jnp.ones((size, LANES), BF16), jnp.zeros((size, LANES), BF16)
+        parts = [
+            jnp.where(row == local[:, at : at + LANES], one, zero) for at in range(0, names.shape[1], LANES)
+        ]
+        blocks.append(jnp.concatenate(parts, axis=1))
+    return jnp.concatenate(blocks, axis=0)
 
 
 def touched_by(names):
@@ -96,7 +106,7 @@
 
 
 def split_kernel(own_ref, *out_refs):
-    for out_ref, part in zip(out_refs, split3(own_ref[...])):
+    for out_ref, part in zip(out_refs, split2(own_ref[...])):
         out_ref[...] = part
 
 
@@ -106,8 +116,8 @@
     present = touched_by(names_ref[0:1, :] - lax.axis_index("strata") * run)(run)
     rank = ranks(jnp.broadcast_to(present, (run, LANES)))[:, :TOUCHED]
     sel = (iota(rank.shape, 1).astype(F32) == rank).astype(F32).astype(BF16)
-    hi, mid, lo = [dot(sel, ref[...], TN) for ref in part_refs]
-    out_ref[...] = (hi + mid) + lo
+    hi, lo = [dot(sel, ref[...], TN) for ref in part_refs]
+    out_ref[...] = hi + lo
 
 
 def run_names(user_ref, t, k, run):
@@ -156,13 +166,10 @@
         jnp.concatenate([entry_ref[at : at + 1, :] for at in range(low + f * per, low + (f + 1) * per)], axis=1)
         for f in range(FIELDS)
     ]
-    users = fields[0].astype(jnp.int32)
-    hot = (iota((touched, users.shape[1]), 0) == users).astype(F32)
-    values = split3(fields[2])
-    left = [hot.astype(BF16)] + [(hot * v.astype(F32)).astype(BF16) for v in values]
+    hot = one_hot(fields[0].astype(jnp.int32), touched)
+    left = [hot] + [hot * value for value in split2(fields[2])]
     table = dot(jnp.concatenate(left, axis=0), one_hot(fields[1].astype(jnp.int32), items), NT)
-    sums = (table[touched : 2 * touched] + table[2 * touched : 3 * touched]) + table[3 * touched :]
-    return table[:touched], sums
+    return table[:touched], table[touched : 2 * touched] + table[2 * touched :]
 
 
 def prep_kernel(entry_ref, n_ref, r_ref):
@@ -215,7 +222,7 @@
 
 def item_update(step, weights, rows, v):
     (wh, wl), (uh, ul) = split2(weights), split2(rows)
-    grads = dot(wh, uh, TN) + (dot(wl, uh, TN) + dot(wh, ul, TN))
+    grads = dot(jnp.concatenate([wh, wl, wh], axis=0), jnp.concatenate([uh, uh, ul], axis=0), TN)
     return v + step * (grads - 0.1 * v)
 
 
@@ -333,7 +340,7 @@
         return factors
 
     whole = tuple(k for k in WHOLE if k < n)
-    pieces = call(split_kernel, [shaped((run, rank), BF16)] * 3, user_factors, flops=FLOPS["split"])
+    pieces = call(split_kernel, [shaped((run, rank), BF16)] * 2, user_factors, flops=FLOPS["split"])
     rows = [pieces[0]] + [None] * (n - 1)
     picked = []
     for k in range(1, n):

time: 39.9 us -> 39.2 us (0.982)
  Pallas kernels: 13.2 us -> 12 us
  waiting for transfers between devices: 4.55 us -> 5.05 us
    pallas_call x18, Pallas kernels: 13.2 us -> 12 us  [call(): pl.pallas_call(body, out_shape=list(outs), in_specs=[pl.BlockSpec(memory_...]
    ppermute x16, waiting for transfers between devices: 4.55 us -> 5.05 us  [exchange(): return lax.ppermute(value, ('rows', 'strata'), pairs)]
  transfers between devices with their start and end apart: 16 -> 16, of which waited for: 8 -> 9; matrix products, arithmetic and copies ran while one was open for 0% -> 0% of each run, Pallas kernels for 31% -> 28%
where the time goes in v5:
time: 39.2 us; the launch traced here: 39.1 us
  starting transfers between devices  19.5 us (50%)
  Pallas kernels  12 us (31%)
  waiting for transfers between devices  5.05 us (13%)
  local copies, waits for them, and re-layouts  1.64 us (4%)
  between operations  0.85 us (2%)
    ppermute x16, starting transfers between devices, exchange(): return lax.ppermute(value, ('rows', 'strata'), pairs)  19.5 us
    pallas_call x18, Pallas kernels, call(): pl.pallas_call(body, out_shape=list(outs), in_specs=[pl.BlockSpec(memory_...  12 us
    ppermute x16, waiting for transfers between devices, exchange(): return lax.ppermute(value, ('rows', 'strata'), pairs)  5.05 us
    unnamed x14, local copies, waits for them, and re-layouts  1.64 us
  transfers between devices with their start and end apart: 16, of which 9 were waited for; matrix products, arithmetic and copies ran while one was open for 0% of the time, Pallas kernels for 28%

profile of v5, /device:TPU:0, one launch (start us, length us, event | category | flops | bytes accessed | tf_op | source)
XLA Modules:
  0.0 39.1 jit_solution(13167219774996603594)
XLA Ops:
  0.6 4.0 %collective-permute-start.1 = (s32[2,1024]{1,0:T(2,128)}, s32[2,1024]{1,0:T(2,128)S(1)}, u32[]{:S(2)}, u32[]{:S(2)}) collective-permute-start(s32[2,1024]{1,0:T(2,128)} %refs_0_.7), channel_id=1, source_target_pairs={{0,3},{1,2},{2,1},{3,0},{4,7},{5,6},{6,5},{7,4},{8,11},{9,10},{10,... | collective-permute-start | bytes 24584 | tf_op jit(solution)/shard_map/ppermute | solution.py:323
  4.6 0.5 %collective-permute-start = (f32[128,512]{1,0:T(8,128)}, f32[128,512]{1,0:T(8,128)S(1)}, u32[]{:S(2)}, u32[]{:S(2)}) collective-permute-start(f32[128,512]{1,0:T(8,128)} %refs_4_.1), channel_id=1, source_target_pairs={{0,1},{1,0},{2,3},{3,2},{4,5},{5,4},{6,7},{7,6},{8,9},{9,8},{10,11... | collective-permute-start | bytes 786440 | tf_op jit(solution)/shard_map/ppermute | solution.py:323
  5.2 1.0 %copy-done.1 = f32[128,512]{1,0:T(8,128)S(1)} copy-done((f32[128,512]{1,0:T(8,128)S(1)}, f32[128,512]{1,0:T(8,128)}, u32[]{:S(2)}) %copy-start.1) | copy-done | bytes 262168
  6.9 3.1 %collective-permute-start.2 = (f32[32,512]{1,0:T(8,128)S(1)}, f32[32,512]{1,0:T(8,128)S(1)}, u32[]{:S(2)}, u32[]{:S(2)}) collective-permute-start(f32[32,512]{1,0:T(8,128)S(1)} %shard_map.78.refs_4_.refs_1_), channel_id=1, source_target_pairs={{0,3},{1,2},{2,1},{3,0},{4,7},{5,6},{6,5},{7,4},{8,11},{9,10},{10,... | collective-permute-start | bytes 196616 | tf_op jit(solution)/shard_map/ppermute | solution.py:323
  10.2 0.6 %copy-done.6 = s32[2,1]{0,1:T(1,128)S(1)} copy-done((s32[2,1]{0,1:T(1,128)S(1)}, s32[2,1]{0,1:T(1,128)}, u32[]{:S(2)}) %copy-start.6) | copy-done | bytes 32
  10.8 1.2 %shard_map.79 = (f32[128,128]{1,0:T(8,128)S(1)}, f32[8,128]{1,0:T(8,128)S(1)}, f32[3,1024]{1,0:T(4,128)S(1)}) custom-call(s32[2,1024]{1,0:T(2,128)S(1)} %copy-done.3, s32[2,1024]{1,0:T(2,128)S(1)} %copy-done.4, f32[2,1024]{1,0:T(2,128)S(1)} %copy-done.5, s32[1,2]{1,0:T(1,128)S(1)} %bitcast.1, f32[32,512]{1,0:T(8,128)S(1)} %shard_map.78.refs_4_.refs_1_), custom_call_target="tpu_custom_call" | custom-call | flops 1400000000 | bytes 106504 | tf_op jit(solution)/shard_map/pallas_call | solution.py:93
  12.0 0.6 %shard_map.81 = (f32[128,512]{1,0:T(8,128)S(1)}, f32[128,512]{1,0:T(8,128)S(1)}) custom-call(f32[3,1024]{1,0:T(4,128)S(1)} %get-tuple-element.41.refs_0_.refs_2_), custom_call_target="tpu_custom_call" | custom-call | flops 900000000 | bytes 536576 | tf_op jit(solution)/shard_map/pallas_call | solution.py:93
  12.7 0.8 %shard_map.82 = (f32[40,512]{1,0:T(8,128)S(1)}, f32[40,512]{1,0:T(8,128)S(1)}, f32[64,1024]{1,0:T(8,128)S(1)}) custom-call(bf16[128,512]{1,0:T(8,128)(2,1)S(1)} %get-tuple-element.36.refs_1_.refs_0_, f32[128,512]{1,0:T(8,128)S(1)} %collective-permute-done.refs_1_, f32[8,128]{1,0:T(8,128)S(1)} %get-tuple-element.38.refs_2_, ...), custom_call_target="tpu_custom_call" | custom-call | flops 1000000000 | bytes 2527232 | tf_op jit(solution)/shard_map/pallas_call | solution.py:93
  13.5 0.6 %collective-permute-done.2.refs_0_ = f32[32,512]{1,0:T(8,128)S(1)} collective-permute-done((f32[32,512]{1,0:T(8,128)S(1)}, f32[32,512]{1,0:T(8,128)S(1)}, u32[]{:S(2)}, u32[]{:S(2)}) %collective-permute-start.2) | collective-permute-done | bytes 65568 | tf_op jit(solution)/shard_map/ppermute | solution.py:323
  14.2 0.8 %shard_map.83 = (f32[40,512]{1,0:T(8,128)S(1)}, f32[40,512]{1,0:T(8,128)S(1)}, f32[64,1024]{1,0:T(8,128)S(1)}) custom-call(f32[32,512]{1,0:T(8,128)S(1)} %collective-permute-done.2.refs_0_, f32[128,512]{1,0:T(8,128)S(1)} %collective-permute-done.3.refs_1_, f32[8,128]{1,0:T(8,128)S(1)} %get-tuple-element.38.refs_2_, ...), custom_call_target="tpu_custom_call" | custom-call | flops 1000000000 | bytes 2461696 | tf_op jit(solution)/shard_map/pallas_call | solution.py:93
  15.0 1.5 %collective-permute-start.4 = (f32[40,512]{1,0:T(8,128)S(1)}, f32[40,512]{1,0:T(8,128)S(1)}, u32[]{:S(2)}, u32[]{:S(2)}) collective-permute-start(f32[40,512]{1,0:T(8,128)S(1)} %get-tuple-element.46), channel_id=1, source_target_pairs={{0,3},{1,2},{2,1},{3,0},{4,7},{5,6},{6,5},{7,4},{8,11},{9,10},{10,... | collective-permute-start | bytes 245768 | tf_op jit(solution)/shard_map/ppermute | solution.py:323
  16.5 1.5 %collective-permute-start.5 = (f32[40,512]{1,0:T(8,128)S(1)}, f32[40,512]{1,0:T(8,128)S(1)}, u32[]{:S(2)}, u32[]{:S(2)}) collective-permute-start(f32[40,512]{1,0:T(8,128)S(1)} %get-tuple-element.47), channel_id=1, source_target_pairs={{0,2},{1,3},{2,0},{3,1},{4,6},{5,7},{6,4},{7,5},{8,10},{9,11},{10,... | collective-permute-start | bytes 245768 | tf_op jit(solution)/shard_map/ppermute | solution.py:323
  18.0 0.5 %collective-permute-start.6 = (f32[40,512]{1,0:T(8,128)S(1)}, f32[40,512]{1,0:T(8,128)S(1)}, u32[]{:S(2)}, u32[]{:S(2)}) collective-permute-start(f32[40,512]{1,0:T(8,128)S(1)} %get-tuple-element.48), channel_id=1, source_target_pairs={{0,1},{1,0},{2,3},{3,2},{4,5},{5,4},{6,7},{7,6},{8,9},{9,8},{10,11... | collective-permute-start | bytes 245768 | tf_op jit(solution)/shard_map/ppermute | solution.py:323
  18.6 0.6 %shard_map.84 = (f32[512,512]{1,0:T(8,128)S(1)}, bf16[512,512]{1,0:T(8,128)(2,1)S(1)}, bf16[512,512]{1,0:T(8,128)(2,1)S(1)}) custom-call(f32[64,1024]{1,0:T(8,128)S(1)} %get-tuple-element.45.refs_8_.refs_0_, f32[64,1024]{1,0:T(8,128)S(1)} %get-tuple-element.49.refs_1_, f32[512,512]{1,0:T(8,128)S(1)} %copy-done), custom_call_target="tpu_custom_call" | custom-call | flops 900000000 | bytes 3670016 | tf_op jit(solution)/shard_map/pallas_call | solution.py:93
  19.7 0.6 %shard_map.86 = (f32[128,512]{1,0:T(8,128)S(1)}, f32[128,512]{1,0:T(8,128)S(1)}) custom-call(f32[3,1024]{1,0:T(4,128)S(1)} %shard_map.85.refs_0_.refs_4_), custom_call_target="tpu_custom_call" | custom-call | flops 900000000 | bytes 536576 | tf_op jit(solution)/shard_map/pallas_call | solution.py:93
  20.3 0.6 %collective-permute-done.4.refs_1_.refs_5_ = f32[40,512]{1,0:T(8,128)S(1)} collective-permute-done((f32[40,512]{1,0:T(8,128)S(1)}, f32[40,512]{1,0:T(8,128)S(1)}, u32[]{:S(2)}, u32[]{:S(2)}) %collective-permute-start.4) | collective-permute-done | bytes 81952 | tf_op jit(solution)/shard_map/ppermute | solution.py:323
  20.9 1.4 %collective-permute-done.5.refs_2_.refs_6_ = f32[40,512]{1,0:T(8,128)S(1)} collective-permute-done((f32[40,512]{1,0:T(8,128)S(1)}, f32[40,512]{1,0:T(8,128)S(1)}, u32[]{:S(2)}, u32[]{:S(2)}) %collective-permute-start.5) | collective-permute-done | bytes 81952 | tf_op jit(solution)/shard_map/ppermute | solution.py:323
  22.9 1.4 %collective-permute-start.7 = (f32[32,512]{1,0:T(8,128)S(1)}, f32[32,512]{1,0:T(8,128)S(1)}, u32[]{:S(2)}, u32[]{:S(2)}) collective-permute-start(f32[32,512]{1,0:T(8,128)S(1)} %get-tuple-element.55), channel_id=1, source_target_pairs={{0,3},{1,2},{2,1},{3,0},{4,7},{5,6},{6,5},{7,4},{8,11},{9,10},{10,... | collective-permute-start | bytes 196616 | tf_op jit(solution)/shard_map/ppermute | solution.py:323
  24.3 0.6 %collective-permute-start.8 = (f32[32,512]{1,0:T(8,128)S(1)}, f32[32,512]{1,0:T(8,128)S(1)}, u32[]{:S(2)}, u32[]{:S(2)}) collective-permute-start(f32[32,512]{1,0:T(8,128)S(1)} %get-tuple-element.56), channel_id=1, source_target_pairs={{0,2},{1,3},{2,0},{3,1},{4,6},{5,7},{6,4},{7,5},{8,10},{9,11},{10,... | collective-permute-start | bytes 196616 | tf_op jit(solution)/shard_map/ppermute | solution.py:323
  24.9 1.5 %collective-permute-start.13 = (f32[32,512]{1,0:T(8,128)S(1)}, f32[32,512]{1,0:T(8,128)S(1)}, u32[]{:S(2)}, u32[]{:S(2)}) collective-permute-start(f32[32,512]{1,0:T(8,128)S(1)} %get-tuple-element.62), channel_id=1, source_target_pairs={{0,1},{1,0},{2,3},{3,2},{4,5},{5,4},{6,7},{7,6},{8,9},{9,8},{10,11... | collective-permute-start | bytes 196616 | tf_op jit(solution)/shard_map/ppermute | solution.py:323
  26.4 1.4 %shard_map.89 = (bf16[512,512]{1,0:T(8,128)(2,1)S(1)}, bf16[512,512]{1,0:T(8,128)(2,1)S(1)}) custom-call(f32[134,512]{1,0:T(8,128)S(1)} %collective-permute-done.9.refs_0_, f32[512,512]{1,0:T(8,128)S(1)} %collective-permute-done.10.refs_1_), custom_call_target="tpu_custom_call" | custom-call | flops 2000000000 | bytes 2371584 | tf_op jit(solution)/shard_map/pallas_call | solution.py:93
  27.9 0.6 %collective-permute-done.7.refs_1_.refs_3_ = f32[32,512]{1,0:T(8,128)S(1)} collective-permute-done((f32[32,512]{1,0:T(8,128)S(1)}, f32[32,512]{1,0:T(8,128)S(1)}, u32[]{:S(2)}, u32[]{:S(2)}) %collective-permute-start.7) | collective-permute-done | bytes 65568 | tf_op jit(solution)/shard_map/ppermute | solution.py:323
  28.4 0.7 %collective-permute-done.8.refs_2_ = f32[32,512]{1,0:T(8,128)S(1)} collective-permute-done((f32[32,512]{1,0:T(8,128)S(1)}, f32[32,512]{1,0:T(8,128)S(1)}, u32[]{:S(2)}, u32[]{:S(2)}) %collective-permute-start.8) | collective-permute-done | bytes 65568 | tf_op jit(solution)/shard_map/ppermute | solution.py:323
  29.2 0.7 %shard_map.90 = (f32[32,512]{1,0:T(8,128)S(1)}, f32[32,512]{1,0:T(8,128)S(1)}, f32[32,512]{1,0:T(8,128)S(1)}, f32[8,128]{1,0:T(8,128)S(1)}) custom-call(f32[32,512]{1,0:T(8,128)S(1)} %get-tuple-element.54.refs_0_, f32[32,512]{1,0:T(8,128)S(1)} %collective-permute-done.7.refs_1_.refs_3_, f32[32,512]{1,0:T(8,128)S(1)} %collective-permute-done.8.refs_2_, ...), custom_call_target="tpu_custom_call" | custom-call | flops 800000000 | bytes 1970176 | tf_op jit(solution)/shard_map/pallas_call | solution.py:93
  30.0 1.2 %collective-permute-start.15 = (f32[134,512]{1,0:T(8,128)S(1)}, f32[134,512]{1,0:T(8,128)S(1)}, u32[]{:S(2)}, u32[]{:S(2)}) collective-permute-start(f32[134,512]{1,0:T(8,128)S(1)} %shard_map.92), channel_id=1, source_target_pairs={{0,28},{1,29},{2,30},{3,31},{4,0},{5,1},{6,2},{7,3},{8,4},{9,5},{1... | collective-permute-start | bytes 823304 | tf_op jit(solution)/shard_map/ppermute | solution.py:323
  31.1 1.0 %collective-permute-start.11 = (f32[32,512]{1,0:T(8,128)S(1)}, f32[32,512]{1,0:T(8,128)S(1)}, u32[]{:S(2)}, u32[]{:S(2)}) collective-permute-start(f32[32,512]{1,0:T(8,128)S(1)} %get-tuple-element.60), channel_id=1, source_target_pairs={{0,3},{1,2},{2,1},{3,0},{4,7},{5,6},{6,5},{7,4},{8,11},{9,10},{10,... | collective-permute-start | bytes 196616 | tf_op jit(solution)/shard_map/ppermute | solution.py:323
  32.1 1.1 %collective-permute-start.12 = (f32[32,512]{1,0:T(8,128)S(1)}, f32[32,512]{1,0:T(8,128)S(1)}, u32[]{:S(2)}, u32[]{:S(2)}) collective-permute-start(f32[32,512]{1,0:T(8,128)S(1)} %get-tuple-element.61), channel_id=1, source_target_pairs={{0,2},{1,3},{2,0},{3,1},{4,6},{5,7},{6,4},{7,5},{8,10},{9,11},{10,... | collective-permute-start | bytes 196616 | tf_op jit(solution)/shard_map/ppermute | solution.py:323
  33.2 0.7 %shard_map.91 = (f32[32,512]{1,0:T(8,128)S(1)}, f32[8,128]{1,0:T(8,128)}) custom-call(f32[32,512]{1,0:T(8,128)S(1)} %collective-permute-done.13.refs_0_.refs_1_, bf16[512,512]{1,0:T(8,128)(2,1)S(1)} %get-tuple-element.57.refs_3_.refs_1_, bf16[512,512]{1,0:T(8,128)(2,1)S(1)} %get-tuple-element.58.refs_4_.refs_2_, ...), custom_call_target="tpu_custom_call" | custom-call | flops 800000000 | bytes 1708032 | tf_op jit(solution)/shard_map/pallas_call | solution.py:93
  33.8 1.5 %collective-permute-start.14 = (f32[32,512]{1,0:T(8,128)S(1)}, f32[32,512]{1,0:T(8,128)S(1)}, u32[]{:S(2)}, u32[]{:S(2)}) collective-permute-start(f32[32,512]{1,0:T(8,128)S(1)} %get-tuple-element.64.refs_4_), channel_id=1, source_target_pairs={{0,1},{1,0},{2,3},{3,2},{4,5},{5,4},{6,7},{7,6},{8,9},{9,8},{10,11... | collective-permute-start | bytes 196616 | tf_op jit(solution)/shard_map/ppermute | solution.py:323
  35.3 2.1 %shard_map.93 = (f32[512,512]{1,0:T(8,128)}, f32[8,128]{1,0:T(8,128)S(1)}) custom-call(f32[134,512]{1,0:T(8,128)S(1)} %collective-permute-done.15.refs_0_, f32[512,512]{1,0:T(8,128)S(1)} %get-tuple-element.50.refs_5_.refs_1_, bf16[512,512]{1,0:T(8,128)(2,1)S(1)} %get-tuple-element.66.refs_2_, bf16[512,512]{1,0:T(8,128)(2,1)S(1)} %get-tuple-element.67.refs_3_, ...), custom_call_target="tpu_custom_call" | custom-call | flops 2500000000 | bytes 3424256 | tf_op jit(solution)/shard_map/pallas_call | solution.py:93
  37.5 0.7 %collective-permute-done.14.refs_3_ = f32[32,512]{1,0:T(8,128)S(1)} collective-permute-done((f32[32,512]{1,0:T(8,128)S(1)}, f32[32,512]{1,0:T(8,128)S(1)}, u32[]{:S(2)}, u32[]{:S(2)}) %collective-permute-start.14) | collective-permute-done | bytes 65568 | tf_op jit(solution)/shard_map/ppermute | solution.py:323
  38.1 0.9 %shard_map.94 = f32[128,512]{1,0:T(8,128)} custom-call(f32[32,512]{1,0:T(8,128)S(1)} %get-tuple-element.59.refs_5_.refs_0_, f32[32,512]{1,0:T(8,128)S(1)} %collective-permute-done.11.refs_1_, f32[32,512]{1,0:T(8,128)S(1)} %collective-permute-done.12.refs_2_, f32[32,512]{1,0:T(8,128)S(1)} %collective-permute-done.14.refs_3_, ...), custom_call_target="tpu_custom_call" | custom-call | flops 1200000000 | bytes 1114112 | tf_op jit(solution)/shard_map/pallas_call | solution.py:93
  (32 shorter events, 2.2 us)
Async XLA Ops:
  0.6 5.8 %collective-permute-start.1 = (s32[2,1024]{1,0:T(2,128)}, s32[2,1024]{1,0:T(2,128)S(1)}, u32[]{:S(2)}, u32[]{:S(2)}) collective-permute-start(s32[2,1024]{1,0:T(2,128)} %refs_0_.7), channel_id=1, source_target_pairs={{0,3},{1,2},{2,1},{3,0},{4,7},{5,6},{6,5},{7,4},{8,11},{9,10},{10,... | collective-permute-start | bytes 24584 | tf_op jit(solution)/shard_map/ppermute | solution.py:323
  4.6 8.1 %collective-permute-start = (f32[128,512]{1,0:T(8,128)}, f32[128,512]{1,0:T(8,128)S(1)}, u32[]{:S(2)}, u32[]{:S(2)}) collective-permute-start(f32[128,512]{1,0:T(8,128)} %refs_4_.1), channel_id=1, source_target_pairs={{0,1},{1,0},{2,3},{3,2},{4,5},{5,4},{6,7},{7,6},{8,9},{9,8},{10,11... | collective-permute-start | bytes 786440 | tf_op jit(solution)/shard_map/ppermute | solution.py:323
  5.1 9.1 %collective-permute-start.3 = (f32[128,512]{1,0:T(8,128)}, f32[128,512]{1,0:T(8,128)S(1)}, u32[]{:S(2)}, u32[]{:S(2)}) collective-permute-start(f32[128,512]{1,0:T(8,128)} %refs_4_.1), channel_id=1, source_target_pairs={{0,2},{1,3},{2,0},{3,1},{4,6},{5,7},{6,4},{7,5},{8,10},{9,11},{10,... | collective-permute-start | bytes 786440 | tf_op jit(solution)/shard_map/ppermute | solution.py:323
  5.2 21.2 %collective-permute-start.10 = (f32[512,512]{1,0:T(8,128)}, f32[512,512]{1,0:T(8,128)S(1)}, u32[]{:S(2)}, u32[]{:S(2)}) collective-permute-start(f32[512,512]{1,0:T(8,128)} %refs_2_.4), channel_id=1, source_target_pairs={{0,4},{1,5},{2,6},{3,7},{4,8},{5,9},{6,10},{7,11},{8,12},{9,13},{1... | collective-permute-start | bytes 3145736 | tf_op jit(solution)/shard_map/ppermute | solution.py:323
  5.2 1.0 %copy-start.1 = (f32[128,512]{1,0:T(8,128)S(1)}, f32[128,512]{1,0:T(8,128)}, u32[]{:S(2)}) copy-start(f32[128,512]{1,0:T(8,128)} %refs_4_.1) | copy-start | bytes 786436
  6.4 3.6 %copy-start = (f32[512,512]{1,0:T(8,128)S(1)}, f32[512,512]{1,0:T(8,128)}, u32[]{:S(2)}) copy-start(f32[512,512]{1,0:T(8,128)} %refs_2_.4) | copy-start | bytes 3145732
  6.9 3.3 %copy-start.3 = (s32[2,1024]{1,0:T(2,128)S(1)}, s32[2,1024]{1,0:T(2,128)}, u32[]{:S(2)}) copy-start(s32[2,1024]{1,0:T(2,128)} %refs_0_.7) | copy-start | bytes 24580
  6.9 3.3 %copy-start.4 = (s32[2,1024]{1,0:T(2,128)S(1)}, s32[2,1024]{1,0:T(2,128)}, u32[]{:S(2)}) copy-start(s32[2,1024]{1,0:T(2,128)} %refs_1_.3) | copy-start | bytes 24580
  6.9 3.3 %copy-start.5 = (f32[2,1024]{1,0:T(2,128)S(1)}, f32[2,1024]{1,0:T(2,128)}, u32[]{:S(2)}) copy-start(f32[2,1024]{1,0:T(2,128)} %refs_2_.5) | copy-start | bytes 24580
  6.9 7.1 %collective-permute-start.2 = (f32[32,512]{1,0:T(8,128)S(1)}, f32[32,512]{1,0:T(8,128)S(1)}, u32[]{:S(2)}, u32[]{:S(2)}) collective-permute-start(f32[32,512]{1,0:T(8,128)S(1)} %shard_map.78.refs_4_.refs_1_), channel_id=1, source_target_pairs={{0,3},{1,2},{2,1},{3,0},{4,7},{5,6},{6,5},{7,4},{8,11},{9,10},{10,... | collective-permute-start | bytes 196616 | tf_op jit(solution)/shard_map/ppermute | solution.py:323
  10.2 0.7 %copy-start.6 = (s32[2,1]{0,1:T(1,128)S(1)}, s32[2,1]{0,1:T(1,128)}, u32[]{:S(2)}) copy-start(s32[2,1]{0,1:T(1,128)} %param.11) | copy-start | bytes 28
  15.0 5.9 %collective-permute-start.4 = (f32[40,512]{1,0:T(8,128)S(1)}, f32[40,512]{1,0:T(8,128)S(1)}, u32[]{:S(2)}, u32[]{:S(2)}) collective-permute-start(f32[40,512]{1,0:T(8,128)S(1)} %get-tuple-element.46), channel_id=1, source_target_pairs={{0,3},{1,2},{2,1},{3,0},{4,7},{5,6},{6,5},{7,4},{8,11},{9,10},{10,... | collective-permute-start | bytes 245768 | tf_op jit(solution)/shard_map/ppermute | solution.py:323
  16.5 5.9 %collective-permute-start.5 = (f32[40,512]{1,0:T(8,128)S(1)}, f32[40,512]{1,0:T(8,128)S(1)}, u32[]{:S(2)}, u32[]{:S(2)}) collective-permute-start(f32[40,512]{1,0:T(8,128)S(1)} %get-tuple-element.47), channel_id=1, source_target_pairs={{0,2},{1,3},{2,0},{3,1},{4,6},{5,7},{6,4},{7,5},{8,10},{9,11},{10,... | collective-permute-start | bytes 245768 | tf_op jit(solution)/shard_map/ppermute | solution.py:323
  18.0 4.4 %collective-permute-start.6 = (f32[40,512]{1,0:T(8,128)S(1)}, f32[40,512]{1,0:T(8,128)S(1)}, u32[]{:S(2)}, u32[]{:S(2)}) collective-permute-start(f32[40,512]{1,0:T(8,128)S(1)} %get-tuple-element.48), channel_id=1, source_target_pairs={{0,1},{1,0},{2,3},{3,2},{4,5},{5,4},{6,7},{7,6},{8,9},{9,8},{10,11... | collective-permute-start | bytes 245768 | tf_op jit(solution)/shard_map/ppermute | solution.py:323
  18.6 7.9 %collective-permute-start.9 = (f32[134,512]{1,0:T(8,128)S(1)}, f32[134,512]{1,0:T(8,128)S(1)}, u32[]{:S(2)}, u32[]{:S(2)}) collective-permute-start(f32[134,512]{1,0:T(8,128)S(1)} %shard_map.88), channel_id=1, source_target_pairs={{0,4},{1,5},{2,6},{3,7},{4,8},{5,9},{6,10},{7,11},{8,12},{9,13},{1... | collective-permute-start | bytes 823304 | tf_op jit(solution)/shard_map/ppermute | solution.py:323
  19.7 2.8 %copy-start.2 = (f32[128,512]{1,0:T(8,128)S(1)}, f32[128,512]{1,0:T(8,128)}, u32[]{:S(2)}) copy-start(f32[128,512]{1,0:T(8,128)} %refs_4_.1) | copy-start | bytes 786436
  22.9 5.6 %collective-permute-start.7 = (f32[32,512]{1,0:T(8,128)S(1)}, f32[32,512]{1,0:T(8,128)S(1)}, u32[]{:S(2)}, u32[]{:S(2)}) collective-permute-start(f32[32,512]{1,0:T(8,128)S(1)} %get-tuple-element.55), channel_id=1, source_target_pairs={{0,3},{1,2},{2,1},{3,0},{4,7},{5,6},{6,5},{7,4},{8,11},{9,10},{10,... | collective-permute-start | bytes 196616 | tf_op jit(solution)/shard_map/ppermute | solution.py:323
  24.3 4.9 %collective-permute-start.8 = (f32[32,512]{1,0:T(8,128)S(1)}, f32[32,512]{1,0:T(8,128)S(1)}, u32[]{:S(2)}, u32[]{:S(2)}) collective-permute-start(f32[32,512]{1,0:T(8,128)S(1)} %get-tuple-element.56), channel_id=1, source_target_pairs={{0,2},{1,3},{2,0},{3,1},{4,6},{5,7},{6,4},{7,5},{8,10},{9,11},{10,... | collective-permute-start | bytes 196616 | tf_op jit(solution)/shard_map/ppermute | solution.py:323
  24.9 5.0 %collective-permute-start.13 = (f32[32,512]{1,0:T(8,128)S(1)}, f32[32,512]{1,0:T(8,128)S(1)}, u32[]{:S(2)}, u32[]{:S(2)}) collective-permute-start(f32[32,512]{1,0:T(8,128)S(1)} %get-tuple-element.62), channel_id=1, source_target_pairs={{0,1},{1,0},{2,3},{3,2},{4,5},{5,4},{6,7},{7,6},{8,9},{9,8},{10,11... | collective-permute-start | bytes 196616 | tf_op jit(solution)/shard_map/ppermute | solution.py:323
  30.0 5.4 %collective-permute-start.15 = (f32[134,512]{1,0:T(8,128)S(1)}, f32[134,512]{1,0:T(8,128)S(1)}, u32[]{:S(2)}, u32[]{:S(2)}) collective-permute-start(f32[134,512]{1,0:T(8,128)S(1)} %shard_map.92), channel_id=1, source_target_pairs={{0,28},{1,29},{2,30},{3,31},{4,0},{5,1},{6,2},{7,3},{8,4},{9,5},{1... | collective-permute-start | bytes 823304 | tf_op jit(solution)/shard_map/ppermute | solution.py:323
  31.1 6.3 %collective-permute-start.11 = (f32[32,512]{1,0:T(8,128)S(1)}, f32[32,512]{1,0:T(8,128)S(1)}, u32[]{:S(2)}, u32[]{:S(2)}) collective-permute-start(f32[32,512]{1,0:T(8,128)S(1)} %get-tuple-element.60), channel_id=1, source_target_pairs={{0,3},{1,2},{2,1},{3,0},{4,7},{5,6},{6,5},{7,4},{8,11},{9,10},{10,... | collective-permute-start | bytes 196616 | tf_op jit(solution)/shard_map/ppermute | solution.py:323
  32.1 5.4 %collective-permute-start.12 = (f32[32,512]{1,0:T(8,128)S(1)}, f32[32,512]{1,0:T(8,128)S(1)}, u32[]{:S(2)}, u32[]{:S(2)}) collective-permute-start(f32[32,512]{1,0:T(8,128)S(1)} %get-tuple-element.61), channel_id=1, source_target_pairs={{0,2},{1,3},{2,0},{3,1},{4,6},{5,7},{6,4},{7,5},{8,10},{9,11},{10,... | collective-permute-start | bytes 196616 | tf_op jit(solution)/shard_map/ppermute | solution.py:323
  33.8 4.3 %collective-permute-start.14 = (f32[32,512]{1,0:T(8,128)S(1)}, f32[32,512]{1,0:T(8,128)S(1)}, u32[]{:S(2)}, u32[]{:S(2)}) collective-permute-start(f32[32,512]{1,0:T(8,128)S(1)} %get-tuple-element.64.refs_4_), channel_id=1, source_target_pairs={{0,1},{1,0},{2,3},{3,2},{4,5},{5,4},{6,7},{7,6},{8,9},{9,8},{10,11... | collective-permute-start | bytes 196616 | tf_op jit(solution)/shard_map/ppermute | solution.py:323

commit v6 on v5

--- a/solution.py
+++ b/solution.py
@@ -10,7 +10,7 @@
 TOUCHED = 32
 WHOLE = (0, 1, 2)
 
-HOME_CHUNKS = 4
+HOME_CHUNKS = 2
 FLOPS = dict(
     split=8 * 10**7, first=10**11, pack=14 * 10**8, prep0=9 * 10**8, block=2 * 10**8, tile0=10**9, tile1=8 * 10**8,
     items=9 * 10**8, pack1=5 * 10**8, prep1=9 * 10**8, stack=0, next=2 * 10**9, owner=6 * 10**9, join=0,
@@ -36,13 +36,6 @@
     return hi, (x - hi.astype(F32)).astype(BF16)
 
 
-def split3(x):
-    hi = x.astype(BF16)
-    rest = x - hi.astype(F32)
-    mid = rest.astype(BF16)
-    return hi, mid, (rest - mid.astype(F32)).astype(BF16)
-
-
 def pick(selector, x, dims):
     over = dims[0][0][0]
     return dot(jnp.concatenate([selector, selector], axis=over), jnp.concatenate(split2(x), axis=0), dims)
@@ -53,17 +46,7 @@
 
 
 def one_hot(names, rows):
-    blocks = []
-    for low in range(0, rows, 256):
-        size = min(256, rows - low)
-        local = jnp.clip(names - low, -1, 256).astype(F32).astype(BF16)
-        row = iota((size, LANES), 0).astype(F32).astype(BF16)
-        one, zero = jnp.ones((size, LANES), BF16), jnp.zeros((size, LANES), BF16)
-        parts = [
-            jnp.where(row == local[:, at : at + LANES], one, zero) for at in range(0, names.shape[1], LANES)
-        ]
-        blocks.append(jnp.concatenate(parts, axis=1))
-    return jnp.concatenate(blocks, axis=0)
+    return (iota((rows, names.shape[1]), 0) == names).astype(F32).astype(BF16)
 
 
 def touched_by(names):
@@ -166,8 +149,8 @@
         jnp.concatenate([entry_ref[at : at + 1, :] for at in range(low + f * per, low + (f + 1) * per)], axis=1)
         for f in range(FIELDS)
     ]
-    hot = one_hot(fields[0].astype(jnp.int32), touched)
-    left = [hot] + [hot * value for value in split2(fields[2])]
+    hot = (iota((touched, entry_ref.shape[1] * per), 0) == fields[0].astype(jnp.int32)).astype(F32)
+    left = [hot.astype(BF16)] + [(hot * value.astype(F32)).astype(BF16) for value in split2(fields[2])]
     table = dot(jnp.concatenate(left, axis=0), one_hot(fields[1].astype(jnp.int32), items), NT)
     return table[:touched], table[touched : 2 * touched] + table[2 * touched :]
 

time: 39.2 us -> 39.2 us (level)
  no operation moved by 1% of the time
where the time goes in v6:
time: 39.2 us; the launch traced here: 39.1 us
  starting transfers between devices  19.5 us (50%)
  Pallas kernels  12 us (31%)
  waiting for transfers between devices  4.99 us (13%)
  local copies, waits for them, and re-layouts  1.64 us (4%)
  between operations  0.85 us (2%)
    ppermute x16, starting transfers between devices, exchange(): return lax.ppermute(value, ('rows', 'strata'), pairs)  19.5 us
    pallas_call x18, Pallas kernels, call(): pl.pallas_call(body, out_shape=list(outs), in_specs=[pl.BlockSpec(memory_...  12 us
    ppermute x16, waiting for transfers between devices, exchange(): return lax.ppermute(value, ('rows', 'strata'), pairs)  4.99 us
    unnamed x14, local copies, waits for them, and re-layouts  1.64 us
  transfers between devices with their start and end apart: 16, of which 9 were waited for; matrix products, arithmetic and copies ran while one was open for 0% of the time, Pallas kernels for 28%

profile of v6, /device:TPU:0, one launch (start us, length us, event | category | flops | bytes accessed | tf_op | source)
XLA Modules:
  0.0 39.1 jit_solution(14660687726846824057)
XLA Ops:
  0.6 4.0 %collective-permute-start.1 = (s32[2,1024]{1,0:T(2,128)}, s32[2,1024]{1,0:T(2,128)S(1)}, u32[]{:S(2)}, u32[]{:S(2)}) collective-permute-start(s32[2,1024]{1,0:T(2,128)} %refs_0_.7), channel_id=1, source_target_pairs={{0,3},{1,2},{2,1},{3,0},{4,7},{5,6},{6,5},{7,4},{8,11},{9,10},{10,... | collective-permute-start | bytes 24584 | tf_op jit(solution)/shard_map/ppermute | solution.py:306
  4.6 0.5 %collective-permute-start = (f32[128,512]{1,0:T(8,128)}, f32[128,512]{1,0:T(8,128)S(1)}, u32[]{:S(2)}, u32[]{:S(2)}) collective-permute-start(f32[128,512]{1,0:T(8,128)} %refs_4_.1), channel_id=1, source_target_pairs={{0,1},{1,0},{2,3},{3,2},{4,5},{5,4},{6,7},{7,6},{8,9},{9,8},{10,11... | collective-permute-start | bytes 786440 | tf_op jit(solution)/shard_map/ppermute | solution.py:306
  5.2 1.0 %copy-done.1 = f32[128,512]{1,0:T(8,128)S(1)} copy-done((f32[128,512]{1,0:T(8,128)S(1)}, f32[128,512]{1,0:T(8,128)}, u32[]{:S(2)}) %copy-start.1) | copy-done | bytes 262168
  6.9 3.1 %collective-permute-start.2 = (f32[32,512]{1,0:T(8,128)S(1)}, f32[32,512]{1,0:T(8,128)S(1)}, u32[]{:S(2)}, u32[]{:S(2)}) collective-permute-start(f32[32,512]{1,0:T(8,128)S(1)} %shard_map.78.refs_4_.refs_1_), channel_id=1, source_target_pairs={{0,3},{1,2},{2,1},{3,0},{4,7},{5,6},{6,5},{7,4},{8,11},{9,10},{10,... | collective-permute-start | bytes 196616 | tf_op jit(solution)/shard_map/ppermute | solution.py:306
  10.2 0.6 %copy-done.6 = s32[2,1]{0,1:T(1,128)S(1)} copy-done((s32[2,1]{0,1:T(1,128)S(1)}, s32[2,1]{0,1:T(1,128)}, u32[]{:S(2)}) %copy-start.6) | copy-done | bytes 32
  10.8 1.2 %shard_map.79 = (f32[128,128]{1,0:T(8,128)S(1)}, f32[8,128]{1,0:T(8,128)S(1)}, f32[3,1024]{1,0:T(4,128)S(1)}) custom-call(s32[2,1024]{1,0:T(2,128)S(1)} %copy-done.3, s32[2,1024]{1,0:T(2,128)S(1)} %copy-done.4, f32[2,1024]{1,0:T(2,128)S(1)} %copy-done.5, s32[1,2]{1,0:T(1,128)S(1)} %bitcast.1, f32[32,512]{1,0:T(8,128)S(1)} %shard_map.78.refs_4_.refs_1_), custom_call_target="tpu_custom_call" | custom-call | flops 1400000000 | bytes 106504 | tf_op jit(solution)/shard_map/pallas_call | solution.py:76
  12.0 0.6 %shard_map.81 = (f32[128,512]{1,0:T(8,128)S(1)}, f32[128,512]{1,0:T(8,128)S(1)}) custom-call(f32[3,1024]{1,0:T(4,128)S(1)} %get-tuple-element.41.refs_0_.refs_2_), custom_call_target="tpu_custom_call" | custom-call | flops 900000000 | bytes 536576 | tf_op jit(solution)/shard_map/pallas_call | solution.py:76
  12.6 0.8 %shard_map.82 = (f32[40,512]{1,0:T(8,128)S(1)}, f32[40,512]{1,0:T(8,128)S(1)}, f32[64,1024]{1,0:T(8,128)S(1)}) custom-call(bf16[128,512]{1,0:T(8,128)(2,1)S(1)} %get-tuple-element.36.refs_1_.refs_0_, f32[128,512]{1,0:T(8,128)S(1)} %collective-permute-done.refs_1_, f32[8,128]{1,0:T(8,128)S(1)} %get-tuple-element.38.refs_2_, ...), custom_call_target="tpu_custom_call" | custom-call | flops 1000000000 | bytes 2527232 | tf_op jit(solution)/shard_map/pallas_call | solution.py:76
  13.5 0.6 %collective-permute-done.2.refs_0_ = f32[32,512]{1,0:T(8,128)S(1)} collective-permute-done((f32[32,512]{1,0:T(8,128)S(1)}, f32[32,512]{1,0:T(8,128)S(1)}, u32[]{:S(2)}, u32[]{:S(2)}) %collective-permute-start.2) | collective-permute-done | bytes 65568 | tf_op jit(solution)/shard_map/ppermute | solution.py:306
  14.2 0.8 %shard_map.83 = (f32[40,512]{1,0:T(8,128)S(1)}, f32[40,512]{1,0:T(8,128)S(1)}, f32[64,1024]{1,0:T(8,128)S(1)}) custom-call(f32[32,512]{1,0:T(8,128)S(1)} %collective-permute-done.2.refs_0_, f32[128,512]{1,0:T(8,128)S(1)} %collective-permute-done.3.refs_1_, f32[8,128]{1,0:T(8,128)S(1)} %get-tuple-element.38.refs_2_, ...), custom_call_target="tpu_custom_call" | custom-call | flops 1000000000 | bytes 2461696 | tf_op jit(solution)/shard_map/pallas_call | solution.py:76
  15.0 1.5 %collective-permute-start.4 = (f32[40,512]{1,0:T(8,128)S(1)}, f32[40,512]{1,0:T(8,128)S(1)}, u32[]{:S(2)}, u32[]{:S(2)}) collective-permute-start(f32[40,512]{1,0:T(8,128)S(1)} %get-tuple-element.46), channel_id=1, source_target_pairs={{0,3},{1,2},{2,1},{3,0},{4,7},{5,6},{6,5},{7,4},{8,11},{9,10},{10,... | collective-permute-start | bytes 245768 | tf_op jit(solution)/shard_map/ppermute | solution.py:306
  16.5 1.5 %collective-permute-start.5 = (f32[40,512]{1,0:T(8,128)S(1)}, f32[40,512]{1,0:T(8,128)S(1)}, u32[]{:S(2)}, u32[]{:S(2)}) collective-permute-start(f32[40,512]{1,0:T(8,128)S(1)} %get-tuple-element.47), channel_id=1, source_target_pairs={{0,2},{1,3},{2,0},{3,1},{4,6},{5,7},{6,4},{7,5},{8,10},{9,11},{10,... | collective-permute-start | bytes 245768 | tf_op jit(solution)/shard_map/ppermute | solution.py:306
  18.0 0.5 %collective-permute-start.6 = (f32[40,512]{1,0:T(8,128)S(1)}, f32[40,512]{1,0:T(8,128)S(1)}, u32[]{:S(2)}, u32[]{:S(2)}) collective-permute-start(f32[40,512]{1,0:T(8,128)S(1)} %get-tuple-element.48), channel_id=1, source_target_pairs={{0,1},{1,0},{2,3},{3,2},{4,5},{5,4},{6,7},{7,6},{8,9},{9,8},{10,11... | collective-permute-start | bytes 245768 | tf_op jit(solution)/shard_map/ppermute | solution.py:306
  18.6 0.6 %shard_map.84 = (f32[512,512]{1,0:T(8,128)S(1)}, bf16[512,512]{1,0:T(8,128)(2,1)S(1)}, bf16[512,512]{1,0:T(8,128)(2,1)S(1)}) custom-call(f32[64,1024]{1,0:T(8,128)S(1)} %get-tuple-element.45.refs_8_.refs_0_, f32[64,1024]{1,0:T(8,128)S(1)} %get-tuple-element.49.refs_1_, f32[512,512]{1,0:T(8,128)S(1)} %copy-done), custom_call_target="tpu_custom_call" | custom-call | flops 900000000 | bytes 3670016 | tf_op jit(solution)/shard_map/pallas_call | solution.py:76
  19.7 0.6 %shard_map.86 = (f32[128,512]{1,0:T(8,128)S(1)}, f32[128,512]{1,0:T(8,128)S(1)}) custom-call(f32[3,1024]{1,0:T(4,128)S(1)} %shard_map.85.refs_0_.refs_4_), custom_call_target="tpu_custom_call" | custom-call | flops 900000000 | bytes 536576 | tf_op jit(solution)/shard_map/pallas_call | solution.py:76
  20.3 0.6 %collective-permute-done.4.refs_1_.refs_5_ = f32[40,512]{1,0:T(8,128)S(1)} collective-permute-done((f32[40,512]{1,0:T(8,128)S(1)}, f32[40,512]{1,0:T(8,128)S(1)}, u32[]{:S(2)}, u32[]{:S(2)}) %collective-permute-start.4) | collective-permute-done | bytes 81952 | tf_op jit(solution)/shard_map/ppermute | solution.py:306
  20.9 1.4 %collective-permute-done.5.refs_2_.refs_6_ = f32[40,512]{1,0:T(8,128)S(1)} collective-permute-done((f32[40,512]{1,0:T(8,128)S(1)}, f32[40,512]{1,0:T(8,128)S(1)}, u32[]{:S(2)}, u32[]{:S(2)}) %collective-permute-start.5) | collective-permute-done | bytes 81952 | tf_op jit(solution)/shard_map/ppermute | solution.py:306
  22.9 1.4 %collective-permute-start.7 = (f32[32,512]{1,0:T(8,128)S(1)}, f32[32,512]{1,0:T(8,128)S(1)}, u32[]{:S(2)}, u32[]{:S(2)}) collective-permute-start(f32[32,512]{1,0:T(8,128)S(1)} %get-tuple-element.55), channel_id=1, source_target_pairs={{0,3},{1,2},{2,1},{3,0},{4,7},{5,6},{6,5},{7,4},{8,11},{9,10},{10,... | collective-permute-start | bytes 196616 | tf_op jit(solution)/shard_map/ppermute | solution.py:306
  24.3 0.6 %collective-permute-start.8 = (f32[32,512]{1,0:T(8,128)S(1)}, f32[32,512]{1,0:T(8,128)S(1)}, u32[]{:S(2)}, u32[]{:S(2)}) collective-permute-start(f32[32,512]{1,0:T(8,128)S(1)} %get-tuple-element.56), channel_id=1, source_target_pairs={{0,2},{1,3},{2,0},{3,1},{4,6},{5,7},{6,4},{7,5},{8,10},{9,11},{10,... | collective-permute-start | bytes 196616 | tf_op jit(solution)/shard_map/ppermute | solution.py:306
  24.9 1.5 %collective-permute-start.13 = (f32[32,512]{1,0:T(8,128)S(1)}, f32[32,512]{1,0:T(8,128)S(1)}, u32[]{:S(2)}, u32[]{:S(2)}) collective-permute-start(f32[32,512]{1,0:T(8,128)S(1)} %get-tuple-element.62), channel_id=1, source_target_pairs={{0,1},{1,0},{2,3},{3,2},{4,5},{5,4},{6,7},{7,6},{8,9},{9,8},{10,11... | collective-permute-start | bytes 196616 | tf_op jit(solution)/shard_map/ppermute | solution.py:306
  26.4 1.5 %shard_map.89 = (bf16[512,512]{1,0:T(8,128)(2,1)S(1)}, bf16[512,512]{1,0:T(8,128)(2,1)S(1)}) custom-call(f32[134,512]{1,0:T(8,128)S(1)} %collective-permute-done.9.refs_0_, f32[512,512]{1,0:T(8,128)S(1)} %collective-permute-done.10.refs_1_), custom_call_target="tpu_custom_call" | custom-call | flops 2000000000 | bytes 2371584 | tf_op jit(solution)/shard_map/pallas_call | solution.py:76
  27.9 0.6 %collective-permute-done.7.refs_1_.refs_3_ = f32[32,512]{1,0:T(8,128)S(1)} collective-permute-done((f32[32,512]{1,0:T(8,128)S(1)}, f32[32,512]{1,0:T(8,128)S(1)}, u32[]{:S(2)}, u32[]{:S(2)}) %collective-permute-start.7) | collective-permute-done | bytes 65568 | tf_op jit(solution)/shard_map/ppermute | solution.py:306
  28.4 0.7 %collective-permute-done.8.refs_2_ = f32[32,512]{1,0:T(8,128)S(1)} collective-permute-done((f32[32,512]{1,0:T(8,128)S(1)}, f32[32,512]{1,0:T(8,128)S(1)}, u32[]{:S(2)}, u32[]{:S(2)}) %collective-permute-start.8) | collective-permute-done | bytes 65568 | tf_op jit(solution)/shard_map/ppermute | solution.py:306
  29.2 0.8 %shard_map.90 = (f32[32,512]{1,0:T(8,128)S(1)}, f32[32,512]{1,0:T(8,128)S(1)}, f32[32,512]{1,0:T(8,128)S(1)}, f32[8,128]{1,0:T(8,128)S(1)}) custom-call(f32[32,512]{1,0:T(8,128)S(1)} %get-tuple-element.54.refs_0_, f32[32,512]{1,0:T(8,128)S(1)} %collective-permute-done.7.refs_1_.refs_3_, f32[32,512]{1,0:T(8,128)S(1)} %collective-permute-done.8.refs_2_, ...), custom_call_target="tpu_custom_call" | custom-call | flops 800000000 | bytes 1970176 | tf_op jit(solution)/shard_map/pallas_call | solution.py:76
  30.0 1.1 %collective-permute-start.15 = (f32[134,512]{1,0:T(8,128)S(1)}, f32[134,512]{1,0:T(8,128)S(1)}, u32[]{:S(2)}, u32[]{:S(2)}) collective-permute-start(f32[134,512]{1,0:T(8,128)S(1)} %shard_map.92), channel_id=1, source_target_pairs={{0,28},{1,29},{2,30},{3,31},{4,0},{5,1},{6,2},{7,3},{8,4},{9,5},{1... | collective-permute-start | bytes 823304 | tf_op jit(solution)/shard_map/ppermute | solution.py:306
  31.1 1.0 %collective-permute-start.11 = (f32[32,512]{1,0:T(8,128)S(1)}, f32[32,512]{1,0:T(8,128)S(1)}, u32[]{:S(2)}, u32[]{:S(2)}) collective-permute-start(f32[32,512]{1,0:T(8,128)S(1)} %get-tuple-element.60), channel_id=1, source_target_pairs={{0,3},{1,2},{2,1},{3,0},{4,7},{5,6},{6,5},{7,4},{8,11},{9,10},{10,... | collective-permute-start | bytes 196616 | tf_op jit(solution)/shard_map/ppermute | solution.py:306
  32.1 1.1 %collective-permute-start.12 = (f32[32,512]{1,0:T(8,128)S(1)}, f32[32,512]{1,0:T(8,128)S(1)}, u32[]{:S(2)}, u32[]{:S(2)}) collective-permute-start(f32[32,512]{1,0:T(8,128)S(1)} %get-tuple-element.61), channel_id=1, source_target_pairs={{0,2},{1,3},{2,0},{3,1},{4,6},{5,7},{6,4},{7,5},{8,10},{9,11},{10,... | collective-permute-start | bytes 196616 | tf_op jit(solution)/shard_map/ppermute | solution.py:306
  33.2 0.7 %shard_map.91 = (f32[32,512]{1,0:T(8,128)S(1)}, f32[8,128]{1,0:T(8,128)}) custom-call(f32[32,512]{1,0:T(8,128)S(1)} %collective-permute-done.13.refs_0_.refs_1_, bf16[512,512]{1,0:T(8,128)(2,1)S(1)} %get-tuple-element.57.refs_3_.refs_1_, bf16[512,512]{1,0:T(8,128)(2,1)S(1)} %get-tuple-element.58.refs_4_.refs_2_, ...), custom_call_target="tpu_custom_call" | custom-call | flops 800000000 | bytes 1708032 | tf_op jit(solution)/shard_map/pallas_call | solution.py:76
  33.8 1.5 %collective-permute-start.14 = (f32[32,512]{1,0:T(8,128)S(1)}, f32[32,512]{1,0:T(8,128)S(1)}, u32[]{:S(2)}, u32[]{:S(2)}) collective-permute-start(f32[32,512]{1,0:T(8,128)S(1)} %get-tuple-element.64.refs_4_), channel_id=1, source_target_pairs={{0,1},{1,0},{2,3},{3,2},{4,5},{5,4},{6,7},{7,6},{8,9},{9,8},{10,11... | collective-permute-start | bytes 196616 | tf_op jit(solution)/shard_map/ppermute | solution.py:306
  35.3 2.2 %shard_map.93 = (f32[512,512]{1,0:T(8,128)}, f32[8,128]{1,0:T(8,128)S(1)}) custom-call(f32[134,512]{1,0:T(8,128)S(1)} %collective-permute-done.15.refs_0_, f32[512,512]{1,0:T(8,128)S(1)} %get-tuple-element.50.refs_5_.refs_1_, bf16[512,512]{1,0:T(8,128)(2,1)S(1)} %get-tuple-element.66.refs_2_, bf16[512,512]{1,0:T(8,128)(2,1)S(1)} %get-tuple-element.67.refs_3_, ...), custom_call_target="tpu_custom_call" | custom-call | flops 2500000000 | bytes 3424256 | tf_op jit(solution)/shard_map/pallas_call | solution.py:76
  37.5 0.6 %collective-permute-done.14.refs_3_ = f32[32,512]{1,0:T(8,128)S(1)} collective-permute-done((f32[32,512]{1,0:T(8,128)S(1)}, f32[32,512]{1,0:T(8,128)S(1)}, u32[]{:S(2)}, u32[]{:S(2)}) %collective-permute-start.14) | collective-permute-done | bytes 65568 | tf_op jit(solution)/shard_map/ppermute | solution.py:306
  38.1 0.9 %shard_map.94 = f32[128,512]{1,0:T(8,128)} custom-call(f32[32,512]{1,0:T(8,128)S(1)} %get-tuple-element.59.refs_5_.refs_0_, f32[32,512]{1,0:T(8,128)S(1)} %collective-permute-done.11.refs_1_, f32[32,512]{1,0:T(8,128)S(1)} %collective-permute-done.12.refs_2_, f32[32,512]{1,0:T(8,128)S(1)} %collective-permute-done.14.refs_3_, ...), custom_call_target="tpu_custom_call" | custom-call | flops 1200000000 | bytes 1114112 | tf_op jit(solution)/shard_map/pallas_call | solution.py:76
  (32 shorter events, 2.2 us)
Async XLA Ops:
  0.6 5.8 %collective-permute-start.1 = (s32[2,1024]{1,0:T(2,128)}, s32[2,1024]{1,0:T(2,128)S(1)}, u32[]{:S(2)}, u32[]{:S(2)}) collective-permute-start(s32[2,1024]{1,0:T(2,128)} %refs_0_.7), channel_id=1, source_target_pairs={{0,3},{1,2},{2,1},{3,0},{4,7},{5,6},{6,5},{7,4},{8,11},{9,10},{10,... | collective-permute-start | bytes 24584 | tf_op jit(solution)/shard_map/ppermute | solution.py:306
  4.6 8.1 %collective-permute-start = (f32[128,512]{1,0:T(8,128)}, f32[128,512]{1,0:T(8,128)S(1)}, u32[]{:S(2)}, u32[]{:S(2)}) collective-permute-start(f32[128,512]{1,0:T(8,128)} %refs_4_.1), channel_id=1, source_target_pairs={{0,1},{1,0},{2,3},{3,2},{4,5},{5,4},{6,7},{7,6},{8,9},{9,8},{10,11... | collective-permute-start | bytes 786440 | tf_op jit(solution)/shard_map/ppermute | solution.py:306
  5.1 9.1 %collective-permute-start.3 = (f32[128,512]{1,0:T(8,128)}, f32[128,512]{1,0:T(8,128)S(1)}, u32[]{:S(2)}, u32[]{:S(2)}) collective-permute-start(f32[128,512]{1,0:T(8,128)} %refs_4_.1), channel_id=1, source_target_pairs={{0,2},{1,3},{2,0},{3,1},{4,6},{5,7},{6,4},{7,5},{8,10},{9,11},{10,... | collective-permute-start | bytes 786440 | tf_op jit(solution)/shard_map/ppermute | solution.py:306
  5.2 21.2 %collective-permute-start.10 = (f32[512,512]{1,0:T(8,128)}, f32[512,512]{1,0:T(8,128)S(1)}, u32[]{:S(2)}, u32[]{:S(2)}) collective-permute-start(f32[512,512]{1,0:T(8,128)} %refs_2_.4), channel_id=1, source_target_pairs={{0,4},{1,5},{2,6},{3,7},{4,8},{5,9},{6,10},{7,11},{8,12},{9,13},{1... | collective-permute-start | bytes 3145736 | tf_op jit(solution)/shard_map/ppermute | solution.py:306
  5.2 1.0 %copy-start.1 = (f32[128,512]{1,0:T(8,128)S(1)}, f32[128,512]{1,0:T(8,128)}, u32[]{:S(2)}) copy-start(f32[128,512]{1,0:T(8,128)} %refs_4_.1) | copy-start | bytes 786436
  6.4 3.6 %copy-start = (f32[512,512]{1,0:T(8,128)S(1)}, f32[512,512]{1,0:T(8,128)}, u32[]{:S(2)}) copy-start(f32[512,512]{1,0:T(8,128)} %refs_2_.4) | copy-start | bytes 3145732
  6.9 3.3 %copy-start.3 = (s32[2,1024]{1,0:T(2,128)S(1)}, s32[2,1024]{1,0:T(2,128)}, u32[]{:S(2)}) copy-start(s32[2,1024]{1,0:T(2,128)} %refs_0_.7) | copy-start | bytes 24580
  6.9 3.3 %copy-start.4 = (s32[2,1024]{1,0:T(2,128)S(1)}, s32[2,1024]{1,0:T(2,128)}, u32[]{:S(2)}) copy-start(s32[2,1024]{1,0:T(2,128)} %refs_1_.3) | copy-start | bytes 24580
  6.9 3.3 %copy-start.5 = (f32[2,1024]{1,0:T(2,128)S(1)}, f32[2,1024]{1,0:T(2,128)}, u32[]{:S(2)}) copy-start(f32[2,1024]{1,0:T(2,128)} %refs_2_.5) | copy-start | bytes 24580
  6.9 7.1 %collective-permute-start.2 = (f32[32,512]{1,0:T(8,128)S(1)}, f32[32,512]{1,0:T(8,128)S(1)}, u32[]{:S(2)}, u32[]{:S(2)}) collective-permute-start(f32[32,512]{1,0:T(8,128)S(1)} %shard_map.78.refs_4_.refs_1_), channel_id=1, source_target_pairs={{0,3},{1,2},{2,1},{3,0},{4,7},{5,6},{6,5},{7,4},{8,11},{9,10},{10,... | collective-permute-start | bytes 196616 | tf_op jit(solution)/shard_map/ppermute | solution.py:306
  10.2 0.7 %copy-start.6 = (s32[2,1]{0,1:T(1,128)S(1)}, s32[2,1]{0,1:T(1,128)}, u32[]{:S(2)}) copy-start(s32[2,1]{0,1:T(1,128)} %param.11) | copy-start | bytes 28
  15.0 5.9 %collective-permute-start.4 = (f32[40,512]{1,0:T(8,128)S(1)}, f32[40,512]{1,0:T(8,128)S(1)}, u32[]{:S(2)}, u32[]{:S(2)}) collective-permute-start(f32[40,512]{1,0:T(8,128)S(1)} %get-tuple-element.46), channel_id=1, source_target_pairs={{0,3},{1,2},{2,1},{3,0},{4,7},{5,6},{6,5},{7,4},{8,11},{9,10},{10,... | collective-permute-start | bytes 245768 | tf_op jit(solution)/shard_map/ppermute | solution.py:306
  16.5 5.9 %collective-permute-start.5 = (f32[40,512]{1,0:T(8,128)S(1)}, f32[40,512]{1,0:T(8,128)S(1)}, u32[]{:S(2)}, u32[]{:S(2)}) collective-permute-start(f32[40,512]{1,0:T(8,128)S(1)} %get-tuple-element.47), channel_id=1, source_target_pairs={{0,2},{1,3},{2,0},{3,1},{4,6},{5,7},{6,4},{7,5},{8,10},{9,11},{10,... | collective-permute-start | bytes 245768 | tf_op jit(solution)/shard_map/ppermute | solution.py:306
  18.0 4.4 %collective-permute-start.6 = (f32[40,512]{1,0:T(8,128)S(1)}, f32[40,512]{1,0:T(8,128)S(1)}, u32[]{:S(2)}, u32[]{:S(2)}) collective-permute-start(f32[40,512]{1,0:T(8,128)S(1)} %get-tuple-element.48), channel_id=1, source_target_pairs={{0,1},{1,0},{2,3},{3,2},{4,5},{5,4},{6,7},{7,6},{8,9},{9,8},{10,11... | collective-permute-start | bytes 245768 | tf_op jit(solution)/shard_map/ppermute | solution.py:306
  18.6 7.9 %collective-permute-start.9 = (f32[134,512]{1,0:T(8,128)S(1)}, f32[134,512]{1,0:T(8,128)S(1)}, u32[]{:S(2)}, u32[]{:S(2)}) collective-permute-start(f32[134,512]{1,0:T(8,128)S(1)} %shard_map.88), channel_id=1, source_target_pairs={{0,4},{1,5},{2,6},{3,7},{4,8},{5,9},{6,10},{7,11},{8,12},{9,13},{1... | collective-permute-start | bytes 823304 | tf_op jit(solution)/shard_map/ppermute | solution.py:306
  19.7 2.8 %copy-start.2 = (f32[128,512]{1,0:T(8,128)S(1)}, f32[128,512]{1,0:T(8,128)}, u32[]{:S(2)}) copy-start(f32[128,512]{1,0:T(8,128)} %refs_4_.1) | copy-start | bytes 786436
  22.9 5.6 %collective-permute-start.7 = (f32[32,512]{1,0:T(8,128)S(1)}, f32[32,512]{1,0:T(8,128)S(1)}, u32[]{:S(2)}, u32[]{:S(2)}) collective-permute-start(f32[32,512]{1,0:T(8,128)S(1)} %get-tuple-element.55), channel_id=1, source_target_pairs={{0,3},{1,2},{2,1},{3,0},{4,7},{5,6},{6,5},{7,4},{8,11},{9,10},{10,... | collective-permute-start | bytes 196616 | tf_op jit(solution)/shard_map/ppermute | solution.py:306
  24.3 4.9 %collective-permute-start.8 = (f32[32,512]{1,0:T(8,128)S(1)}, f32[32,512]{1,0:T(8,128)S(1)}, u32[]{:S(2)}, u32[]{:S(2)}) collective-permute-start(f32[32,512]{1,0:T(8,128)S(1)} %get-tuple-element.56), channel_id=1, source_target_pairs={{0,2},{1,3},{2,0},{3,1},{4,6},{5,7},{6,4},{7,5},{8,10},{9,11},{10,... | collective-permute-start | bytes 196616 | tf_op jit(solution)/shard_map/ppermute | solution.py:306
  24.9 5.0 %collective-permute-start.13 = (f32[32,512]{1,0:T(8,128)S(1)}, f32[32,512]{1,0:T(8,128)S(1)}, u32[]{:S(2)}, u32[]{:S(2)}) collective-permute-start(f32[32,512]{1,0:T(8,128)S(1)} %get-tuple-element.62), channel_id=1, source_target_pairs={{0,1},{1,0},{2,3},{3,2},{4,5},{5,4},{6,7},{7,6},{8,9},{9,8},{10,11... | collective-permute-start | bytes 196616 | tf_op jit(solution)/shard_map/ppermute | solution.py:306
  30.0 5.4 %collective-permute-start.15 = (f32[134,512]{1,0:T(8,128)S(1)}, f32[134,512]{1,0:T(8,128)S(1)}, u32[]{:S(2)}, u32[]{:S(2)}) collective-permute-start(f32[134,512]{1,0:T(8,128)S(1)} %shard_map.92), channel_id=1, source_target_pairs={{0,28},{1,29},{2,30},{3,31},{4,0},{5,1},{6,2},{7,3},{8,4},{9,5},{1... | collective-permute-start | bytes 823304 | tf_op jit(solution)/shard_map/ppermute | solution.py:306
  31.1 6.4 %collective-permute-start.11 = (f32[32,512]{1,0:T(8,128)S(1)}, f32[32,512]{1,0:T(8,128)S(1)}, u32[]{:S(2)}, u32[]{:S(2)}) collective-permute-start(f32[32,512]{1,0:T(8,128)S(1)} %get-tuple-element.60), channel_id=1, source_target_pairs={{0,3},{1,2},{2,1},{3,0},{4,7},{5,6},{6,5},{7,4},{8,11},{9,10},{10,... | collective-permute-start | bytes 196616 | tf_op jit(solution)/shard_map/ppermute | solution.py:306
  32.1 5.4 %collective-permute-start.12 = (f32[32,512]{1,0:T(8,128)S(1)}, f32[32,512]{1,0:T(8,128)S(1)}, u32[]{:S(2)}, u32[]{:S(2)}) collective-permute-start(f32[32,512]{1,0:T(8,128)S(1)} %get-tuple-element.61), channel_id=1, source_target_pairs={{0,2},{1,3},{2,0},{3,1},{4,6},{5,7},{6,4},{7,5},{8,10},{9,11},{10,... | collective-permute-start | bytes 196616 | tf_op jit(solution)/shard_map/ppermute | solution.py:306
  33.8 4.3 %collective-permute-start.14 = (f32[32,512]{1,0:T(8,128)S(1)}, f32[32,512]{1,0:T(8,128)S(1)}, u32[]{:S(2)}, u32[]{:S(2)}) collective-permute-start(f32[32,512]{1,0:T(8,128)S(1)} %get-tuple-element.64.refs_4_), channel_id=1, source_target_pairs={{0,1},{1,0},{2,3},{3,2},{4,5},{5,4},{6,7},{7,6},{8,9},{9,8},{10,11... | collective-permute-start | bytes 196616 | tf_op jit(solution)/shard_map/ppermute | solution.py:306

commit v7 on v6

--- a/solution.py
+++ b/solution.py
@@ -365,7 +365,7 @@
         *listed, ranked, flops=FLOPS["pack1"], after=[block],
     )[0]
     tables = prepare(packed, FLOPS["prep1"])
-    joined = join(first_pieces, factors, entries_first, FLOPS["stack"], [])
+    joined = join(first_pieces, factors, entries_first, FLOPS["stack"], [block])
     next_parts = call(
         functools.partial(next_kernel, steps[0], touched), [shaped(item_factors.shape, BF16)] * 2,
         exchange(joined, 0, 1), next_block, flops=FLOPS["next"],

time: 39.2 us -> 39.2 us (level)
  no operation moved by 1% of the time
where the time goes in v7:
time: 39.2 us; the launch traced here: 39.1 us
  starting transfers between devices  19.6 us (50%)
  Pallas kernels  12 us (31%)
  waiting for transfers between devices  4.97 us (13%)
  local copies, waits for them, and re-layouts  1.64 us (4%)
  between operations  0.86 us (2%)
    ppermute x16, starting transfers between devices, exchange(): return lax.ppermute(value, ('rows', 'strata'), pairs)  19.6 us
    pallas_call x18, Pallas kernels, call(): pl.pallas_call(body, out_shape=list(outs), in_specs=[pl.BlockSpec(memory_...  12 us
    ppermute x16, waiting for transfers between devices, exchange(): return lax.ppermute(value, ('rows', 'strata'), pairs)  4.97 us
    unnamed x14, local copies, waits for them, and re-layouts  1.64 us
  transfers between devices with their start and end apart: 16, of which 9 were waited for; matrix products, arithmetic and copies ran while one was open for 0% of the time, Pallas kernels for 28%

profile of v7, /device:TPU:0, one launch (start us, length us, event | category | flops | bytes accessed | tf_op | source)
XLA Modules:
  0.0 39.1 jit_solution(5070192293552378766)
XLA Ops:
  0.6 4.0 %collective-permute-start.1 = (s32[2,1024]{1,0:T(2,128)}, s32[2,1024]{1,0:T(2,128)S(1)}, u32[]{:S(2)}, u32[]{:S(2)}) collective-permute-start(s32[2,1024]{1,0:T(2,128)} %refs_0_.7), channel_id=1, source_target_pairs={{0,3},{1,2},{2,1},{3,0},{4,7},{5,6},{6,5},{7,4},{8,11},{9,10},{10,... | collective-permute-start | bytes 24584 | tf_op jit(solution)/shard_map/ppermute | solution.py:306
  4.6 0.5 %collective-permute-start = (f32[128,512]{1,0:T(8,128)}, f32[128,512]{1,0:T(8,128)S(1)}, u32[]{:S(2)}, u32[]{:S(2)}) collective-permute-start(f32[128,512]{1,0:T(8,128)} %refs_4_.1), channel_id=1, source_target_pairs={{0,1},{1,0},{2,3},{3,2},{4,5},{5,4},{6,7},{7,6},{8,9},{9,8},{10,11... | collective-permute-start | bytes 786440 | tf_op jit(solution)/shard_map/ppermute | solution.py:306
  5.2 1.0 %copy-done.1 = f32[128,512]{1,0:T(8,128)S(1)} copy-done((f32[128,512]{1,0:T(8,128)S(1)}, f32[128,512]{1,0:T(8,128)}, u32[]{:S(2)}) %copy-start.1) | copy-done | bytes 262168
  6.9 3.1 %collective-permute-start.2 = (f32[32,512]{1,0:T(8,128)S(1)}, f32[32,512]{1,0:T(8,128)S(1)}, u32[]{:S(2)}, u32[]{:S(2)}) collective-permute-start(f32[32,512]{1,0:T(8,128)S(1)} %shard_map.78.refs_4_.refs_1_), channel_id=1, source_target_pairs={{0,3},{1,2},{2,1},{3,0},{4,7},{5,6},{6,5},{7,4},{8,11},{9,10},{10,... | collective-permute-start | bytes 196616 | tf_op jit(solution)/shard_map/ppermute | solution.py:306
  10.2 0.6 %copy-done.6 = s32[2,1]{0,1:T(1,128)S(1)} copy-done((s32[2,1]{0,1:T(1,128)S(1)}, s32[2,1]{0,1:T(1,128)}, u32[]{:S(2)}) %copy-start.6) | copy-done | bytes 32
  10.8 1.2 %shard_map.79 = (f32[128,128]{1,0:T(8,128)S(1)}, f32[8,128]{1,0:T(8,128)S(1)}, f32[3,1024]{1,0:T(4,128)S(1)}) custom-call(s32[2,1024]{1,0:T(2,128)S(1)} %copy-done.3, s32[2,1024]{1,0:T(2,128)S(1)} %copy-done.4, f32[2,1024]{1,0:T(2,128)S(1)} %copy-done.5, s32[1,2]{1,0:T(1,128)S(1)} %bitcast.1, f32[32,512]{1,0:T(8,128)S(1)} %shard_map.78.refs_4_.refs_1_), custom_call_target="tpu_custom_call" | custom-call | flops 1400000000 | bytes 106504 | tf_op jit(solution)/shard_map/pallas_call | solution.py:76
  12.0 0.6 %shard_map.81 = (f32[128,512]{1,0:T(8,128)S(1)}, f32[128,512]{1,0:T(8,128)S(1)}) custom-call(f32[3,1024]{1,0:T(4,128)S(1)} %get-tuple-element.41.refs_0_.refs_2_), custom_call_target="tpu_custom_call" | custom-call | flops 900000000 | bytes 536576 | tf_op jit(solution)/shard_map/pallas_call | solution.py:76
  12.6 0.8 %shard_map.82 = (f32[40,512]{1,0:T(8,128)S(1)}, f32[40,512]{1,0:T(8,128)S(1)}, f32[64,1024]{1,0:T(8,128)S(1)}) custom-call(bf16[128,512]{1,0:T(8,128)(2,1)S(1)} %get-tuple-element.36.refs_1_.refs_0_, f32[128,512]{1,0:T(8,128)S(1)} %collective-permute-done.refs_1_, f32[8,128]{1,0:T(8,128)S(1)} %get-tuple-element.38.refs_2_, ...), custom_call_target="tpu_custom_call" | custom-call | flops 1000000000 | bytes 2527232 | tf_op jit(solution)/shard_map/pallas_call | solution.py:76
  13.5 0.6 %collective-permute-done.2.refs_0_ = f32[32,512]{1,0:T(8,128)S(1)} collective-permute-done((f32[32,512]{1,0:T(8,128)S(1)}, f32[32,512]{1,0:T(8,128)S(1)}, u32[]{:S(2)}, u32[]{:S(2)}) %collective-permute-start.2) | collective-permute-done | bytes 65568 | tf_op jit(solution)/shard_map/ppermute | solution.py:306
  14.2 0.8 %shard_map.83 = (f32[40,512]{1,0:T(8,128)S(1)}, f32[40,512]{1,0:T(8,128)S(1)}, f32[64,1024]{1,0:T(8,128)S(1)}) custom-call(f32[32,512]{1,0:T(8,128)S(1)} %collective-permute-done.2.refs_0_, f32[128,512]{1,0:T(8,128)S(1)} %collective-permute-done.3.refs_1_, f32[8,128]{1,0:T(8,128)S(1)} %get-tuple-element.38.refs_2_, ...), custom_call_target="tpu_custom_call" | custom-call | flops 1000000000 | bytes 2461696 | tf_op jit(solution)/shard_map/pallas_call | solution.py:76
  15.0 1.5 %collective-permute-start.4 = (f32[40,512]{1,0:T(8,128)S(1)}, f32[40,512]{1,0:T(8,128)S(1)}, u32[]{:S(2)}, u32[]{:S(2)}) collective-permute-start(f32[40,512]{1,0:T(8,128)S(1)} %get-tuple-element.46), channel_id=1, source_target_pairs={{0,3},{1,2},{2,1},{3,0},{4,7},{5,6},{6,5},{7,4},{8,11},{9,10},{10,... | collective-permute-start | bytes 245768 | tf_op jit(solution)/shard_map/ppermute | solution.py:306
  16.5 1.5 %collective-permute-start.5 = (f32[40,512]{1,0:T(8,128)S(1)}, f32[40,512]{1,0:T(8,128)S(1)}, u32[]{:S(2)}, u32[]{:S(2)}) collective-permute-start(f32[40,512]{1,0:T(8,128)S(1)} %get-tuple-element.47), channel_id=1, source_target_pairs={{0,2},{1,3},{2,0},{3,1},{4,6},{5,7},{6,4},{7,5},{8,10},{9,11},{10,... | collective-permute-start | bytes 245768 | tf_op jit(solution)/shard_map/ppermute | solution.py:306
  18.0 0.5 %collective-permute-start.6 = (f32[40,512]{1,0:T(8,128)S(1)}, f32[40,512]{1,0:T(8,128)S(1)}, u32[]{:S(2)}, u32[]{:S(2)}) collective-permute-start(f32[40,512]{1,0:T(8,128)S(1)} %get-tuple-element.48), channel_id=1, source_target_pairs={{0,1},{1,0},{2,3},{3,2},{4,5},{5,4},{6,7},{7,6},{8,9},{9,8},{10,11... | collective-permute-start | bytes 245768 | tf_op jit(solution)/shard_map/ppermute | solution.py:306
  18.5 0.6 %shard_map.84 = (f32[512,512]{1,0:T(8,128)S(1)}, bf16[512,512]{1,0:T(8,128)(2,1)S(1)}, bf16[512,512]{1,0:T(8,128)(2,1)S(1)}) custom-call(f32[64,1024]{1,0:T(8,128)S(1)} %get-tuple-element.45.refs_8_.refs_0_, f32[64,1024]{1,0:T(8,128)S(1)} %get-tuple-element.49.refs_1_, f32[512,512]{1,0:T(8,128)S(1)} %copy-done), custom_call_target="tpu_custom_call" | custom-call | flops 900000000 | bytes 3670016 | tf_op jit(solution)/shard_map/pallas_call | solution.py:76
  19.7 0.6 %shard_map.86 = (f32[128,512]{1,0:T(8,128)S(1)}, f32[128,512]{1,0:T(8,128)S(1)}) custom-call(f32[3,1024]{1,0:T(4,128)S(1)} %shard_map.85.refs_0_.refs_4_), custom_call_target="tpu_custom_call" | custom-call | flops 900000000 | bytes 536576 | tf_op jit(solution)/shard_map/pallas_call | solution.py:76
  20.3 0.6 %collective-permute-done.4.refs_1_.refs_5_ = f32[40,512]{1,0:T(8,128)S(1)} collective-permute-done((f32[40,512]{1,0:T(8,128)S(1)}, f32[40,512]{1,0:T(8,128)S(1)}, u32[]{:S(2)}, u32[]{:S(2)}) %collective-permute-start.4) | collective-permute-done | bytes 81952 | tf_op jit(solution)/shard_map/ppermute | solution.py:306
  20.9 1.4 %collective-permute-done.5.refs_2_.refs_6_ = f32[40,512]{1,0:T(8,128)S(1)} collective-permute-done((f32[40,512]{1,0:T(8,128)S(1)}, f32[40,512]{1,0:T(8,128)S(1)}, u32[]{:S(2)}, u32[]{:S(2)}) %collective-permute-start.5) | collective-permute-done | bytes 81952 | tf_op jit(solution)/shard_map/ppermute | solution.py:306
  22.9 1.4 %collective-permute-start.7 = (f32[32,512]{1,0:T(8,128)S(1)}, f32[32,512]{1,0:T(8,128)S(1)}, u32[]{:S(2)}, u32[]{:S(2)}) collective-permute-start(f32[32,512]{1,0:T(8,128)S(1)} %get-tuple-element.55), channel_id=1, source_target_pairs={{0,3},{1,2},{2,1},{3,0},{4,7},{5,6},{6,5},{7,4},{8,11},{9,10},{10,... | collective-permute-start | bytes 196616 | tf_op jit(solution)/shard_map/ppermute | solution.py:306
  24.3 0.6 %collective-permute-start.8 = (f32[32,512]{1,0:T(8,128)S(1)}, f32[32,512]{1,0:T(8,128)S(1)}, u32[]{:S(2)}, u32[]{:S(2)}) collective-permute-start(f32[32,512]{1,0:T(8,128)S(1)} %get-tuple-element.56), channel_id=1, source_target_pairs={{0,2},{1,3},{2,0},{3,1},{4,6},{5,7},{6,4},{7,5},{8,10},{9,11},{10,... | collective-permute-start | bytes 196616 | tf_op jit(solution)/shard_map/ppermute | solution.py:306
  24.9 1.5 %collective-permute-start.13 = (f32[32,512]{1,0:T(8,128)S(1)}, f32[32,512]{1,0:T(8,128)S(1)}, u32[]{:S(2)}, u32[]{:S(2)}) collective-permute-start(f32[32,512]{1,0:T(8,128)S(1)} %get-tuple-element.62), channel_id=1, source_target_pairs={{0,1},{1,0},{2,3},{3,2},{4,5},{5,4},{6,7},{7,6},{8,9},{9,8},{10,11... | collective-permute-start | bytes 196616 | tf_op jit(solution)/shard_map/ppermute | solution.py:306
  26.4 0.6 %collective-permute-done.9.refs_0_ = f32[134,512]{1,0:T(8,128)S(1)} collective-permute-done((f32[134,512]{1,0:T(8,128)S(1)}, f32[134,512]{1,0:T(8,128)S(1)}, u32[]{:S(2)}, u32[]{:S(2)}) %collective-permute-start.9) | collective-permute-done | bytes 274464 | tf_op jit(solution)/shard_map/ppermute | solution.py:306
  27.0 1.5 %shard_map.89 = (bf16[512,512]{1,0:T(8,128)(2,1)S(1)}, bf16[512,512]{1,0:T(8,128)(2,1)S(1)}) custom-call(f32[134,512]{1,0:T(8,128)S(1)} %collective-permute-done.9.refs_0_, f32[512,512]{1,0:T(8,128)S(1)} %collective-permute-done.10.refs_1_), custom_call_target="tpu_custom_call" | custom-call | flops 2000000000 | bytes 2371584 | tf_op jit(solution)/shard_map/pallas_call | solution.py:76
  28.5 0.7 %collective-permute-done.8.refs_2_ = f32[32,512]{1,0:T(8,128)S(1)} collective-permute-done((f32[32,512]{1,0:T(8,128)S(1)}, f32[32,512]{1,0:T(8,128)S(1)}, u32[]{:S(2)}, u32[]{:S(2)}) %collective-permute-start.8) | collective-permute-done | bytes 65568 | tf_op jit(solution)/shard_map/ppermute | solution.py:306
  29.2 0.8 %shard_map.90 = (f32[32,512]{1,0:T(8,128)S(1)}, f32[32,512]{1,0:T(8,128)S(1)}, f32[32,512]{1,0:T(8,128)S(1)}, f32[8,128]{1,0:T(8,128)S(1)}) custom-call(f32[32,512]{1,0:T(8,128)S(1)} %get-tuple-element.54.refs_0_, f32[32,512]{1,0:T(8,128)S(1)} %collective-permute-done.7.refs_1_.refs_3_, f32[32,512]{1,0:T(8,128)S(1)} %collective-permute-done.8.refs_2_, ...), custom_call_target="tpu_custom_call" | custom-call | flops 800000000 | bytes 1970176 | tf_op jit(solution)/shard_map/pallas_call | solution.py:76
  30.0 1.2 %collective-permute-start.15 = (f32[134,512]{1,0:T(8,128)S(1)}, f32[134,512]{1,0:T(8,128)S(1)}, u32[]{:S(2)}, u32[]{:S(2)}) collective-permute-start(f32[134,512]{1,0:T(8,128)S(1)} %shard_map.92), channel_id=1, source_target_pairs={{0,28},{1,29},{2,30},{3,31},{4,0},{5,1},{6,2},{7,3},{8,4},{9,5},{1... | collective-permute-start | bytes 823304 | tf_op jit(solution)/shard_map/ppermute | solution.py:306
  31.1 1.0 %collective-permute-start.11 = (f32[32,512]{1,0:T(8,128)S(1)}, f32[32,512]{1,0:T(8,128)S(1)}, u32[]{:S(2)}, u32[]{:S(2)}) collective-permute-start(f32[32,512]{1,0:T(8,128)S(1)} %get-tuple-element.60), channel_id=1, source_target_pairs={{0,3},{1,2},{2,1},{3,0},{4,7},{5,6},{6,5},{7,4},{8,11},{9,10},{10,... | collective-permute-start | bytes 196616 | tf_op jit(solution)/shard_map/ppermute | solution.py:306
  32.1 1.1 %collective-permute-start.12 = (f32[32,512]{1,0:T(8,128)S(1)}, f32[32,512]{1,0:T(8,128)S(1)}, u32[]{:S(2)}, u32[]{:S(2)}) collective-permute-start(f32[32,512]{1,0:T(8,128)S(1)} %get-tuple-element.61), channel_id=1, source_target_pairs={{0,2},{1,3},{2,0},{3,1},{4,6},{5,7},{6,4},{7,5},{8,10},{9,11},{10,... | collective-permute-start | bytes 196616 | tf_op jit(solution)/shard_map/ppermute | solution.py:306
  33.2 0.7 %shard_map.91 = (f32[32,512]{1,0:T(8,128)S(1)}, f32[8,128]{1,0:T(8,128)}) custom-call(f32[32,512]{1,0:T(8,128)S(1)} %collective-permute-done.13.refs_0_.refs_1_, bf16[512,512]{1,0:T(8,128)(2,1)S(1)} %get-tuple-element.57.refs_3_.refs_1_, bf16[512,512]{1,0:T(8,128)(2,1)S(1)} %get-tuple-element.58.refs_4_.refs_2_, ...), custom_call_target="tpu_custom_call" | custom-call | flops 800000000 | bytes 1708032 | tf_op jit(solution)/shard_map/pallas_call | solution.py:76
  33.8 1.5 %collective-permute-start.14 = (f32[32,512]{1,0:T(8,128)S(1)}, f32[32,512]{1,0:T(8,128)S(1)}, u32[]{:S(2)}, u32[]{:S(2)}) collective-permute-start(f32[32,512]{1,0:T(8,128)S(1)} %get-tuple-element.64.refs_4_), channel_id=1, source_target_pairs={{0,1},{1,0},{2,3},{3,2},{4,5},{5,4},{6,7},{7,6},{8,9},{9,8},{10,11... | collective-permute-start | bytes 196616 | tf_op jit(solution)/shard_map/ppermute | solution.py:306
  35.3 2.2 %shard_map.93 = (f32[512,512]{1,0:T(8,128)}, f32[8,128]{1,0:T(8,128)S(1)}) custom-call(f32[134,512]{1,0:T(8,128)S(1)} %collective-permute-done.15.refs_0_, f32[512,512]{1,0:T(8,128)S(1)} %get-tuple-element.50.refs_5_.refs_3_.refs_1_, bf16[512,512]{1,0:T(8,128)(2,1)S(1)} %get-tuple-element.66.refs_2_, bf16[512,512]{1,0:T(8,128)(2,1)S(1)} %get-tuple-element.67.refs_3_, ...), custom_call_target="tpu_custom_call" | custom-call | flops 2500000000 | bytes 3424256 | tf_op jit(solution)/shard_map/pallas_call | solution.py:76
  37.5 0.6 %collective-permute-done.14.refs_3_ = f32[32,512]{1,0:T(8,128)S(1)} collective-permute-done((f32[32,512]{1,0:T(8,128)S(1)}, f32[32,512]{1,0:T(8,128)S(1)}, u32[]{:S(2)}, u32[]{:S(2)}) %collective-permute-start.14) | collective-permute-done | bytes 65568 | tf_op jit(solution)/shard_map/ppermute | solution.py:306
  38.1 0.9 %shard_map.94 = f32[128,512]{1,0:T(8,128)} custom-call(f32[32,512]{1,0:T(8,128)S(1)} %get-tuple-element.59.refs_5_.refs_0_, f32[32,512]{1,0:T(8,128)S(1)} %collective-permute-done.11.refs_1_, f32[32,512]{1,0:T(8,128)S(1)} %collective-permute-done.12.refs_2_, f32[32,512]{1,0:T(8,128)S(1)} %collective-permute-done.14.refs_3_, ...), custom_call_target="tpu_custom_call" | custom-call | flops 1200000000 | bytes 1114112 | tf_op jit(solution)/shard_map/pallas_call | solution.py:76
  (32 shorter events, 2.2 us)
Async XLA Ops:
  0.6 5.8 %collective-permute-start.1 = (s32[2,1024]{1,0:T(2,128)}, s32[2,1024]{1,0:T(2,128)S(1)}, u32[]{:S(2)}, u32[]{:S(2)}) collective-permute-start(s32[2,1024]{1,0:T(2,128)} %refs_0_.7), channel_id=1, source_target_pairs={{0,3},{1,2},{2,1},{3,0},{4,7},{5,6},{6,5},{7,4},{8,11},{9,10},{10,... | collective-permute-start | bytes 24584 | tf_op jit(solution)/shard_map/ppermute | solution.py:306
  4.6 8.1 %collective-permute-start = (f32[128,512]{1,0:T(8,128)}, f32[128,512]{1,0:T(8,128)S(1)}, u32[]{:S(2)}, u32[]{:S(2)}) collective-permute-start(f32[128,512]{1,0:T(8,128)} %refs_4_.1), channel_id=1, source_target_pairs={{0,1},{1,0},{2,3},{3,2},{4,5},{5,4},{6,7},{7,6},{8,9},{9,8},{10,11... | collective-permute-start | bytes 786440 | tf_op jit(solution)/shard_map/ppermute | solution.py:306
  5.1 9.1 %collective-permute-start.3 = (f32[128,512]{1,0:T(8,128)}, f32[128,512]{1,0:T(8,128)S(1)}, u32[]{:S(2)}, u32[]{:S(2)}) collective-permute-start(f32[128,512]{1,0:T(8,128)} %refs_4_.1), channel_id=1, source_target_pairs={{0,2},{1,3},{2,0},{3,1},{4,6},{5,7},{6,4},{7,5},{8,10},{9,11},{10,... | collective-permute-start | bytes 786440 | tf_op jit(solution)/shard_map/ppermute | solution.py:306
  5.2 21.8 %collective-permute-start.10 = (f32[512,512]{1,0:T(8,128)}, f32[512,512]{1,0:T(8,128)S(1)}, u32[]{:S(2)}, u32[]{:S(2)}) collective-permute-start(f32[512,512]{1,0:T(8,128)} %refs_2_.4), channel_id=1, source_target_pairs={{0,4},{1,5},{2,6},{3,7},{4,8},{5,9},{6,10},{7,11},{8,12},{9,13},{1... | collective-permute-start | bytes 3145736 | tf_op jit(solution)/shard_map/ppermute | solution.py:306
  5.2 1.0 %copy-start.1 = (f32[128,512]{1,0:T(8,128)S(1)}, f32[128,512]{1,0:T(8,128)}, u32[]{:S(2)}) copy-start(f32[128,512]{1,0:T(8,128)} %refs_4_.1) | copy-start | bytes 786436
  6.4 3.6 %copy-start = (f32[512,512]{1,0:T(8,128)S(1)}, f32[512,512]{1,0:T(8,128)}, u32[]{:S(2)}) copy-start(f32[512,512]{1,0:T(8,128)} %refs_2_.4) | copy-start | bytes 3145732
  6.9 3.3 %copy-start.3 = (s32[2,1024]{1,0:T(2,128)S(1)}, s32[2,1024]{1,0:T(2,128)}, u32[]{:S(2)}) copy-start(s32[2,1024]{1,0:T(2,128)} %refs_0_.7) | copy-start | bytes 24580
  6.9 3.3 %copy-start.4 = (s32[2,1024]{1,0:T(2,128)S(1)}, s32[2,1024]{1,0:T(2,128)}, u32[]{:S(2)}) copy-start(s32[2,1024]{1,0:T(2,128)} %refs_1_.3) | copy-start | bytes 24580
  6.9 3.3 %copy-start.5 = (f32[2,1024]{1,0:T(2,128)S(1)}, f32[2,1024]{1,0:T(2,128)}, u32[]{:S(2)}) copy-start(f32[2,1024]{1,0:T(2,128)} %refs_2_.5) | copy-start | bytes 24580
  6.9 7.1 %collective-permute-start.2 = (f32[32,512]{1,0:T(8,128)S(1)}, f32[32,512]{1,0:T(8,128)S(1)}, u32[]{:S(2)}, u32[]{:S(2)}) collective-permute-start(f32[32,512]{1,0:T(8,128)S(1)} %shard_map.78.refs_4_.refs_1_), channel_id=1, source_target_pairs={{0,3},{1,2},{2,1},{3,0},{4,7},{5,6},{6,5},{7,4},{8,11},{9,10},{10,... | collective-permute-start | bytes 196616 | tf_op jit(solution)/shard_map/ppermute | solution.py:306
  10.2 0.7 %copy-start.6 = (s32[2,1]{0,1:T(1,128)S(1)}, s32[2,1]{0,1:T(1,128)}, u32[]{:S(2)}) copy-start(s32[2,1]{0,1:T(1,128)} %param.11) | copy-start | bytes 28
  15.0 5.9 %collective-permute-start.4 = (f32[40,512]{1,0:T(8,128)S(1)}, f32[40,512]{1,0:T(8,128)S(1)}, u32[]{:S(2)}, u32[]{:S(2)}) collective-permute-start(f32[40,512]{1,0:T(8,128)S(1)} %get-tuple-element.46), channel_id=1, source_target_pairs={{0,3},{1,2},{2,1},{3,0},{4,7},{5,6},{6,5},{7,4},{8,11},{9,10},{10,... | collective-permute-start | bytes 245768 | tf_op jit(solution)/shard_map/ppermute | solution.py:306
  16.5 5.9 %collective-permute-start.5 = (f32[40,512]{1,0:T(8,128)S(1)}, f32[40,512]{1,0:T(8,128)S(1)}, u32[]{:S(2)}, u32[]{:S(2)}) collective-permute-start(f32[40,512]{1,0:T(8,128)S(1)} %get-tuple-element.47), channel_id=1, source_target_pairs={{0,2},{1,3},{2,0},{3,1},{4,6},{5,7},{6,4},{7,5},{8,10},{9,11},{10,... | collective-permute-start | bytes 245768 | tf_op jit(solution)/shard_map/ppermute | solution.py:306
  18.0 4.4 %collective-permute-start.6 = (f32[40,512]{1,0:T(8,128)S(1)}, f32[40,512]{1,0:T(8,128)S(1)}, u32[]{:S(2)}, u32[]{:S(2)}) collective-permute-start(f32[40,512]{1,0:T(8,128)S(1)} %get-tuple-element.48), channel_id=1, source_target_pairs={{0,1},{1,0},{2,3},{3,2},{4,5},{5,4},{6,7},{7,6},{8,9},{9,8},{10,11... | collective-permute-start | bytes 245768 | tf_op jit(solution)/shard_map/ppermute | solution.py:306
  19.2 7.8 %collective-permute-start.9 = (f32[134,512]{1,0:T(8,128)S(1)}, f32[134,512]{1,0:T(8,128)S(1)}, u32[]{:S(2)}, u32[]{:S(2)}) collective-permute-start(f32[134,512]{1,0:T(8,128)S(1)} %shard_map.88), channel_id=1, source_target_pairs={{0,4},{1,5},{2,6},{3,7},{4,8},{5,9},{6,10},{7,11},{8,12},{9,13},{1... | collective-permute-start | bytes 823304 | tf_op jit(solution)/shard_map/ppermute | solution.py:306
  19.7 2.8 %copy-start.2 = (f32[128,512]{1,0:T(8,128)S(1)}, f32[128,512]{1,0:T(8,128)}, u32[]{:S(2)}) copy-start(f32[128,512]{1,0:T(8,128)} %refs_4_.1) | copy-start | bytes 786436
  22.9 5.6 %collective-permute-start.7 = (f32[32,512]{1,0:T(8,128)S(1)}, f32[32,512]{1,0:T(8,128)S(1)}, u32[]{:S(2)}, u32[]{:S(2)}) collective-permute-start(f32[32,512]{1,0:T(8,128)S(1)} %get-tuple-element.55), channel_id=1, source_target_pairs={{0,3},{1,2},{2,1},{3,0},{4,7},{5,6},{6,5},{7,4},{8,11},{9,10},{10,... | collective-permute-start | bytes 196616 | tf_op jit(solution)/shard_map/ppermute | solution.py:306
  24.3 4.9 %collective-permute-start.8 = (f32[32,512]{1,0:T(8,128)S(1)}, f32[32,512]{1,0:T(8,128)S(1)}, u32[]{:S(2)}, u32[]{:S(2)}) collective-permute-start(f32[32,512]{1,0:T(8,128)S(1)} %get-tuple-element.56), channel_id=1, source_target_pairs={{0,2},{1,3},{2,0},{3,1},{4,6},{5,7},{6,4},{7,5},{8,10},{9,11},{10,... | collective-permute-start | bytes 196616 | tf_op jit(solution)/shard_map/ppermute | solution.py:306
  24.9 5.0 %collective-permute-start.13 = (f32[32,512]{1,0:T(8,128)S(1)}, f32[32,512]{1,0:T(8,128)S(1)}, u32[]{:S(2)}, u32[]{:S(2)}) collective-permute-start(f32[32,512]{1,0:T(8,128)S(1)} %get-tuple-element.62), channel_id=1, source_target_pairs={{0,1},{1,0},{2,3},{3,2},{4,5},{5,4},{6,7},{7,6},{8,9},{9,8},{10,11... | collective-permute-start | bytes 196616 | tf_op jit(solution)/shard_map/ppermute | solution.py:306
  30.0 5.4 %collective-permute-start.15 = (f32[134,512]{1,0:T(8,128)S(1)}, f32[134,512]{1,0:T(8,128)S(1)}, u32[]{:S(2)}, u32[]{:S(2)}) collective-permute-start(f32[134,512]{1,0:T(8,128)S(1)} %shard_map.92), channel_id=1, source_target_pairs={{0,28},{1,29},{2,30},{3,31},{4,0},{5,1},{6,2},{7,3},{8,4},{9,5},{1... | collective-permute-start | bytes 823304 | tf_op jit(solution)/shard_map/ppermute | solution.py:306
  31.1 6.4 %collective-permute-start.11 = (f32[32,512]{1,0:T(8,128)S(1)}, f32[32,512]{1,0:T(8,128)S(1)}, u32[]{:S(2)}, u32[]{:S(2)}) collective-permute-start(f32[32,512]{1,0:T(8,128)S(1)} %get-tuple-element.60), channel_id=1, source_target_pairs={{0,3},{1,2},{2,1},{3,0},{4,7},{5,6},{6,5},{7,4},{8,11},{9,10},{10,... | collective-permute-start | bytes 196616 | tf_op jit(solution)/shard_map/ppermute | solution.py:306
  32.1 5.4 %collective-permute-start.12 = (f32[32,512]{1,0:T(8,128)S(1)}, f32[32,512]{1,0:T(8,128)S(1)}, u32[]{:S(2)}, u32[]{:S(2)}) collective-permute-start(f32[32,512]{1,0:T(8,128)S(1)} %get-tuple-element.61), channel_id=1, source_target_pairs={{0,2},{1,3},{2,0},{3,1},{4,6},{5,7},{6,4},{7,5},{8,10},{9,11},{10,... | collective-permute-start | bytes 196616 | tf_op jit(solution)/shard_map/ppermute | solution.py:306
  33.8 4.3 %collective-permute-start.14 = (f32[32,512]{1,0:T(8,128)S(1)}, f32[32,512]{1,0:T(8,128)S(1)}, u32[]{:S(2)}, u32[]{:S(2)}) collective-permute-start(f32[32,512]{1,0:T(8,128)S(1)} %get-tuple-element.64.refs_4_), channel_id=1, source_target_pairs={{0,1},{1,0},{2,3},{3,2},{4,5},{5,4},{6,7},{7,6},{8,9},{9,8},{10,11... | collective-permute-start | bytes 196616 | tf_op jit(solution)/shard_map/ppermute | solution.py:306
